TPU v7x, 128 devices: a whole 4x4x4 slice. The times are simulated.
128 devices in a mesh: rep: 4 (over y_lo, core), fsdp: 32 (over x, y_hi, z).
Axes of the slice: x: 4, y: 4 (y_hi: 2, y_lo: 2; y = y_hi * 2 + y_lo), z: 4, core: 2. Of those that a mesh axis runs over, the one named last changes fastest.
Arguments:
- tokens: bfloat16 [65536, 16384], P(('rep', 'fsdp')), may hold values from -24 to 24
- cotangent: bfloat16 [65536, 512], P(('rep', 'fsdp')), may hold values from -0.0625 to 0.0625
- master: float32 [16384, 512], P('fsdp'), may hold values from -4 to 4
- moment1: float32 [16384, 512], P('fsdp'), may hold values from -3 to 3
- moment2: float32 [16384, 512], P('fsdp'), may hold values from 0.05 to 5
- owner: int32 [8192], replicated, may hold values from 0 to 127, as said below
Outputs:
- master_new: float32 [16384, 512], P('fsdp')
- moment1_new: float32 [16384, 512], P('fsdp')
- moment2_new: float32 [16384, 512], P('fsdp')
- upload: bfloat16 [16384, 2, 512], P(('rep', 'fsdp'))
Inputs may be any that keep to these rules, and one draw needn't show every extreme that they name: For every shard s and device w, at most 4 blocks of shard s have owner w, and some device owns exactly 4 blocks of each shard.
All inputs are finite; a program needn't handle non-finite values.
Results may differ from a plain program's by a relative error of at most 0.015.
Values may be sent and summed in bfloat16 or wider, within the bound.
No kernel may reach another device: no remote copies, remote signals or barrier semaphores. Data moves between devices by JAX's collectives and lax.ppermute only.
A program may use at most 192 MiB of HBM per device.

v0:
```python
import jax
import jax.numpy as jnp
from jax import lax
from jax.sharding import PartitionSpec as P

BLOCK_ROWS = 2


bias_first = 1.0 - 0.9**10
bias_second = 1.0 - 0.95**10


def adam_update(grad, master, moment1, moment2):
    first = 0.9 * moment1 + 0.1 * grad
    second = 0.95 * moment2 + 0.05 * grad * grad
    update = first / bias_first / (jnp.sqrt(second / bias_second) + 1e-08)
    return (master - 0.05 * (update + 0.1 * master), first, second)


def per_device(tokens, cotangent, master, moment1, moment2, owner):
    fsdp_count = lax.axis_size("fsdp")
    rep_count = lax.axis_size("rep")
    shard_rows = master.shape[0]
    columns = master.shape[1]
    shard_grad = lax.psum_scatter(
        lax.dot_general(
            tokens, cotangent, (((0,), (0,)), ((), ())), preferred_element_type=jnp.float32
        ).astype(jnp.bfloat16),
        "fsdp",
        scatter_dimension=0,
        tiled=True,
    )
    grad = lax.psum(shard_grad, "rep").astype(jnp.float32)
    master_new, moment1_new, moment2_new = adam_update(grad, master, moment1, moment2)
    weight = master_new.astype(jnp.bfloat16)
    local_blocks = shard_rows // BLOCK_ROWS
    capacity = 2 * local_blocks // (rep_count * fsdp_count)
    blocks = weight.reshape(local_blocks, BLOCK_ROWS * columns)
    owners = lax.dynamic_slice_in_dim(owner, lax.axis_index("fsdp") * local_blocks, local_blocks)
    in_row = owners // fsdp_count == lax.axis_index("rep")
    target = owners % fsdp_count
    places = jnp.arange(local_blocks, dtype=jnp.int32)
    equal = owners[:, None] == owners[None, :]
    earlier = places[None, :] < places[:, None]
    ranks = jnp.sum(jnp.logical_and(equal, earlier), axis=1)
    slots = target * capacity + ranks
    slot_ids = jnp.arange(fsdp_count * capacity, dtype=jnp.int32)
    selector = jnp.logical_and(slot_ids[:, None] == slots[None, :], in_row[None, :]).astype(
        jnp.bfloat16
    )
    outgoing = jnp.dot(selector, blocks, preferred_element_type=jnp.float32).astype(jnp.bfloat16)
    outgoing = outgoing.reshape(fsdp_count, capacity, BLOCK_ROWS, columns)
    received = lax.all_to_all(outgoing, "fsdp", split_axis=0, concat_axis=0, tiled=True)
    upload = received.reshape(fsdp_count * capacity, BLOCK_ROWS, columns)
    return (master_new, moment1_new, moment2_new, upload)


def solution(mesh):
    placed = (
        P(("rep", "fsdp"), None),
        P(("rep", "fsdp"), None),
        P("fsdp", None),
        P("fsdp", None),
        P("fsdp", None),
        P(),
    )
    return jax.shard_map(
        per_device,
        mesh=mesh,
        in_specs=placed,
        out_specs=(
            P("fsdp", None),
            P("fsdp", None),
            P("fsdp", None),
            P(("rep", "fsdp"), None, None),
        ),
        check_vma=False,
    )
```

profile of v0, /device:TPU:0, one launch (start us, length us, event | category | flops | bytes accessed | tf_op | source)
XLA Modules:
  0.0 323.5 jit_solution(2834063317738364155)
XLA Ops:
  7.2 0.0 copy-start
  7.2 0.0 reduce-scatter.2.cloned.1.call-start
  7.2 1.0 copy-done
  8.2 18.4 %convolution_convert_fusion = bf16[16384,512]{1,0:T(8,128)(2,1)} fusion(bf16[512,16384]{1,0:T(8,128)(2,1)} %param.6, bf16[512,512]{1,0:T(8,128)(2,1)S(1)} %copy-done), kind=kOutput, calls=%fused_computation | convolution fusion | flops 8598323200 | bytes 34078720 | tf_op jit(solution)/shard_map/dot_general | solution.py:26
  26.6 0.0 copy-start.1
  26.6 0.0 copy-start.2
  26.6 0.0 reduce-scatter.2.cloned.1.call-update
  26.6 0.0 all-reduce.2.cloned.1.call-start
  26.7 226.5 %reduce-scatter.2.cloned.1.call-done = bf16[512,512]{1,0:T(8,128)(2,1)} async-done(((bf16[16384,512]{1,0:T(8,128)(2,1)}), bf16[512,512]{1,0:T(8,128)(2,1)}) %reduce-scatter.2.cloned.1.call-update) | async-done | bytes 524304 | tf_op jit(solution)/shard_map/reduce_scatter | solution.py:25
  253.2 0.0 all-reduce.2.cloned.1.call-update
  253.2 0.8 fusion.9
  254.0 0.2 convert_reduce_fusion
  254.2 37.2 %all-reduce.2.cloned.1.call-done = bf16[512,512]{1,0:T(8,128)(2,1)} async-done(((bf16[512,512]{1,0:T(8,128)(2,1)}), bf16[512,512]{1,0:T(8,128)(2,1)}) %all-reduce.2.cloned.1.call-update) | async-done | bytes 524304 | tf_op jit(solution)/shard_map/psum | solution.py:33
  291.3 0.0 copy-done.1
  291.3 0.0 copy-done.2
  291.3 3.6 %fusion.10 = (bf16[512,512]{1,0:T(8,128)(2,1)S(1)}, f32[512,512]{1,0:T(8,128)}, f32[512,512]{1,0:T(8,128)}, f32[512,512]{1,0:T(8,128)}) fusion(f32[512,512]{1,0:T(8,128)S(1)} %copy-done.1, bf16[512,512]{1,0:T(8,128)(2,1)} %all-reduce.2.cloned.1.call-done, f32[512,512]{1,0:T(8,128)S(1)} %copy-done.2, f32[512,512]{1,0:T(8,128)} %param.10), kind=kLoop, calls=%fused_computation.24 | loop fusion | flops 4456448 | bytes 7340032 | tf_op jit(solution)/shard_map/convert_element_type | solution.py:35
  294.9 0.2 reshape.21
  295.1 0.2 convolution_convert_fusion.1
  295.4 0.2 reshape.22
  295.6 20.4 %all_to_all.5 = bf16[32,4,2,512]{3,2,1,0:T(2,128)(2,1)S(1)} all-to-all(bf16[32,4,2,512]{3,2,1,0:T(2,128)(2,1)S(1)} %reshape.22), channel_id=1, replica_groups=mesh['rep'=4,'fsdp'=32] {'fsdp'}, dimensions={0} | all-to-all | bytes 524288 | tf_op jit(solution)/shard_map/all_to_all | solution.py:53
  316.0 0.7 copy.12
  (1 shorter events, 0.0 us)
Async XLA Ops:
  7.2 1.0 copy-start
  7.2 246.0 %reduce-scatter.2.cloned.1.call-start = ((), (), s32[]{:S(2)}) async-start(), calls=%async_computation.2 | async-start | bytes 17301504 | tf_op jit(solution)/shard_map/reduce_scatter | solution.py:25
  26.6 264.8 %copy-start.1 = (f32[512,512]{1,0:T(8,128)S(1)}, f32[512,512]{1,0:T(8,128)}, u32[]{:S(2)}) copy-start(f32[512,512]{1,0:T(8,128)} %param.8) | copy-start | bytes 3145732
  26.6 264.8 %copy-start.2 = (f32[512,512]{1,0:T(8,128)S(1)}, f32[512,512]{1,0:T(8,128)}, u32[]{:S(2)}) copy-start(f32[512,512]{1,0:T(8,128)} %param.9) | copy-start | bytes 3145732
  26.6 264.7 %all-reduce.2.cloned.1.call-start = ((), (), s32[]{:S(2)}) async-start(), calls=%async_computation.3 | async-start | bytes 1048576 | tf_op jit(solution)/shard_map/psum | solution.py:33
Sparse Core Ops, SparseCore 0:
  26.7 226.3 reduce-scatter.1
  255.7 35.6 all-reduce.1
where the time goes:
time: 324 us
  waiting for transfers between devices  264 us (81%)
  blocking collectives  20.4 us (6%)
  matrix products  18.6 us (6%)
  between operations  14.1 us (4%)
  other arithmetic  4.57 us (1%)
    reduce_scatter x1, waiting for transfers between devices, per_device(): lax.psum_scatter(lax.dot_general(tokens, cotangent, (((0,), (0,)), ((), (...  227 us
    psum x1, waiting for transfers between devices, per_device(): grad = lax.psum(shard_grad, 'rep').astype(jnp.float32)  37.2 us
    all_to_all x1, blocking collectives, per_device(): lax.all_to_all(outgoing, 'fsdp', split_axis=0, concat_axis=0, tiled=True)  20.4 us
    dot_general x1, matrix products, per_device(): lax.dot_general(tokens, cotangent, (((0,), (0,)), ((), ())), preferred_el...  18.4 us
  transfers between devices with their start and end apart: 2, of which 2 were waited for; matrix products, arithmetic and copies ran while one was open for 0% of the time, Pallas kernels for 0%

commit v1 on v0

--- a/solution.py
+++ b/solution.py
@@ -1,20 +1,177 @@
+import functools
+
 import jax
 import jax.numpy as jnp
 from jax import lax
+from jax.experimental import pallas as pl
+from jax.experimental.pallas import tpu as pltpu
 from jax.sharding import PartitionSpec as P
 
 BLOCK_ROWS = 2
-
+AXES = ("rep", "fsdp")
+SIDE = 4
+PARTS = ((0, 176), (176, 256))
 
 bias_first = 1.0 - 0.9**10
 bias_second = 1.0 - 0.95**10
 
-
-def adam_update(grad, master, moment1, moment2):
-    first = 0.9 * moment1 + 0.1 * grad
-    second = 0.95 * moment2 + 0.05 * grad * grad
+ORDERS = (((0, 1, 2), (1, 2, 0)), ((2, 0, 1), (2, 0, 1)))
+
+
+def coords(index):
+    rep, fsdp = divmod(index, 32)
+    y_lo, core = divmod(rep, 2)
+    x, rest = divmod(fsdp, 8)
+    y_hi, z = divmod(rest, 4)
+    return x, y_hi * 2 + y_lo, z, core
+
+
+def index_of(x, y, z, core):
+    return ((y % 2) * 2 + core) * 32 + x * 8 + (y // 2) * 4 + z
+
+
+def ring_pairs(part, stage, distance):
+    pairs = []
+    for device in range(128):
+        place = list(coords(device))
+        axis = ORDERS[part][place[3]][stage]
+        place[axis] = (place[axis] + distance) % SIDE
+        pairs.append((device, index_of(*place)))
+    return pairs
+
+
+def rep_pairs(bit):
+    return [(device, (((device // 32) ^ bit) * 32) + device % 32) for device in range(128)]
+
+
+def send(value, pairs):
+    return lax.ppermute(value, AXES, pairs)
+
+
+def matmul_body(rows, count, has_sum, table, cot, *refs):
+    first, last = rows
+    tokens = refs[:count]
+    out = refs[-1]
+    left = cot[first:last, :]
+    for at in range(count):
+        total = jnp.dot(left, tokens[at][...], preferred_element_type=jnp.float32)
+        if has_sum:
+            total = total + refs[count][at].astype(jnp.float32)
+        out[at] = total.astype(jnp.bfloat16)
+
+
+def pieces(table, cot_t, tokens, part, side, distance, received=None):
+    rows = PARTS[part]
+    width = rows[1] - rows[0]
+    depth, lanes = tokens.shape[0], 256
+    base = 12 * (part * 2 + side)
+
+    def token_map(at, step, table):
+        return (0, table[base + distance] + table[base + 4 + step] + table[base + 8 + at])
+
+    in_specs = [pl.BlockSpec((256, depth), lambda step, table: (table[48 + side], 0))]
+    in_specs += [
+        pl.BlockSpec((depth, lanes), functools.partial(token_map, at)) for at in range(SIDE)
+    ]
+    operands = [table, cot_t] + [tokens] * SIDE
+    piece_spec = pl.BlockSpec((SIDE, width, lanes), lambda step, table: (step, 0, 0))
+    if received is not None:
+        in_specs.append(piece_spec)
+        operands.append(received)
+    return pl.pallas_call(
+        functools.partial(matmul_body, rows, SIDE, received is not None),
+        out_shape=jax.ShapeDtypeStruct((SIDE * SIDE, width, lanes), jnp.bfloat16),
+        grid_spec=pltpu.PrefetchScalarGridSpec(
+            num_scalar_prefetch=1, grid=(SIDE,), in_specs=in_specs, out_specs=piece_spec
+        ),
+        compiler_params=pltpu.CompilerParams(vmem_limit_bytes=24 * 1024 * 1024),
+        cost_estimate=pl.CostEstimate(
+            flops=2 * width * depth * lanes * 16, bytes_accessed=6_000_000, transcendentals=0
+        ),
+    )(*operands)
+
+
+def adam_body(table, own, other, master, moment1, moment2, master_new, first_new, second_new, weight):
+    mine = own[0].T.astype(jnp.float32)
+    theirs = other[0].T.astype(jnp.float32)
+    is_first = table[50] == 0
+    grad = jnp.concatenate(
+        [jnp.where(is_first, mine, theirs), jnp.where(is_first, theirs, mine)], axis=1
+    )
+    first = 0.9 * moment1[...] + 0.1 * grad
+    second = 0.95 * moment2[...] + 0.05 * grad * grad
     update = first / bias_first / (jnp.sqrt(second / bias_second) + 1e-08)
-    return (master - 0.05 * (update + 0.1 * master), first, second)
+    new = master[...] - 0.05 * (update + 0.1 * master[...])
+    master_new[...] = new
+    first_new[...] = first
+    second_new[...] = second
+    weight[...] = new.astype(jnp.bfloat16)
+
+
+def adam(table, own, other, master, moment1, moment2):
+    rows, columns = master.shape
+    half = rows // 2
+    grad_spec = pl.BlockSpec((1, columns // 2, half), lambda i, table: (i ^ table[51], 0, 0))
+    row_spec = pl.BlockSpec((half, columns), lambda i, table: (i, 0))
+    return pl.pallas_call(
+        adam_body,
+        out_shape=[jax.ShapeDtypeStruct((rows, columns), jnp.float32)] * 3
+        + [jax.ShapeDtypeStruct((rows, columns), jnp.bfloat16)],
+        grid_spec=pltpu.PrefetchScalarGridSpec(
+            num_scalar_prefetch=1,
+            grid=(2,),
+            in_specs=[grad_spec, grad_spec, row_spec, row_spec, row_spec],
+            out_specs=[row_spec] * 4,
+        ),
+        compiler_params=pltpu.CompilerParams(vmem_limit_bytes=32 * 1024 * 1024),
+        cost_estimate=pl.CostEstimate(
+            flops=20 * rows * columns, bytes_accessed=28 * rows * columns, transcendentals=0
+        ),
+    )(table, own, other, master, moment1, moment2)
+
+
+def position_table():
+    rep, fsdp = lax.axis_index("rep"), lax.axis_index("fsdp")
+    core, y_lo = rep % 2, rep // 2
+    place = (fsdp // 8, (fsdp // 4) % 2 * 2 + y_lo, fsdp % 4)
+    away = jnp.arange(SIDE, dtype=jnp.int32)
+    steps = []
+    for axis in range(3):
+        at = (place[axis] + away) % SIDE
+        steps.append((at * 16, (at // 2) * 8 + at % 2, at * 2)[axis])
+    rows = []
+    for part in range(2):
+        for side in range(2):
+            target = core ^ side
+            rows.append(
+                jnp.where(
+                    target == 0,
+                    jnp.concatenate([steps[axis] for axis in ORDERS[part][0]]),
+                    jnp.concatenate([steps[axis] for axis in ORDERS[part][1]]),
+                )
+            )
+    rest = jnp.stack([core, 1 - core, core, y_lo]).astype(jnp.int32)
+    return jnp.concatenate(rows + [rest]).astype(jnp.int32)
+
+
+def reduce_part(table, cot_t, tokens, part):
+    own = {}
+    for distance in (1, 3, 2, 0):
+        other = pieces(table, cot_t, tokens, part, 1, distance)
+        arrived = send(other, rep_pairs(1))
+        own[distance] = pieces(table, cot_t, tokens, part, 0, distance, arrived)
+    width = PARTS[part][1] - PARTS[part][0]
+    groups = [own[distance].reshape(SIDE, SIDE, width, 256) for distance in range(SIDE)]
+    for stage in range(3):
+        arrived = [groups[0]]
+        for distance in (1, 3, 2):
+            arrived.append(send(groups[distance], ring_pairs(part, stage, distance)))
+        if stage == 2:
+            return sum(value.astype(jnp.float32) for value in arrived).astype(jnp.bfloat16)
+        groups = [
+            sum(value[at].astype(jnp.float32) for value in arrived).astype(jnp.bfloat16)
+            for at in range(SIDE)
+        ]
 
 
 def per_device(tokens, cotangent, master, moment1, moment2, owner):
@@ -22,17 +179,15 @@
     rep_count = lax.axis_size("rep")
     shard_rows = master.shape[0]
     columns = master.shape[1]
-    shard_grad = lax.psum_scatter(
-        lax.dot_general(
-            tokens, cotangent, (((0,), (0,)), ((), ())), preferred_element_type=jnp.float32
-        ).astype(jnp.bfloat16),
-        "fsdp",
-        scatter_dimension=0,
-        tiled=True,
-    )
-    grad = lax.psum(shard_grad, "rep").astype(jnp.float32)
-    master_new, moment1_new, moment2_new = adam_update(grad, master, moment1, moment2)
-    weight = master_new.astype(jnp.bfloat16)
+    table = position_table()
+    cot_t = cotangent.T
+    mine = jnp.concatenate([reduce_part(table, cot_t, tokens, part) for part in range(2)], axis=0)
+    beside = send(mine, rep_pairs(2))
+    own = jnp.stack([mine, beside])
+    other = send(own, rep_pairs(1))
+    master_new, moment1_new, moment2_new, weight = adam(
+        table, own, other, master, moment1, moment2
+    )
     local_blocks = shard_rows // BLOCK_ROWS
     capacity = 2 * local_blocks // (rep_count * fsdp_count)
     blocks = weight.reshape(local_blocks, BLOCK_ROWS * columns)

time: 324 us -> 148 us (0.46)
  waiting for transfers between devices: 264 us -> 35 us
  Pallas kernels: 0 us -> 50.6 us
  starting transfers between devices: 0.08 us -> 32.9 us
  matrix products: 18.6 us -> 0.24 us
  between operations: 14.1 us -> 1.04 us
  local copies, waits for them, and re-layouts: 2.06 us -> 10 us
  blocking collectives: 20.4 us -> 15.4 us
    reduce_scatter x1 -> x0, waiting for transfers between devices: 227 us -> none  [per_device(): lax.psum_scatter(lax.dot_general(tokens, cotangent, (((0,), (0,)), ((), (...]
    pallas_call x0 -> x17, Pallas kernels: none -> 50.6 us  [the longest x16 47.8 us: pieces(): pl.pallas_call(functools.partial(matmul_body, rows, SIDE, received is not...]
    psum x1 -> x0, waiting for transfers between devices: 37.2 us -> none  [per_device(): grad = lax.psum(shard_grad, 'rep').astype(jnp.float32)]
    ppermute x0 -> x28, waiting for transfers between devices: none -> 35 us  [send(): return lax.ppermute(value, AXES, pairs)]
    ppermute x0 -> x28, starting transfers between devices: none -> 32.9 us  [send(): return lax.ppermute(value, AXES, pairs)]
    dot_general x1 -> x0, matrix products: 18.4 us -> none  [per_device(): lax.dot_general(tokens, cotangent, (((0,), (0,)), ((), ())), preferred_el...]
    unnamed x7 -> x12, local copies, waits for them, and re-layouts: 1.7 us -> 8.53 us
    all_to_all x1, blocking collectives: 20.4 us -> 15.4 us  [per_device(): lax.all_to_all(outgoing, 'fsdp', split_axis=0, concat_axis=0, tiled=True)]
  transfers between devices with their start and end apart: 2 -> 28, of which waited for: 2 -> 9; matrix products, arithmetic and copies ran while one was open for 0% -> 2% of each run, Pallas kernels for 0% -> 30%
where the time goes in v1:
time: 148 us
  Pallas kernels  50.6 us (34%)
  waiting for transfers between devices  35 us (24%)
  starting transfers between devices  32.9 us (22%)
  blocking collectives  15.4 us (10%)
  local copies, waits for them, and re-layouts  10 us (7%)
  other arithmetic  2.62 us (2%)
    pallas_call x16, Pallas kernels, pieces(): pl.pallas_call(functools.partial(matmul_body, rows, SIDE, received is not...  47.8 us
    ppermute x28, waiting for transfers between devices, send(): return lax.ppermute(value, AXES, pairs)  35 us
    ppermute x28, starting transfers between devices, send(): return lax.ppermute(value, AXES, pairs)  32.9 us
    all_to_all x1, blocking collectives, per_device(): lax.all_to_all(outgoing, 'fsdp', split_axis=0, concat_axis=0, tiled=True)  15.4 us
    unnamed x12, local copies, waits for them, and re-layouts  8.53 us
  transfers between devices with their start and end apart: 28, of which 9 were waited for; matrix products, arithmetic and copies ran while one was open for 2% of the time, Pallas kernels for 30%

profile of v1, /device:TPU:0, one launch (start us, length us, event | category | flops | bytes accessed | tf_op | source)
XLA Modules:
  0.0 147.8 jit_solution(8838843148711299392)
XLA Ops:
  2.2 5.8 %copy-done = bf16[512,16384]{1,0:T(8,128)(2,1)S(1)} copy-done((bf16[512,16384]{1,0:T(8,128)(2,1)S(1)}, bf16[512,16384]{1,0:T(8,128)(2,1)}, u32[]{:S(2)}) %copy-start) | copy-done | bytes 16777240
  8.0 2.8 %shard_map.95 = bf16[16,176,256]{2,1,0:T(8,128)(2,1)S(1)} custom-call(s32[52]{0:T(128)S(1)} %concatenate.21.table, bf16[512,512]{1,0:T(8,128)(2,1)S(1)} %bitcast.157, bf16[512,16384]{1,0:T(8,128)(2,1)S(1)} %copy-done, bf16[512,16384]{1,0:T(8,128)(2,1)S(1)} %copy-done, bf16[512,16384]{1,0:T(8,128)(2,1)S(1)} %copy-done, bf16[512,16384]{1,0:T(8,128)(2,1)S(1)} %copy-done), custom_call_target="tpu_custom_call" | custom-call | flops 738197504 | bytes 6000000 | tf_op jit(solution)/shard_map/pallas_call | solution.py:81
  10.9 3.7 %shard_map.97 = bf16[16,176,256]{2,1,0:T(8,128)(2,1)} custom-call(s32[52]{0:T(128)S(1)} %concatenate.21.table, bf16[512,512]{1,0:T(8,128)(2,1)S(1)} %bitcast.158, bf16[512,16384]{1,0:T(8,128)(2,1)S(1)} %copy-done, bf16[512,16384]{1,0:T(8,128)(2,1)S(1)} %copy-done, bf16[512,16384]{1,0:T(8,128)(2,1)S(1)} %copy-done, bf16[512,16384]{1,0:T(8,128)(2,1)S(1)} %copy-done), custom_call_target="tpu_custom_call" | custom-call | flops 738197504 | bytes 6000000 | tf_op jit(solution)/shard_map/pallas_call | solution.py:81
  15.1 3.7 %shard_map.99 = bf16[16,176,256]{2,1,0:T(8,128)(2,1)} custom-call(s32[52]{0:T(128)S(1)} %concatenate.21.table, bf16[512,512]{1,0:T(8,128)(2,1)S(1)} %bitcast.159, bf16[512,16384]{1,0:T(8,128)(2,1)S(1)} %copy-done, bf16[512,16384]{1,0:T(8,128)(2,1)S(1)} %copy-done, bf16[512,16384]{1,0:T(8,128)(2,1)S(1)} %copy-done, bf16[512,16384]{1,0:T(8,128)(2,1)S(1)} %copy-done), custom_call_target="tpu_custom_call" | custom-call | flops 738197504 | bytes 6000000 | tf_op jit(solution)/shard_map/pallas_call | solution.py:81
  18.8 2.6 %shard_map.103 = bf16[16,80,256]{2,1,0:T(8,128)(2,1)S(1)} custom-call(s32[52]{0:T(128)S(1)} %concatenate.21.table, bf16[512,512]{1,0:T(8,128)(2,1)S(1)} %bitcast.160, bf16[512,16384]{1,0:T(8,128)(2,1)S(1)} %copy-done, bf16[512,16384]{1,0:T(8,128)(2,1)S(1)} %copy-done, bf16[512,16384]{1,0:T(8,128)(2,1)S(1)} %copy-done, bf16[512,16384]{1,0:T(8,128)(2,1)S(1)} %copy-done), custom_call_target="tpu_custom_call" | custom-call | flops 335544320 | bytes 6000000 | tf_op jit(solution)/shard_map/pallas_call | solution.py:81
  22.0 2.6 %shard_map.105 = bf16[16,80,256]{2,1,0:T(8,128)(2,1)S(1)} custom-call(s32[52]{0:T(128)S(1)} %concatenate.21.table, bf16[512,512]{1,0:T(8,128)(2,1)S(1)} %bitcast.161, bf16[512,16384]{1,0:T(8,128)(2,1)S(1)} %copy-done, bf16[512,16384]{1,0:T(8,128)(2,1)S(1)} %copy-done, bf16[512,16384]{1,0:T(8,128)(2,1)S(1)} %copy-done, bf16[512,16384]{1,0:T(8,128)(2,1)S(1)} %copy-done), custom_call_target="tpu_custom_call" | custom-call | flops 335544320 | bytes 6000000 | tf_op jit(solution)/shard_map/pallas_call | solution.py:81
  24.7 2.6 %shard_map.107 = bf16[16,80,256]{2,1,0:T(8,128)(2,1)S(1)} custom-call(s32[52]{0:T(128)S(1)} %concatenate.21.table, bf16[512,512]{1,0:T(8,128)(2,1)S(1)} %bitcast.162, bf16[512,16384]{1,0:T(8,128)(2,1)S(1)} %copy-done, bf16[512,16384]{1,0:T(8,128)(2,1)S(1)} %copy-done, bf16[512,16384]{1,0:T(8,128)(2,1)S(1)} %copy-done, bf16[512,16384]{1,0:T(8,128)(2,1)S(1)} %copy-done), custom_call_target="tpu_custom_call" | custom-call | flops 335544320 | bytes 6000000 | tf_op jit(solution)/shard_map/pallas_call | solution.py:81
  27.2 2.6 %shard_map.101 = bf16[16,80,256]{2,1,0:T(8,128)(2,1)S(1)} custom-call(s32[52]{0:T(128)S(1)} %concatenate.21.table, bf16[512,512]{1,0:T(8,128)(2,1)S(1)} %bitcast.163, bf16[512,16384]{1,0:T(8,128)(2,1)S(1)} %copy-done, bf16[512,16384]{1,0:T(8,128)(2,1)S(1)} %copy-done, bf16[512,16384]{1,0:T(8,128)(2,1)S(1)} %copy-done, bf16[512,16384]{1,0:T(8,128)(2,1)S(1)} %copy-done), custom_call_target="tpu_custom_call" | custom-call | flops 335544320 | bytes 6000000 | tf_op jit(solution)/shard_map/pallas_call | solution.py:81
  30.4 2.6 %shard_map.104 = bf16[16,80,256]{2,1,0:T(8,128)(2,1)S(1)} custom-call(s32[52]{0:T(128)S(1)} %concatenate.21.table, bf16[512,512]{1,0:T(8,128)(2,1)S(1)} %bitcast.164, bf16[512,16384]{1,0:T(8,128)(2,1)S(1)} %copy-done, bf16[512,16384]{1,0:T(8,128)(2,1)S(1)} %copy-done, bf16[512,16384]{1,0:T(8,128)(2,1)S(1)} %copy-done, bf16[512,16384]{1,0:T(8,128)(2,1)S(1)} %copy-done, ...), custom_call_target="tpu_custom_call" | custom-call | flops 335544320 | bytes 6000000 | tf_op jit(solution)/shard_map/pallas_call | solution.py:81
  33.1 2.1 %collective-permute-start.15 = (bf16[4,4,80,256]{3,2,1,0:T(8,128)(2,1)S(1)}, bf16[4,4,80,256]{3,2,1,0:T(8,128)(2,1)S(1)}, u32[]{:S(2)}, u32[]{:S(2)}) collective-permute-start(bf16[4,4,80,256]{3,2,1,0:T(8,128)(2,1)S(1)} %bitcast.176), channel_id=1, source_target_pairs={{0,1},{1,2},{2,3},{3,0},{4,5},{5,6},{6,7},{7,4},{8,9},{9,10},{10,1... | collective-permute-start | bytes 1966088 | tf_op jit(solution)/shard_map/ppermute | solution.py:48
  35.2 2.8 %shard_map.93 = bf16[16,176,256]{2,1,0:T(8,128)(2,1)S(1)} custom-call(s32[52]{0:T(128)S(1)} %concatenate.21.table, bf16[512,512]{1,0:T(8,128)(2,1)S(1)} %bitcast.165, bf16[512,16384]{1,0:T(8,128)(2,1)S(1)} %copy-done, bf16[512,16384]{1,0:T(8,128)(2,1)S(1)} %copy-done, bf16[512,16384]{1,0:T(8,128)(2,1)S(1)} %copy-done, bf16[512,16384]{1,0:T(8,128)(2,1)S(1)} %copy-done), custom_call_target="tpu_custom_call" | custom-call | flops 738197504 | bytes 6000000 | tf_op jit(solution)/shard_map/pallas_call | solution.py:81
  38.0 2.6 %shard_map.106 = bf16[16,80,256]{2,1,0:T(8,128)(2,1)S(1)} custom-call(s32[52]{0:T(128)S(1)} %concatenate.21.table, bf16[512,512]{1,0:T(8,128)(2,1)S(1)} %bitcast.166, bf16[512,16384]{1,0:T(8,128)(2,1)S(1)} %copy-done, bf16[512,16384]{1,0:T(8,128)(2,1)S(1)} %copy-done, bf16[512,16384]{1,0:T(8,128)(2,1)S(1)} %copy-done, bf16[512,16384]{1,0:T(8,128)(2,1)S(1)} %copy-done, ...), custom_call_target="tpu_custom_call" | custom-call | flops 335544320 | bytes 6000000 | tf_op jit(solution)/shard_map/pallas_call | solution.py:81
  40.6 2.2 %collective-permute-start.17 = (bf16[4,4,80,256]{3,2,1,0:T(8,128)(2,1)S(1)}, bf16[4,4,80,256]{3,2,1,0:T(8,128)(2,1)S(1)}, u32[]{:S(2)}, u32[]{:S(2)}) collective-permute-start(bf16[4,4,80,256]{3,2,1,0:T(8,128)(2,1)S(1)} %bitcast.177), channel_id=1, source_target_pairs={{0,3},{1,0},{2,1},{3,2},{4,7},{5,4},{6,5},{7,6},{8,11},{9,8},{10,9... | collective-permute-start | bytes 1966088 | tf_op jit(solution)/shard_map/ppermute | solution.py:48
  42.8 2.8 %shard_map.96 = bf16[16,176,256]{2,1,0:T(8,128)(2,1)S(1)} custom-call(s32[52]{0:T(128)S(1)} %concatenate.21.table, bf16[512,512]{1,0:T(8,128)(2,1)S(1)} %bitcast.167, bf16[512,16384]{1,0:T(8,128)(2,1)S(1)} %copy-done, bf16[512,16384]{1,0:T(8,128)(2,1)S(1)} %copy-done, bf16[512,16384]{1,0:T(8,128)(2,1)S(1)} %copy-done, bf16[512,16384]{1,0:T(8,128)(2,1)S(1)} %copy-done, ...), custom_call_target="tpu_custom_call" | custom-call | flops 738197504 | bytes 6000000 | tf_op jit(solution)/shard_map/pallas_call | solution.py:81
  45.6 4.3 %shard_map.98 = bf16[16,176,256]{2,1,0:T(8,128)(2,1)S(1)} custom-call(s32[52]{0:T(128)S(1)} %concatenate.21.table, bf16[512,512]{1,0:T(8,128)(2,1)S(1)} %bitcast.168, bf16[512,16384]{1,0:T(8,128)(2,1)S(1)} %copy-done, bf16[512,16384]{1,0:T(8,128)(2,1)S(1)} %copy-done, bf16[512,16384]{1,0:T(8,128)(2,1)S(1)} %copy-done, bf16[512,16384]{1,0:T(8,128)(2,1)S(1)} %copy-done, ...), custom_call_target="tpu_custom_call" | custom-call | flops 738197504 | bytes 6000000 | tf_op jit(solution)/shard_map/pallas_call | solution.py:81
  50.1 4.3 %shard_map.100 = bf16[16,176,256]{2,1,0:T(8,128)(2,1)S(1)} custom-call(s32[52]{0:T(128)S(1)} %concatenate.21.table, bf16[512,512]{1,0:T(8,128)(2,1)S(1)} %bitcast.169, bf16[512,16384]{1,0:T(8,128)(2,1)S(1)} %copy-done, bf16[512,16384]{1,0:T(8,128)(2,1)S(1)} %copy-done, bf16[512,16384]{1,0:T(8,128)(2,1)S(1)} %copy-done, bf16[512,16384]{1,0:T(8,128)(2,1)S(1)} %copy-done, ...), custom_call_target="tpu_custom_call" | custom-call | flops 738197504 | bytes 6000000 | tf_op jit(solution)/shard_map/pallas_call | solution.py:81
  57.7 1.8 %collective-permute-start.6 = (bf16[4,4,176,256]{3,2,1,0:T(8,128)(2,1)S(1)}, bf16[4,4,176,256]{3,2,1,0:T(8,128)(2,1)S(1)}, u32[]{:S(2)}, u32[]{:S(2)}) collective-permute-start(bf16[4,4,176,256]{3,2,1,0:T(8,128)(2,1)S(1)} %bitcast.175), channel_id=1, source_target_pairs={{0,16},{1,17},{2,18},{3,19},{4,20},{5,21},{6,22},{7,23},{8,24},{9,... | collective-permute-start | bytes 4325384 | tf_op jit(solution)/shard_map/ppermute | solution.py:48
  59.5 2.6 %shard_map.108 = bf16[16,80,256]{2,1,0:T(8,128)(2,1)S(1)} custom-call(s32[52]{0:T(128)S(1)} %concatenate.21.table, bf16[512,512]{1,0:T(8,128)(2,1)S(1)} %bitcast.170, bf16[512,16384]{1,0:T(8,128)(2,1)S(1)} %copy-done, bf16[512,16384]{1,0:T(8,128)(2,1)S(1)} %copy-done, bf16[512,16384]{1,0:T(8,128)(2,1)S(1)} %copy-done, bf16[512,16384]{1,0:T(8,128)(2,1)S(1)} %copy-done, ...), custom_call_target="tpu_custom_call" | custom-call | flops 335544320 | bytes 6000000 | tf_op jit(solution)/shard_map/pallas_call | solution.py:81
  62.1 1.8 %collective-permute-start.19 = (bf16[4,4,80,256]{3,2,1,0:T(8,128)(2,1)S(1)}, bf16[4,4,80,256]{3,2,1,0:T(8,128)(2,1)S(1)}, u32[]{:S(2)}, u32[]{:S(2)}) collective-permute-start(bf16[4,4,80,256]{3,2,1,0:T(8,128)(2,1)S(1)} %bitcast.178), channel_id=1, source_target_pairs={{0,2},{1,3},{2,0},{3,1},{4,6},{5,7},{6,4},{7,5},{8,10},{9,11},{10,... | collective-permute-start | bytes 1966088 | tf_op jit(solution)/shard_map/ppermute | solution.py:48
  63.9 2.6 %shard_map.102 = bf16[16,80,256]{2,1,0:T(8,128)(2,1)S(1)} custom-call(s32[52]{0:T(128)S(1)} %concatenate.21.table, bf16[512,512]{1,0:T(8,128)(2,1)S(1)} %bitcast.171, bf16[512,16384]{1,0:T(8,128)(2,1)S(1)} %copy-done, bf16[512,16384]{1,0:T(8,128)(2,1)S(1)} %copy-done, bf16[512,16384]{1,0:T(8,128)(2,1)S(1)} %copy-done, bf16[512,16384]{1,0:T(8,128)(2,1)S(1)} %copy-done, ...), custom_call_target="tpu_custom_call" | custom-call | flops 335544320 | bytes 6000000 | tf_op jit(solution)/shard_map/pallas_call | solution.py:81
  66.5 13.5 %collective-permute-done.19 = bf16[4,4,80,256]{3,2,1,0:T(8,128)(2,1)S(1)} collective-permute-done((bf16[4,4,80,256]{3,2,1,0:T(8,128)(2,1)S(1)}, bf16[4,4,80,256]{3,2,1,0:T(8,128)(2,1)S(1)}, u32[]{:S(2)}, u32[]{:S(2)}) %collective-permute-start.19) | collective-permute-done | bytes 655392 | tf_op jit(solution)/shard_map/ppermute | solution.py:48
  83.7 2.8 %shard_map.94 = bf16[16,176,256]{2,1,0:T(8,128)(2,1)S(1)} custom-call(s32[52]{0:T(128)S(1)} %concatenate.21.table, bf16[512,512]{1,0:T(8,128)(2,1)S(1)} %bitcast.172, bf16[512,16384]{1,0:T(8,128)(2,1)S(1)} %copy-done, bf16[512,16384]{1,0:T(8,128)(2,1)S(1)} %copy-done, bf16[512,16384]{1,0:T(8,128)(2,1)S(1)} %copy-done, bf16[512,16384]{1,0:T(8,128)(2,1)S(1)} %copy-done, ...), custom_call_target="tpu_custom_call" | custom-call | flops 738197504 | bytes 6000000 | tf_op jit(solution)/shard_map/pallas_call | solution.py:81
  86.5 1.8 %collective-permute-start.22 = (bf16[4,80,256]{2,1,0:T(8,128)(2,1)S(1)}, bf16[4,80,256]{2,1,0:T(8,128)(2,1)S(1)}, u32[]{:S(2)}, u32[]{:S(2)}) collective-permute-start(bf16[4,80,256]{2,1,0:T(8,128)(2,1)S(1)} %get-tuple-element.19), channel_id=1, source_target_pairs={{0,16},{1,17},{2,18},{3,19},{4,20},{5,21},{6,22},{7,23},{8,24},{9,... | collective-permute-start | bytes 491528 | tf_op jit(solution)/shard_map/ppermute | solution.py:48
  88.4 6.3 %collective-permute-done.6 = bf16[4,4,176,256]{3,2,1,0:T(8,128)(2,1)S(1)} collective-permute-done((bf16[4,4,176,256]{3,2,1,0:T(8,128)(2,1)S(1)}, bf16[4,4,176,256]{3,2,1,0:T(8,128)(2,1)S(1)}, u32[]{:S(2)}, u32[]{:S(2)}) %collective-permute-start.6) | collective-permute-done | bytes 1441824 | tf_op jit(solution)/shard_map/ppermute | solution.py:48
  101.6 1.8 %collective-permute-start.24 = (bf16[80,256]{1,0:T(8,128)(2,1)S(1)}, bf16[80,256]{1,0:T(8,128)(2,1)S(1)}, u32[]{:S(2)}, u32[]{:S(2)}) collective-permute-start(bf16[80,256]{1,0:T(8,128)(2,1)S(1)} %get-tuple-element.27), channel_id=1, source_target_pairs={{0,68},{1,69},{2,70},{3,71},{4,64},{5,65},{6,66},{7,67},{8,76},{9,... | collective-permute-start | bytes 122888 | tf_op jit(solution)/shard_map/ppermute | solution.py:48
  105.8 4.3 %collective-permute-done.9 = bf16[4,176,256]{2,1,0:T(8,128)(2,1)S(1)} collective-permute-done((bf16[4,176,256]{2,1,0:T(8,128)(2,1)S(1)}, bf16[4,176,256]{2,1,0:T(8,128)(2,1)S(1)}, u32[]{:S(2)}, u32[]{:S(2)}) %collective-permute-start.9) | collective-permute-done | bytes 360480 | tf_op jit(solution)/shard_map/ppermute | solution.py:48
  110.4 3.2 %collective-permute-start.11 = (bf16[176,256]{1,0:T(8,128)(2,1)S(1)}, bf16[176,256]{1,0:T(8,128)(2,1)S(1)}, u32[]{:S(2)}, u32[]{:S(2)}) collective-permute-start(bf16[176,256]{1,0:T(8,128)(2,1)S(1)} %get-tuple-element.24), channel_id=1, source_target_pairs={{0,3},{1,0},{2,1},{3,2},{4,7},{5,4},{6,5},{7,6},{8,11},{9,8},{10,9... | collective-permute-start | bytes 270344 | tf_op jit(solution)/shard_map/ppermute | solution.py:48
  114.2 1.9 %collective-permute-done.10 = bf16[176,256]{1,0:T(8,128)(2,1)S(1)} collective-permute-done((bf16[176,256]{1,0:T(8,128)(2,1)S(1)}, bf16[176,256]{1,0:T(8,128)(2,1)S(1)}, u32[]{:S(2)}, u32[]{:S(2)}) %collective-permute-start.10) | collective-permute-done | bytes 90144 | tf_op jit(solution)/shard_map/ppermute | solution.py:48
  116.7 3.0 %collective-permute-done.12 = bf16[176,256]{1,0:T(8,128)(2,1)S(1)} collective-permute-done((bf16[176,256]{1,0:T(8,128)(2,1)S(1)}, bf16[176,256]{1,0:T(8,128)(2,1)S(1)}, u32[]{:S(2)}, u32[]{:S(2)}) %collective-permute-start.12) | collective-permute-done | bytes 90144 | tf_op jit(solution)/shard_map/ppermute | solution.py:48
  122.1 2.8 %collective-permute-done.26 = bf16[256,256]{1,0:T(8,128)(2,1)S(1)} collective-permute-done((bf16[256,256]{1,0:T(8,128)(2,1)S(1)}, bf16[256,256]{1,0:T(8,128)(2,1)S(1)}, u32[]{:S(2)}, u32[]{:S(2)}) %collective-permute-start.26) | collective-permute-done | bytes 131104 | tf_op jit(solution)/shard_map/ppermute | solution.py:48
  126.5 2.8 %shard_map.109 = (f32[512,512]{1,0:T(8,128)}, f32[512,512]{1,0:T(8,128)}, f32[512,512]{1,0:T(8,128)}, bf16[512,512]{1,0:T(8,128)(2,1)S(1)}) custom-call(s32[52]{0:T(128)S(1)} %concatenate.21.table, bf16[2,256,256]{2,1,0:T(8,128)(2,1)S(1)} %pad_maximum_fusion.own, bf16[2,256,256]{2,1,0:T(8,128)(2,1)S(1)} %collective-permute-done.27.other, ...), custom_call_target="tpu_custom_call" | custom-call | flops 5242880 | bytes 7340032 | tf_op jit(solution)/shard_map/pallas_call | solution.py:116
  131.7 15.4 %all_to_all.5 = bf16[32,4,2,512]{3,2,1,0:T(2,128)(2,1)S(1)} all-to-all(bf16[32,4,2,512]{3,2,1,0:T(2,128)(2,1)S(1)} %reshape.176), channel_id=1, replica_groups=mesh['rep'=4,'fsdp'=32] {'fsdp'}, dimensions={0} | all-to-all | bytes 524288 | tf_op jit(solution)/shard_map/all_to_all | solution.py:208
  (72 shorter events, 28.4 us)
Async XLA Ops:
  2.2 5.8 %copy-start = (bf16[512,16384]{1,0:T(8,128)(2,1)S(1)}, bf16[512,16384]{1,0:T(8,128)(2,1)}, u32[]{:S(2)}) copy-start(bf16[512,16384]{1,0:T(8,128)(2,1)} %refs_3_.31) | copy-start | bytes 50331652
  10.8 22.3 %collective-permute-start.1 = (bf16[16,176,256]{2,1,0:T(8,128)(2,1)S(1)}, bf16[16,176,256]{2,1,0:T(8,128)(2,1)S(1)}, u32[]{:S(2)}, u32[]{:S(2)}) collective-permute-start(bf16[16,176,256]{2,1,0:T(8,128)(2,1)S(1)} %shard_map.95), channel_id=1, source_target_pairs={{0,32},{1,33},{2,34},{3,35},{4,36},{5,37},{6,38},{7,39},{8,40},{9,... | collective-permute-start | bytes 4325384 | tf_op jit(solution)/shard_map/ppermute | solution.py:48
  14.6 25.9 %collective-permute-start.3 = (bf16[16,176,256]{2,1,0:T(8,128)(2,1)}, bf16[16,176,256]{2,1,0:T(8,128)(2,1)}, u32[]{:S(2)}, u32[]{:S(2)}) collective-permute-start(bf16[16,176,256]{2,1,0:T(8,128)(2,1)} %shard_map.97), channel_id=1, source_target_pairs={{0,32},{1,33},{2,34},{3,35},{4,36},{5,37},{6,38},{7,39},{8,40},{9,... | collective-permute-start | bytes 4325384 | tf_op jit(solution)/shard_map/ppermute | solution.py:48
  18.8 31.1 %collective-permute-start.5 = (bf16[16,176,256]{2,1,0:T(8,128)(2,1)}, bf16[16,176,256]{2,1,0:T(8,128)(2,1)}, u32[]{:S(2)}, u32[]{:S(2)}) collective-permute-start(bf16[16,176,256]{2,1,0:T(8,128)(2,1)} %shard_map.99), channel_id=1, source_target_pairs={{0,32},{1,33},{2,34},{3,35},{4,36},{5,37},{6,38},{7,39},{8,40},{9,... | collective-permute-start | bytes 4325384 | tf_op jit(solution)/shard_map/ppermute | solution.py:48
  21.4 8.4 %collective-permute-start.14 = (bf16[16,80,256]{2,1,0:T(8,128)(2,1)S(1)}, bf16[16,80,256]{2,1,0:T(8,128)(2,1)S(1)}, u32[]{:S(2)}, u32[]{:S(2)}) collective-permute-start(bf16[16,80,256]{2,1,0:T(8,128)(2,1)S(1)} %shard_map.103), channel_id=1, source_target_pairs={{0,32},{1,33},{2,34},{3,35},{4,36},{5,37},{6,38},{7,39},{8,40},{9,... | collective-permute-start | bytes 1966088 | tf_op jit(solution)/shard_map/ppermute | solution.py:48
  24.6 8.4 %collective-permute-start.16 = (bf16[16,80,256]{2,1,0:T(8,128)(2,1)S(1)}, bf16[16,80,256]{2,1,0:T(8,128)(2,1)S(1)}, u32[]{:S(2)}, u32[]{:S(2)}) collective-permute-start(bf16[16,80,256]{2,1,0:T(8,128)(2,1)S(1)} %shard_map.105), channel_id=1, source_target_pairs={{0,32},{1,33},{2,34},{3,35},{4,36},{5,37},{6,38},{7,39},{8,40},{9,... | collective-permute-start | bytes 1966088 | tf_op jit(solution)/shard_map/ppermute | solution.py:48
  29.8 24.5 %collective-permute-start.18 = (bf16[16,80,256]{2,1,0:T(8,128)(2,1)S(1)}, bf16[16,80,256]{2,1,0:T(8,128)(2,1)S(1)}, u32[]{:S(2)}, u32[]{:S(2)}) collective-permute-start(bf16[16,80,256]{2,1,0:T(8,128)(2,1)S(1)} %shard_map.107), channel_id=1, source_target_pairs={{0,32},{1,33},{2,34},{3,35},{4,36},{5,37},{6,38},{7,39},{8,40},{9,... | collective-permute-start | bytes 1966088 | tf_op jit(solution)/shard_map/ppermute | solution.py:48
  33.0 23.0 %collective-permute-start.13 = (bf16[16,80,256]{2,1,0:T(8,128)(2,1)S(1)}, bf16[16,80,256]{2,1,0:T(8,128)(2,1)S(1)}, u32[]{:S(2)}, u32[]{:S(2)}) collective-permute-start(bf16[16,80,256]{2,1,0:T(8,128)(2,1)S(1)} %shard_map.101), channel_id=1, source_target_pairs={{0,32},{1,33},{2,34},{3,35},{4,36},{5,37},{6,38},{7,39},{8,40},{9,... | collective-permute-start | bytes 1966088 | tf_op jit(solution)/shard_map/ppermute | solution.py:48
  33.1 24.6 %collective-permute-start.15 = (bf16[4,4,80,256]{3,2,1,0:T(8,128)(2,1)S(1)}, bf16[4,4,80,256]{3,2,1,0:T(8,128)(2,1)S(1)}, u32[]{:S(2)}, u32[]{:S(2)}) collective-permute-start(bf16[4,4,80,256]{3,2,1,0:T(8,128)(2,1)S(1)} %bitcast.176), channel_id=1, source_target_pairs={{0,1},{1,2},{2,3},{3,0},{4,5},{5,6},{6,7},{7,4},{8,9},{9,10},{10,1... | collective-permute-start | bytes 1966088 | tf_op jit(solution)/shard_map/ppermute | solution.py:48
  40.6 21.5 %collective-permute-start.17 = (bf16[4,4,80,256]{3,2,1,0:T(8,128)(2,1)S(1)}, bf16[4,4,80,256]{3,2,1,0:T(8,128)(2,1)S(1)}, u32[]{:S(2)}, u32[]{:S(2)}) collective-permute-start(bf16[4,4,80,256]{3,2,1,0:T(8,128)(2,1)S(1)} %bitcast.177), channel_id=1, source_target_pairs={{0,3},{1,0},{2,1},{3,2},{4,7},{5,4},{6,5},{7,6},{8,11},{9,8},{10,9... | collective-permute-start | bytes 1966088 | tf_op jit(solution)/shard_map/ppermute | solution.py:48
  49.9 32.1 %collective-permute-start = (bf16[16,176,256]{2,1,0:T(8,128)(2,1)S(1)}, bf16[16,176,256]{2,1,0:T(8,128)(2,1)S(1)}, u32[]{:S(2)}, u32[]{:S(2)}) collective-permute-start(bf16[16,176,256]{2,1,0:T(8,128)(2,1)S(1)} %shard_map.93), channel_id=1, source_target_pairs={{0,32},{1,33},{2,34},{3,35},{4,36},{5,37},{6,38},{7,39},{8,40},{9,... | collective-permute-start | bytes 4325384 | tf_op jit(solution)/shard_map/ppermute | solution.py:48
  54.4 32.1 %collective-permute-start.2 = (bf16[4,4,176,256]{3,2,1,0:T(8,128)(2,1)S(1)}, bf16[4,4,176,256]{3,2,1,0:T(8,128)(2,1)S(1)}, u32[]{:S(2)}, u32[]{:S(2)}) collective-permute-start(bf16[4,4,176,256]{3,2,1,0:T(8,128)(2,1)S(1)} %bitcast.174), channel_id=1, source_target_pairs={{0,8},{1,9},{2,10},{3,11},{4,12},{5,13},{6,14},{7,15},{8,16},{9,17... | collective-permute-start | bytes 4325384 | tf_op jit(solution)/shard_map/ppermute | solution.py:48
  55.9 32.4 %collective-permute-start.4 = (bf16[4,4,176,256]{3,2,1,0:T(8,128)(2,1)S(1)}, bf16[4,4,176,256]{3,2,1,0:T(8,128)(2,1)S(1)}, u32[]{:S(2)}, u32[]{:S(2)}) collective-permute-start(bf16[4,4,176,256]{3,2,1,0:T(8,128)(2,1)S(1)} %bitcast.173), channel_id=1, source_target_pairs={{0,24},{1,25},{2,26},{3,27},{4,28},{5,29},{6,30},{7,31},{8,0},{9,1... | collective-permute-start | bytes 4325384 | tf_op jit(solution)/shard_map/ppermute | solution.py:48
  57.7 37.0 %collective-permute-start.6 = (bf16[4,4,176,256]{3,2,1,0:T(8,128)(2,1)S(1)}, bf16[4,4,176,256]{3,2,1,0:T(8,128)(2,1)S(1)}, u32[]{:S(2)}, u32[]{:S(2)}) collective-permute-start(bf16[4,4,176,256]{3,2,1,0:T(8,128)(2,1)S(1)} %bitcast.175), channel_id=1, source_target_pairs={{0,16},{1,17},{2,18},{3,19},{4,20},{5,21},{6,22},{7,23},{8,24},{9,... | collective-permute-start | bytes 4325384 | tf_op jit(solution)/shard_map/ppermute | solution.py:48
  62.1 17.9 %collective-permute-start.19 = (bf16[4,4,80,256]{3,2,1,0:T(8,128)(2,1)S(1)}, bf16[4,4,80,256]{3,2,1,0:T(8,128)(2,1)S(1)}, u32[]{:S(2)}, u32[]{:S(2)}) collective-permute-start(bf16[4,4,80,256]{3,2,1,0:T(8,128)(2,1)S(1)} %bitcast.178), channel_id=1, source_target_pairs={{0,2},{1,3},{2,0},{3,1},{4,6},{5,7},{6,4},{7,5},{8,10},{9,11},{10,... | collective-permute-start | bytes 1966088 | tf_op jit(solution)/shard_map/ppermute | solution.py:48
  80.4 18.4 %collective-permute-start.20 = (bf16[4,80,256]{2,1,0:T(8,128)(2,1)S(1)}, bf16[4,80,256]{2,1,0:T(8,128)(2,1)S(1)}, u32[]{:S(2)}, u32[]{:S(2)}) collective-permute-start(bf16[4,80,256]{2,1,0:T(8,128)(2,1)S(1)} %get-tuple-element.21), channel_id=1, source_target_pairs={{0,8},{1,9},{2,10},{3,11},{4,12},{5,13},{6,14},{7,15},{8,16},{9,17... | collective-permute-start | bytes 491528 | tf_op jit(solution)/shard_map/ppermute | solution.py:48
  81.9 18.1 %collective-permute-start.21 = (bf16[4,80,256]{2,1,0:T(8,128)(2,1)S(1)}, bf16[4,80,256]{2,1,0:T(8,128)(2,1)S(1)}, u32[]{:S(2)}, u32[]{:S(2)}) collective-permute-start(bf16[4,80,256]{2,1,0:T(8,128)(2,1)S(1)} %get-tuple-element.20), channel_id=1, source_target_pairs={{0,24},{1,25},{2,26},{3,27},{4,28},{5,29},{6,30},{7,31},{8,0},{9,1... | collective-permute-start | bytes 491528 | tf_op jit(solution)/shard_map/ppermute | solution.py:48
  86.5 13.5 %collective-permute-start.22 = (bf16[4,80,256]{2,1,0:T(8,128)(2,1)S(1)}, bf16[4,80,256]{2,1,0:T(8,128)(2,1)S(1)}, u32[]{:S(2)}, u32[]{:S(2)}) collective-permute-start(bf16[4,80,256]{2,1,0:T(8,128)(2,1)S(1)} %get-tuple-element.19), channel_id=1, source_target_pairs={{0,16},{1,17},{2,18},{3,19},{4,20},{5,21},{6,22},{7,23},{8,24},{9,... | collective-permute-start | bytes 491528 | tf_op jit(solution)/shard_map/ppermute | solution.py:48
  95.5 9.1 %collective-permute-start.7 = (bf16[4,176,256]{2,1,0:T(8,128)(2,1)S(1)}, bf16[4,176,256]{2,1,0:T(8,128)(2,1)S(1)}, u32[]{:S(2)}, u32[]{:S(2)}) collective-permute-start(bf16[4,176,256]{2,1,0:T(8,128)(2,1)S(1)} %get-tuple-element.17), channel_id=1, source_target_pairs={{0,64},{1,65},{2,66},{3,67},{4,68},{5,69},{6,70},{7,71},{8,72},{9,... | collective-permute-start | bytes 1081352 | tf_op jit(solution)/shard_map/ppermute | solution.py:48
  97.1 8.7 %collective-permute-start.8 = (bf16[4,176,256]{2,1,0:T(8,128)(2,1)S(1)}, bf16[4,176,256]{2,1,0:T(8,128)(2,1)S(1)}, u32[]{:S(2)}, u32[]{:S(2)}) collective-permute-start(bf16[4,176,256]{2,1,0:T(8,128)(2,1)S(1)} %get-tuple-element.16), channel_id=1, source_target_pairs={{0,68},{1,69},{2,70},{3,71},{4,64},{5,65},{6,66},{7,67},{8,76},{9,... | collective-permute-start | bytes 1081352 | tf_op jit(solution)/shard_map/ppermute | solution.py:48
  98.8 11.4 %collective-permute-start.9 = (bf16[4,176,256]{2,1,0:T(8,128)(2,1)S(1)}, bf16[4,176,256]{2,1,0:T(8,128)(2,1)S(1)}, u32[]{:S(2)}, u32[]{:S(2)}) collective-permute-start(bf16[4,176,256]{2,1,0:T(8,128)(2,1)S(1)} %get-tuple-element.15), channel_id=1, source_target_pairs={{0,4},{1,5},{2,6},{3,7},{4,0},{5,1},{6,2},{7,3},{8,12},{9,13},{10,... | collective-permute-start | bytes 1081352 | tf_op jit(solution)/shard_map/ppermute | solution.py:48
  100.1 13.5 %collective-permute-start.23 = (bf16[80,256]{1,0:T(8,128)(2,1)S(1)}, bf16[80,256]{1,0:T(8,128)(2,1)S(1)}, u32[]{:S(2)}, u32[]{:S(2)}) collective-permute-start(bf16[80,256]{1,0:T(8,128)(2,1)S(1)} %get-tuple-element.25), channel_id=1, source_target_pairs={{0,64},{1,65},{2,66},{3,67},{4,68},{5,69},{6,70},{7,71},{8,72},{9,... | collective-permute-start | bytes 122888 | tf_op jit(solution)/shard_map/ppermute | solution.py:48
  101.6 12.5 %collective-permute-start.24 = (bf16[80,256]{1,0:T(8,128)(2,1)S(1)}, bf16[80,256]{1,0:T(8,128)(2,1)S(1)}, u32[]{:S(2)}, u32[]{:S(2)}) collective-permute-start(bf16[80,256]{1,0:T(8,128)(2,1)S(1)} %get-tuple-element.27), channel_id=1, source_target_pairs={{0,68},{1,69},{2,70},{3,71},{4,64},{5,65},{6,66},{7,67},{8,76},{9,... | collective-permute-start | bytes 122888 | tf_op jit(solution)/shard_map/ppermute | solution.py:48
  104.6 9.5 %collective-permute-start.25 = (bf16[80,256]{1,0:T(8,128)(2,1)S(1)}, bf16[80,256]{1,0:T(8,128)(2,1)S(1)}, u32[]{:S(2)}, u32[]{:S(2)}) collective-permute-start(bf16[80,256]{1,0:T(8,128)(2,1)S(1)} %get-tuple-element.26), channel_id=1, source_target_pairs={{0,4},{1,5},{2,6},{3,7},{4,0},{5,1},{6,2},{7,3},{8,12},{9,13},{10,... | collective-permute-start | bytes 122888 | tf_op jit(solution)/shard_map/ppermute | solution.py:48
  110.2 16.3 %copy-start.1 = (f32[512,512]{1,0:T(8,128)S(1)}, f32[512,512]{1,0:T(8,128)}, u32[]{:S(2)}) copy-start(f32[512,512]{1,0:T(8,128)} %master.1) | copy-start | bytes 3145732
  110.2 16.3 %copy-start.2 = (f32[512,512]{1,0:T(8,128)S(1)}, f32[512,512]{1,0:T(8,128)}, u32[]{:S(2)}) copy-start(f32[512,512]{1,0:T(8,128)} %moment1.1) | copy-start | bytes 3145732
  110.2 16.3 %copy-start.3 = (f32[512,512]{1,0:T(8,128)S(1)}, f32[512,512]{1,0:T(8,128)}, u32[]{:S(2)}) copy-start(f32[512,512]{1,0:T(8,128)} %moment2.1) | copy-start | bytes 3145732
  110.3 5.8 %collective-permute-start.10 = (bf16[176,256]{1,0:T(8,128)(2,1)S(1)}, bf16[176,256]{1,0:T(8,128)(2,1)S(1)}, u32[]{:S(2)}, u32[]{:S(2)}) collective-permute-start(bf16[176,256]{1,0:T(8,128)(2,1)S(1)} %get-tuple-element.22), channel_id=1, source_target_pairs={{0,1},{1,2},{2,3},{3,0},{4,5},{5,6},{6,7},{7,4},{8,9},{9,10},{10,1... | collective-permute-start | bytes 270344 | tf_op jit(solution)/shard_map/ppermute | solution.py:48
  110.4 6.3 %collective-permute-start.11 = (bf16[176,256]{1,0:T(8,128)(2,1)S(1)}, bf16[176,256]{1,0:T(8,128)(2,1)S(1)}, u32[]{:S(2)}, u32[]{:S(2)}) collective-permute-start(bf16[176,256]{1,0:T(8,128)(2,1)S(1)} %get-tuple-element.24), channel_id=1, source_target_pairs={{0,3},{1,0},{2,1},{3,2},{4,7},{5,4},{6,5},{7,6},{8,11},{9,8},{10,9... | collective-permute-start | bytes 270344 | tf_op jit(solution)/shard_map/ppermute | solution.py:48
  113.6 6.0 %collective-permute-start.12 = (bf16[176,256]{1,0:T(8,128)(2,1)S(1)}, bf16[176,256]{1,0:T(8,128)(2,1)S(1)}, u32[]{:S(2)}, u32[]{:S(2)}) collective-permute-start(bf16[176,256]{1,0:T(8,128)(2,1)S(1)} %get-tuple-element.23), channel_id=1, source_target_pairs={{0,2},{1,3},{2,0},{3,1},{4,6},{5,7},{6,4},{7,5},{8,10},{9,11},{10,... | collective-permute-start | bytes 270344 | tf_op jit(solution)/shard_map/ppermute | solution.py:48
  119.8 5.0 %collective-permute-start.26 = (bf16[256,256]{1,0:T(8,128)(2,1)S(1)}, bf16[256,256]{1,0:T(8,128)(2,1)S(1)}, u32[]{:S(2)}, u32[]{:S(2)}) collective-permute-start(bf16[256,256]{1,0:T(8,128)(2,1)S(1)} %get-tuple-element.29), channel_id=1, source_target_pairs={{0,64},{1,65},{2,66},{3,67},{4,68},{5,69},{6,70},{7,71},{8,72},{9,... | collective-permute-start | bytes 393224 | tf_op jit(solution)/shard_map/ppermute | solution.py:48
  124.9 1.6 %collective-permute-start.27 = (bf16[2,256,256]{2,1,0:T(8,128)(2,1)S(1)}, bf16[2,256,256]{2,1,0:T(8,128)(2,1)S(1)}, u32[]{:S(2)}, u32[]{:S(2)}) collective-permute-start(bf16[2,256,256]{2,1,0:T(8,128)(2,1)S(1)} %pad_maximum_fusion.own), channel_id=1, source_target_pairs={{0,32},{1,33},{2,34},{3,35},{4,36},{5,37},{6,38},{7,39},{8,40},{9,... | collective-permute-start | bytes 786440 | tf_op jit(solution)/shard_map/ppermute | solution.py:48
  (1 other events, 0.8 us)

commit v2 on v0

v2 whole, which is shorter than its diff:
```python
import jax
import jax.numpy as jnp
from jax import lax
from jax.experimental import pallas as pl
from jax.experimental.pallas import tpu as pltpu
from jax.sharding import PartitionSpec as P

BLOCK_ROWS = 2
AXES = ("rep", "fsdp")
SIDE = 4
PARTS = ((0, 352), (352, 512))

bias_first = 1.0 - 0.9**10
bias_second = 1.0 - 0.95**10

ORDERS = (((0, 1, 2), (1, 2, 0)), ((2, 0, 1), (2, 0, 1)))


def coords(index):
    rep, fsdp = divmod(index, 32)
    y_lo, core = divmod(rep, 2)
    x, rest = divmod(fsdp, 8)
    y_hi, z = divmod(rest, 4)
    return x, y_hi * 2 + y_lo, z, core


def index_of(x, y, z, core):
    return ((y % 2) * 2 + core) * 32 + x * 8 + (y // 2) * 4 + z


def ring_pairs(part, stage, distance):
    pairs = []
    for device in range(128):
        place = list(coords(device))
        axis = ORDERS[part][place[3]][stage]
        place[axis] = (place[axis] + distance) % SIDE
        pairs.append((device, index_of(*place)))
    return pairs


def swap_pairs(part, odd):
    pairs = []
    for device in range(128):
        place = list(coords(device))
        axis = ORDERS[part][place[3]][0]
        place[axis] = (((place[axis] + odd) ^ 1) - odd) % SIDE
        pairs.append((device, index_of(*place)))
    return pairs


def rep_pairs(bit):
    return [(device, (((device // 32) ^ bit) * 32) + device % 32) for device in range(128)]


def send(value, pairs):
    return lax.ppermute(value, AXES, pairs)


def split_body(cot, tokens, *refs):
    own, other = refs[:4], refs[4:8]
    cot_t, held, kept, in_sem, cot_sem, sem = refs[8:]
    steps, _, lanes = held.shape
    rep, fsdp = lax.axis_index("rep"), lax.axis_index("fsdp")
    core, y_lo = lax.rem(rep, 2), rep // 2
    place = (fsdp // 8, lax.rem(fsdp // 4, 2) * 2 + y_lo, lax.rem(fsdp, 4))
    count = SIDE * SIDE
    ahead = 2
    first_rows = 2 * count * (PARTS[0][1] - PARTS[0][0]) // 2

    def fetch(step):
        columns = pl.ds(pl.multiple_of(step * lanes, lanes), lanes)
        return pltpu.make_async_copy(tokens.at[:, columns], held.at[step], in_sem.at[step])

    def drain(slot):
        pltpu.make_async_copy(kept.at[slot], kept.at[slot], sem.at[slot]).wait()

    def group(axis, away):
        parity = lax.rem(place[axis], 2)
        is_even = away == 1 + 2 * parity
        is_odd = away == 3 - 2 * parity
        is_far = away == 2
        one = lambda flag: jnp.where(flag, 1, 0)
        return (
            (one(is_even) + one(is_far), one(is_far) + one(is_odd)),
            (one(is_odd) + one(is_far), one(is_far) + one(is_even)),
        )

    cot_copy = pltpu.make_async_copy(cot, cot_t.at[1], cot_sem)
    cot_copy.start()
    for step in range(ahead):
        fetch(step).start()
    cot_copy.wait()
    cot_t[0] = cot_t[1].T

    def one_step(step, carry):
        slot = lax.rem(step, 2)
        fetch(step).wait()

        @pl.when(step + ahead < steps)
        def _():
            fetch(step + ahead).start()

        @pl.when(step >= 2)
        def _():
            drain(slot)

        total = jnp.dot(cot_t[0], held[step], preferred_element_type=jnp.float32)
        for at in range(count):
            kept[slot, at] = total[:, at * 128 : (at + 1) * 128].astype(jnp.bfloat16)

        away_x = lax.rem(step // 2 - place[0] + SIDE, SIDE)
        groups_x = group(0, away_x)
        for z in range(SIDE):
            away_z = lax.rem(z - place[2] + SIDE, SIDE)
            groups_z = group(2, away_z)
            for low in range(2):
                away_y = lax.rem(lax.rem(step, 2) * 2 + low - place[1] + SIDE, SIDE)
                groups_y = group(1, away_y)
                for side, arrays in ((1, other), (0, own)):
                    target = core if side == 0 else 1 - core
                    source = z * 4 + low * 2 + target
                    is_first = target == 0
                    rest_a = jnp.where(is_first, away_y * 4 + away_z, away_z * 4 + away_x)
                    rest_b = away_x * 4 + away_y
                    for odd in range(2):
                        for part in range(2):
                            low_column, high_column = PARTS[part]
                            width = (high_column - low_column) // 2
                            column = low_column + odd * width
                            if part == 0:
                                sent = jnp.where(is_first, groups_x[odd][0], groups_y[odd][0])
                                second = jnp.where(is_first, groups_x[odd][1], groups_y[odd][1])
                                row = (second * count + rest_a) * width
                            else:
                                sent, second = groups_z[odd]
                                row = first_rows + (second * count + rest_b) * width
                            row = pl.multiple_of(row, 16)
                            for array, flag in ((arrays[odd], 1), (arrays[2 + odd], 0)):

                                @pl.when(sent == flag)
                                def _(
                                    array=array, source=source, column=column, width=width, row=row
                                ):
                                    pltpu.make_async_copy(
                                        kept.at[slot, source, pl.ds(column, width)],
                                        array.at[pl.ds(row, width)],
                                        sem.at[slot],
                                    ).start()

        return carry

    lax.fori_loop(0, steps, one_step, 0)
    drain(0)
    drain(1)


def split_sums(tokens, cotangent):
    depth, rows = tokens.shape
    columns = cotangent.shape[1]
    lanes = 16 * 128
    steps = rows // lanes
    count = SIDE * SIDE
    sums = jax.ShapeDtypeStruct((count * columns, 128), jnp.bfloat16)
    anywhere = pl.BlockSpec(memory_space=pl.ANY)
    results = pl.pallas_call(
        split_body,
        out_shape=[sums] * 8,
        in_specs=[anywhere] * 2,
        out_specs=[anywhere] * 8,
        scratch_shapes=[
            pltpu.VMEM((2, columns, depth), jnp.bfloat16),
            pltpu.VMEM((steps, depth, lanes), jnp.bfloat16),
            pltpu.VMEM((2, count, columns, 128), jnp.bfloat16),
            pltpu.SemaphoreType.DMA((steps,)),
            pltpu.SemaphoreType.DMA,
            pltpu.SemaphoreType.DMA((2,)),
        ],
        compiler_params=pltpu.CompilerParams(vmem_limit_bytes=56 * 1024 * 1024),
        cost_estimate=pl.CostEstimate(
            flops=2 * depth * rows * columns, bytes_accessed=4 * depth * rows, transcendentals=0
        ),
    )(cotangent, tokens)
    return results[:4], results[4:]


def updated(grad, master, moment1, moment2):
    first = 0.9 * moment1 + 0.1 * grad
    second = 0.95 * moment2 + 0.05 * grad * grad
    update = first / bias_first / (jnp.sqrt(second / bias_second) + 1e-08)
    return master - 0.05 * (update + 0.1 * master), first, second


def rep_grad(own, other, at):
    rep = lax.axis_index("rep")
    core, y_lo = lax.rem(rep, 2), rep // 2
    index = y_lo if at // 2 == 0 else 1 - y_lo
    piece = jnp.where(core == at % 2, own[index], other[index])
    return piece.T.astype(jnp.float32)


def weight_body(own, other, master, moment1, moment2, selector, outgoing, weight):
    for at in range(4):
        rows = slice(at * 128, (at + 1) * 128)
        new, _, _ = updated(rep_grad(own, other, at), master[rows], moment1[rows], moment2[rows])
        weight[rows] = new.astype(jnp.bfloat16)
    chosen = jnp.dot(selector[...], weight[...], preferred_element_type=jnp.float32)
    outgoing[...] = chosen.astype(jnp.bfloat16).reshape(outgoing.shape)


def adam_body(own, other, master, moment1, moment2, *refs):
    outs, kept, sem = refs[:3], refs[3:6], refs[6]
    copies = []
    for at in range(4):
        rows = slice(at * 128, (at + 1) * 128)
        values = updated(rep_grad(own, other, at), master[rows], moment1[rows], moment2[rows])
        for k in range(3):
            kept[k][rows] = values[k]
            copy = pltpu.make_async_copy(
                kept[k].at[pl.ds(at * 128, 128)], outs[k].at[pl.ds(at * 128, 128)], sem.at[k, at]
            )
            copy.start()
            copies.append(copy)
    for copy in copies:
        copy.wait()


def adam(own, other, master, moment1, moment2, selector):
    rows, columns = master.shape
    size = rows * columns
    params = pltpu.CompilerParams(vmem_limit_bytes=32 * 1024 * 1024)
    vmem = pl.BlockSpec(memory_space=pltpu.VMEM)
    outgoing = pl.pallas_call(
        weight_body,
        out_shape=jax.ShapeDtypeStruct(
            (selector.shape[0] // BLOCK_ROWS, BLOCK_ROWS, columns), jnp.bfloat16
        ),
        in_specs=[vmem] * 6,
        out_specs=vmem,
        scratch_shapes=[pltpu.VMEM((rows, columns), jnp.bfloat16)],
        compiler_params=params,
        cost_estimate=pl.CostEstimate(
            flops=20 * size, bytes_accessed=14 * size, transcendentals=0
        ),
    )(own, other, master, moment1, moment2, selector)
    state = pl.pallas_call(
        adam_body,
        out_shape=[jax.ShapeDtypeStruct((rows, columns), jnp.float32)] * 3,
        in_specs=[vmem] * 5,
        out_specs=[pl.BlockSpec(memory_space=pl.ANY)] * 3,
        scratch_shapes=[pltpu.VMEM((rows, columns), jnp.float32)] * 3
        + [pltpu.SemaphoreType.DMA((3, 4))],
        compiler_params=params,
        cost_estimate=pl.CostEstimate(
            flops=20 * size, bytes_accessed=26 * size, transcendentals=0
        ),
    )(own, other, master, moment1, moment2)
    return outgoing, state


def add(values):
    return sum(value.astype(jnp.float32) for value in values).astype(jnp.bfloat16)


def after(value, *earlier):
    return lax.optimization_barrier((value, *earlier))[0]


def summed(own, other, early):
    count = SIDE * SIDE
    halves = [(last - first) // 2 for first, last in PARTS]
    cut = 2 * count * halves[0]
    rows = (slice(0, cut), slice(cut, None))
    beside = [send(other[odd], rep_pairs(1)) for odd in range(2)]
    beside += [send(after(other[2 + odd], beside[odd]), rep_pairs(1)) for odd in range(2)]
    came = {}
    for odd in range(2):
        both = after(beside[odd], *early)
        for part in range(2):
            value = add([own[odd][rows[part]], both[rows[part]]])
            came[part, odd] = send(value, swap_pairs(part, odd))
    near = {}
    for odd in range(2):
        for part in range(2):
            whole = add([own[2 + odd][rows[part]], beside[2 + odd][rows[part]], came[part, odd]])
            middle = whole.shape[0] // 2
            got = send(whole[middle:], swap_pairs(part, 1 - odd))
            near[part, odd] = (whole[:middle], got)
    values = []
    for part in range(2):
        shape = (SIDE, SIDE, halves[part], 128)
        pairs = [[value.reshape(shape) for value in near[part, odd]] for odd in range(2)]
        sums = [jnp.stack([add([v[at] for v in pair]) for pair in pairs]) for at in range(SIDE)]
        values.append([sums[0]] + [send(sums[at], ring_pairs(part, 1, at)) for at in (1, 3, 2)])
    mine = []
    for part in range(2):
        sums = [add([value[:, at] for value in values[part]]) for at in range(SIDE)]
        got = [sums[0]] + [send(sums[at], ring_pairs(part, 2, at)) for at in (1, 3, 2)]
        mine.append(add(got).reshape(2 * halves[part], 128))
    return jnp.concatenate(mine, axis=0)


def select_blocks(owner, local_blocks, capacity, fsdp_count):
    owners = lax.dynamic_slice_in_dim(owner, lax.axis_index("fsdp") * local_blocks, local_blocks)
    in_row = owners // fsdp_count == lax.axis_index("rep")
    target = owners % fsdp_count
    places = jnp.arange(local_blocks, dtype=jnp.int32)
    equal = owners[:, None] == owners[None, :]
    earlier = places[None, :] < places[:, None]
    ranks = jnp.sum(jnp.logical_and(equal, earlier), axis=1).astype(jnp.int32)
    slots = jnp.where(in_row, target * capacity + ranks, -1)
    row_slots = jnp.repeat(slots, BLOCK_ROWS) * BLOCK_ROWS + jnp.tile(
        jnp.arange(BLOCK_ROWS, dtype=jnp.int32), local_blocks
    )
    slot_rows = jnp.arange(fsdp_count * capacity * BLOCK_ROWS, dtype=jnp.int32)
    return (slot_rows[:, None] == row_slots[None, :]).astype(jnp.bfloat16)


def per_device(tokens, cotangent, master, moment1, moment2, owner):
    fsdp_count = lax.axis_size("fsdp")
    rep_count = lax.axis_size("rep")
    shard_rows = master.shape[0]
    columns = master.shape[1]
    local_blocks = shard_rows // BLOCK_ROWS
    capacity = 2 * local_blocks // (rep_count * fsdp_count)
    selector = select_blocks(owner, local_blocks, capacity, fsdp_count)
    mine = summed(*split_sums(tokens, cotangent), [selector])
    beside = send(mine, rep_pairs(2))
    own = jnp.stack([mine, beside])
    other = send(own, rep_pairs(1))
    outgoing, state = adam(own, other, master, moment1, moment2, selector)
    outgoing = outgoing.reshape(fsdp_count, capacity, BLOCK_ROWS, columns)
    received = lax.all_to_all(outgoing, "fsdp", split_axis=0, concat_axis=0, tiled=True)
    upload = received.reshape(fsdp_count * capacity, BLOCK_ROWS, columns)
    return (*state, upload)


def solution(mesh):
    placed = (
        P(("rep", "fsdp"), None),
        P(("rep", "fsdp"), None),
        P("fsdp", None),
        P("fsdp", None),
        P("fsdp", None),
        P(),
    )
    return jax.shard_map(
        per_device,
        mesh=mesh,
        in_specs=placed,
        out_specs=(
            P("fsdp", None),
            P("fsdp", None),
            P("fsdp", None),
            P(("rep", "fsdp"), None, None),
        ),
        check_vma=False,
    )
```

time: 324 us -> 121 us (0.37)
  waiting for transfers between devices: 264 us -> 40.2 us
  starting transfers between devices: 0.08 us -> 47.9 us
  blocking collectives: 20.4 us -> 0 us
  Pallas kernels: 0 us -> 19.1 us
  matrix products: 18.6 us -> 0 us
  between operations: 14.1 us -> 1.02 us
    reduce_scatter x1 -> x0, waiting for transfers between devices: 227 us -> none  [per_device(): lax.psum_scatter(lax.dot_general(tokens, cotangent, (((0,), (0,)), ((), (...]
    ppermute x0 -> x26, starting transfers between devices: none -> 41 us  [send(): return lax.ppermute(value, AXES, pairs)]
    psum x1 -> x0, waiting for transfers between devices: 37.2 us -> none  [per_device(): grad = lax.psum(shard_grad, 'rep').astype(jnp.float32)]
    ppermute x0 -> x26, waiting for transfers between devices: none -> 32.2 us  [send(): return lax.ppermute(value, AXES, pairs)]
    all_to_all x1 -> x0, blocking collectives: 20.4 us -> none  [per_device(): lax.all_to_all(outgoing, 'fsdp', split_axis=0, concat_axis=0, tiled=True)]
    pallas_call x0 -> x3, Pallas kernels: none -> 19.1 us  [the longest x1 15.7 us: split_sums(): pl.pallas_call(split_body, out_shape=[sums] * 8, in_specs=[anywhere] * 2,...]
    dot_general x2 -> x0, matrix products: 18.6 us -> none  [the longest x1 18.4 us: per_device(): lax.dot_general(tokens, cotangent, (((0,), (0,)), ((), ())), preferred_el...]
    all_to_all x0 -> x1, waiting for transfers between devices: none -> 7.96 us  [per_device(): lax.all_to_all(outgoing, 'fsdp', split_axis=0, concat_axis=0, tiled=True)]
  transfers between devices with their start and end apart: 2 -> 27, of which waited for: 2 -> 14; matrix products, arithmetic and copies ran while one was open for 0% -> 7% of each run, Pallas kernels for 0% -> 2%
where the time goes in v2:
time: 121 us; the launch traced here: 120 us
  starting transfers between devices  47.9 us (40%)
  waiting for transfers between devices  40.2 us (33%)
  Pallas kernels  19.1 us (16%)
  other arithmetic  7.6 us (6%)
  local copies, waits for them, and re-layouts  4.58 us (4%)
    ppermute x26, starting transfers between devices, send(): return lax.ppermute(value, AXES, pairs)  41 us
    ppermute x26, waiting for transfers between devices, send(): return lax.ppermute(value, AXES, pairs)  32.2 us
    pallas_call x1, Pallas kernels, split_sums(): pl.pallas_call(split_body, out_shape=[sums] * 8, in_specs=[anywhere] * 2,...  15.7 us
    all_to_all x1, waiting for transfers between devices, per_device(): lax.all_to_all(outgoing, 'fsdp', split_axis=0, concat_axis=0, tiled=True)  7.96 us
    all_to_all x1, starting transfers between devices, per_device(): lax.all_to_all(outgoing, 'fsdp', split_axis=0, concat_axis=0, tiled=True)  6.96 us
    convert_element_type x14, other arithmetic, add(): sum((value.astype(jnp.float32) for value in values)).astype(jnp.bfloat16)  6.08 us
    unnamed x25, local copies, waits for them, and re-layouts  3.54 us
  transfers between devices with their start and end apart: 27, of which 14 were waited for; matrix products, arithmetic and copies ran while one was open for 7% of the time, Pallas kernels for 2%

profile of v2, /device:TPU:0, one launch (start us, length us, event | category | flops | bytes accessed | tf_op | source)
XLA Modules:
  0.0 120.4 jit_solution(8230560853541922170)
XLA Ops:
  0.6 15.7 %shard_map.93 = (bf16[8192,128]{1,0:T(8,128)(2,1)}, bf16[8192,128]{1,0:T(8,128)(2,1)}, bf16[8192,128]{1,0:T(8,128)(2,1)}, bf16[8192,128]{1,0:T(8,128)(2,1)}, bf1...) custom-call(bf16[512,512]{1,0:T(8,128)(2,1)} %cot.1, ...), custom_call_target="tpu_custom_call" | custom-call | flops 8589934592 | bytes 33554432 | tf_op jit(solution)/shard_map/pallas_call | solution.py:165
  18.9 4.0 %collective-permute-done = bf16[8192,128]{1,0:T(8,128)(2,1)} collective-permute-done((bf16[8192,128]{1,0:T(8,128)(2,1)}, bf16[8192,128]{1,0:T(8,128)(2,1)}, u32[]{:S(2)}, u32[]{:S(2)}) %collective-permute-start) | collective-permute-done | bytes 2097184 | tf_op jit(solution)/shard_map/ppermute | solution.py:56
  23.0 1.5 %add_convert_fusion.7 = bf16[2560,128]{1,0:T(8,128)(2,1)S(1)} fusion(bf16[8192,128]{1,0:T(8,128)(2,1)} %collective-permute-done, bf16[8192,128]{1,0:T(8,128)(2,1)} %get-tuple-element.23), kind=kLoop, calls=%fused_computation.7 | loop fusion | flops 1310720 | bytes 1966080 | tf_op jit(solution)/shard_map/convert_element_type | solution.py:261
  24.4 2.0 %collective-permute-start.14 = (bf16[2560,128]{1,0:T(8,128)(2,1)S(1)}, bf16[2560,128]{1,0:T(8,128)(2,1)S(1)}, u32[]{:S(2)}, u32[]{:S(2)}) collective-permute-start(bf16[2560,128]{1,0:T(8,128)(2,1)S(1)} %add_convert_fusion.7), channel_id=1, source_target_pairs={{0,1},{1,0},{2,3},{3,2},{4,5},{5,4},{6,7},{7,6},{8,9},{9,8},{10,11... | collective-permute-start | bytes 1966088 | tf_op jit(solution)/shard_map/ppermute | solution.py:56
  26.5 1.7 %add_convert_fusion.3 = bf16[5632,128]{1,0:T(8,128)(2,1)S(1)} fusion(bf16[8192,128]{1,0:T(8,128)(2,1)} %collective-permute-done, bf16[8192,128]{1,0:T(8,128)(2,1)S(1)} %copy-done.9), kind=kLoop, calls=%fused_computation.3 | loop fusion | flops 2883584 | bytes 4325376 | tf_op jit(solution)/shard_map/convert_element_type | solution.py:261
  28.2 1.6 %collective-permute-start.2 = (bf16[5632,128]{1,0:T(8,128)(2,1)S(1)}, bf16[5632,128]{1,0:T(8,128)(2,1)S(1)}, u32[]{:S(2)}, u32[]{:S(2)}) collective-permute-start(bf16[5632,128]{1,0:T(8,128)(2,1)S(1)} %add_convert_fusion.3), channel_id=1, source_target_pairs={{0,8},{1,9},{2,10},{3,11},{4,12},{5,13},{6,14},{7,15},{8,0},{9,1},... | collective-permute-start | bytes 4325384 | tf_op jit(solution)/shard_map/ppermute | solution.py:56
  30.4 2.8 %collective-permute-start.16 = (bf16[2560,128]{1,0:T(8,128)(2,1)S(1)}, bf16[2560,128]{1,0:T(8,128)(2,1)S(1)}, u32[]{:S(2)}, u32[]{:S(2)}) collective-permute-start(bf16[2560,128]{1,0:T(8,128)(2,1)S(1)} %add_convert_fusion.5), channel_id=1, source_target_pairs={{0,3},{1,2},{2,1},{3,0},{4,7},{5,6},{6,5},{7,4},{8,11},{9,10},{10,... | collective-permute-start | bytes 1966088 | tf_op jit(solution)/shard_map/ppermute | solution.py:56
  33.3 2.3 %collective-permute-start.6 = (bf16[5632,128]{1,0:T(8,128)(2,1)S(1)}, bf16[5632,128]{1,0:T(8,128)(2,1)S(1)}, u32[]{:S(2)}, u32[]{:S(2)}) collective-permute-start(bf16[5632,128]{1,0:T(8,128)(2,1)S(1)} %add_convert_fusion.1), channel_id=1, source_target_pairs={{0,24},{1,25},{2,26},{3,27},{4,28},{5,29},{6,30},{7,31},{8,16},{9,... | collective-permute-start | bytes 4325384 | tf_op jit(solution)/shard_map/ppermute | solution.py:56
  35.6 5.9 %collective-permute-done.14 = bf16[2560,128]{1,0:T(8,128)(2,1)S(1)} collective-permute-done((bf16[2560,128]{1,0:T(8,128)(2,1)S(1)}, bf16[2560,128]{1,0:T(8,128)(2,1)S(1)}, u32[]{:S(2)}, u32[]{:S(2)}) %collective-permute-start.14) | collective-permute-done | bytes 655392 | tf_op jit(solution)/shard_map/ppermute | solution.py:56
  41.8 3.9 %collective-permute-start.15 = (bf16[1280,128]{1,0:T(8,128)(2,1)S(1)}, bf16[1280,128]{1,0:T(8,128)(2,1)S(1)}, u32[]{:S(2)}, u32[]{:S(2)}) collective-permute-start(bf16[1280,128]{1,0:T(8,128)(2,1)S(1)} %slice.428), channel_id=1, source_target_pairs={{0,3},{1,2},{2,1},{3,0},{4,7},{5,6},{6,5},{7,4},{8,11},{9,10},{10,... | collective-permute-start | bytes 983048 | tf_op jit(solution)/shard_map/ppermute | solution.py:56
  45.8 1.5 %collective-permute-done.2 = bf16[5632,128]{1,0:T(8,128)(2,1)S(1)} collective-permute-done((bf16[5632,128]{1,0:T(8,128)(2,1)S(1)}, bf16[5632,128]{1,0:T(8,128)(2,1)S(1)}, u32[]{:S(2)}, u32[]{:S(2)}) %collective-permute-start.2) | collective-permute-done | bytes 1441824 | tf_op jit(solution)/shard_map/ppermute | solution.py:56
  47.9 2.9 %collective-permute-start.3 = (bf16[2816,128]{1,0:T(8,128)(2,1)S(1)}, bf16[2816,128]{1,0:T(8,128)(2,1)S(1)}, u32[]{:S(2)}, u32[]{:S(2)}) collective-permute-start(bf16[2816,128]{1,0:T(8,128)(2,1)S(1)} %slice.390), channel_id=1, source_target_pairs={{0,24},{1,25},{2,26},{3,27},{4,28},{5,29},{6,30},{7,31},{8,16},{9,... | collective-permute-start | bytes 2162696 | tf_op jit(solution)/shard_map/ppermute | solution.py:56
  51.5 2.0 %collective-permute-done.6 = bf16[5632,128]{1,0:T(8,128)(2,1)S(1)} collective-permute-done((bf16[5632,128]{1,0:T(8,128)(2,1)S(1)}, bf16[5632,128]{1,0:T(8,128)(2,1)S(1)}, u32[]{:S(2)}, u32[]{:S(2)}) %collective-permute-start.6) | collective-permute-done | bytes 1441824 | tf_op jit(solution)/shard_map/ppermute | solution.py:56
  54.2 1.7 %collective-permute-done.15 = bf16[1280,128]{1,0:T(8,128)(2,1)S(1)} collective-permute-done((bf16[1280,128]{1,0:T(8,128)(2,1)S(1)}, bf16[1280,128]{1,0:T(8,128)(2,1)S(1)}, u32[]{:S(2)}, u32[]{:S(2)}) %collective-permute-start.15) | collective-permute-done | bytes 327712 | tf_op jit(solution)/shard_map/ppermute | solution.py:56
  56.0 3.8 %collective-permute-done.17 = bf16[1280,128]{1,0:T(8,128)(2,1)S(1)} collective-permute-done((bf16[1280,128]{1,0:T(8,128)(2,1)S(1)}, bf16[1280,128]{1,0:T(8,128)(2,1)S(1)}, u32[]{:S(2)}, u32[]{:S(2)}) %collective-permute-start.17) | collective-permute-done | bytes 327712 | tf_op jit(solution)/shard_map/ppermute | solution.py:56
  59.9 1.5 %collective-permute-start.18 = (bf16[2,4,80,128]{3,2,0,1:T(8,128)(2,1)S(1)}, bf16[2,4,80,128]{3,2,0,1:T(8,128)(2,1)S(1)}, u32[]{:S(2)}, u32[]{:S(2)}) collective-permute-start(bf16[2,4,80,128]{3,2,0,1:T(8,128)(2,1)S(1)} %pad_maximum_fusion.4), channel_id=1, source_target_pairs={{0,8},{1,9},{2,10},{3,11},{4,12},{5,13},{6,14},{7,15},{8,16},{9,17... | collective-permute-start | bytes 491528 | tf_op jit(solution)/shard_map/ppermute | solution.py:56
  61.5 1.9 %collective-permute-start.19 = (bf16[2,4,80,128]{3,2,0,1:T(8,128)(2,1)S(1)}, bf16[2,4,80,128]{3,2,0,1:T(8,128)(2,1)S(1)}, u32[]{:S(2)}, u32[]{:S(2)}) collective-permute-start(bf16[2,4,80,128]{3,2,0,1:T(8,128)(2,1)S(1)} %pad_maximum_fusion.5), channel_id=1, source_target_pairs={{0,24},{1,25},{2,26},{3,27},{4,28},{5,29},{6,30},{7,31},{8,0},{9,1... | collective-permute-start | bytes 491528 | tf_op jit(solution)/shard_map/ppermute | solution.py:56
  63.3 1.9 %collective-permute-start.20 = (bf16[2,4,80,128]{3,2,0,1:T(8,128)(2,1)S(1)}, bf16[2,4,80,128]{3,2,0,1:T(8,128)(2,1)S(1)}, u32[]{:S(2)}, u32[]{:S(2)}) collective-permute-start(bf16[2,4,80,128]{3,2,0,1:T(8,128)(2,1)S(1)} %pad_maximum_fusion.6), channel_id=1, source_target_pairs={{0,16},{1,17},{2,18},{3,19},{4,20},{5,21},{6,22},{7,23},{8,24},{9,... | collective-permute-start | bytes 491528 | tf_op jit(solution)/shard_map/ppermute | solution.py:56
  65.4 2.0 %collective-permute-done.7 = bf16[2816,128]{1,0:T(8,128)(2,1)S(1)} collective-permute-done((bf16[2816,128]{1,0:T(8,128)(2,1)S(1)}, bf16[2816,128]{1,0:T(8,128)(2,1)S(1)}, u32[]{:S(2)}, u32[]{:S(2)}) %collective-permute-start.7) | collective-permute-done | bytes 720928 | tf_op jit(solution)/shard_map/ppermute | solution.py:56
  67.7 3.3 %collective-permute-start.8 = (bf16[2,4,176,128]{3,2,0,1:T(8,128)(2,1)S(1)}, bf16[2,4,176,128]{3,2,0,1:T(8,128)(2,1)S(1)}, u32[]{:S(2)}, u32[]{:S(2)}) collective-permute-start(bf16[2,4,176,128]{3,2,0,1:T(8,128)(2,1)S(1)} %pad_maximum_fusion), channel_id=1, source_target_pairs={{0,64},{1,65},{2,66},{3,67},{4,68},{5,69},{6,70},{7,71},{8,72},{9,... | collective-permute-start | bytes 1081352 | tf_op jit(solution)/shard_map/ppermute | solution.py:56
  72.5 2.3 %collective-permute-start.10 = (bf16[2,4,176,128]{3,2,0,1:T(8,128)(2,1)S(1)}, bf16[2,4,176,128]{3,2,0,1:T(8,128)(2,1)S(1)}, u32[]{:S(2)}, u32[]{:S(2)}) collective-permute-start(bf16[2,4,176,128]{3,2,0,1:T(8,128)(2,1)S(1)} %pad_maximum_fusion.2), channel_id=1, source_target_pairs={{0,4},{1,5},{2,6},{3,7},{4,0},{5,1},{6,2},{7,3},{8,12},{9,13},{10,... | collective-permute-start | bytes 1081352 | tf_op jit(solution)/shard_map/ppermute | solution.py:56
  75.8 2.8 %collective-permute-start.23 = (bf16[2,80,128]{2,1,0:T(8,128)(2,1)S(1)}, bf16[2,80,128]{2,1,0:T(8,128)(2,1)S(1)}, u32[]{:S(2)}, u32[]{:S(2)}) collective-permute-start(bf16[2,80,128]{2,1,0:T(8,128)(2,1)S(1)} %get-tuple-element.54), channel_id=1, source_target_pairs={{0,4},{1,5},{2,6},{3,7},{4,0},{5,1},{6,2},{7,3},{8,12},{9,13},{10,... | collective-permute-start | bytes 122888 | tf_op jit(solution)/shard_map/ppermute | solution.py:56
  78.6 1.6 %collective-permute-start.22 = (bf16[2,80,128]{2,1,0:T(8,128)(2,1)S(1)}, bf16[2,80,128]{2,1,0:T(8,128)(2,1)S(1)}, u32[]{:S(2)}, u32[]{:S(2)}) collective-permute-start(bf16[2,80,128]{2,1,0:T(8,128)(2,1)S(1)} %get-tuple-element.55), channel_id=1, source_target_pairs={{0,68},{1,69},{2,70},{3,71},{4,64},{5,65},{6,66},{7,67},{8,76},{9,... | collective-permute-start | bytes 122888 | tf_op jit(solution)/shard_map/ppermute | solution.py:56
  80.2 3.4 %collective-permute-done.10 = bf16[2,4,176,128]{3,2,0,1:T(8,128)(2,1)S(1)} collective-permute-done((bf16[2,4,176,128]{3,2,0,1:T(8,128)(2,1)S(1)}, bf16[2,4,176,128]{3,2,0,1:T(8,128)(2,1)S(1)}, u32[]{:S(2)}, u32[]{:S(2)}) %collective-permute-start.10) | collective-permute-done | bytes 360480 | tf_op jit(solution)/shard_map/ppermute | solution.py:56
  84.6 2.6 %collective-permute-start.13 = (bf16[2,176,128]{2,1,0:T(8,128)(2,1)S(1)}, bf16[2,176,128]{2,1,0:T(8,128)(2,1)S(1)}, u32[]{:S(2)}, u32[]{:S(2)}) collective-permute-start(bf16[2,176,128]{2,1,0:T(8,128)(2,1)S(1)} %get-tuple-element.43), channel_id=1, source_target_pairs={{0,2},{1,3},{2,0},{3,1},{4,6},{5,7},{6,4},{7,5},{8,10},{9,11},{10,... | collective-permute-start | bytes 270344 | tf_op jit(solution)/shard_map/ppermute | solution.py:56
  91.8 2.0 %collective-permute-start.24 = (bf16[512,128]{1,0:T(8,128)(2,1)S(1)}, bf16[512,128]{1,0:T(8,128)(2,1)S(1)}, u32[]{:S(2)}, u32[]{:S(2)}) collective-permute-start(bf16[512,128]{1,0:T(8,128)(2,1)S(1)} %get-tuple-element.57), channel_id=1, source_target_pairs={{0,64},{1,65},{2,66},{3,67},{4,68},{5,69},{6,70},{7,71},{8,72},{9,... | collective-permute-start | bytes 393224 | tf_op jit(solution)/shard_map/ppermute | solution.py:56
  93.8 3.0 %collective-permute-done.24 = bf16[512,128]{1,0:T(8,128)(2,1)S(1)} collective-permute-done((bf16[512,128]{1,0:T(8,128)(2,1)S(1)}, bf16[512,128]{1,0:T(8,128)(2,1)S(1)}, u32[]{:S(2)}, u32[]{:S(2)}) %collective-permute-start.24) | collective-permute-done | bytes 131104 | tf_op jit(solution)/shard_map/ppermute | solution.py:56
  97.0 1.5 %collective-permute-done.25.other = bf16[2,512,128]{2,1,0:T(8,128)(2,1)S(1)} collective-permute-done((bf16[2,512,128]{2,1,0:T(8,128)(2,1)S(1)}, bf16[2,512,128]{2,1,0:T(8,128)(2,1)S(1)}, u32[]{:S(2)}, u32[]{:S(2)}) %collective-permute-start.25) | collective-permute-done | bytes 262176 | tf_op jit(solution)/shard_map/ppermute | solution.py:56
  100.6 7.0 %all-to-all-start = ((bf16[32,4,2,512]{3,2,1,0:T(2,128)(2,1)}), bf16[32,4,2,512]{3,2,1,0:T(2,128)(2,1)}, u32[]{:S(2)}, u32[]{:S(2)}) async-start(bf16[32,4,2,512]{3,2,1,0:T(2,128)(2,1)} %bitcast.77), calls=%async_computation | async-start | bytes 524288 | tf_op jit(solution)/shard_map/all_to_all | solution.py:332
  108.5 2.1 %shard_map.94 = (f32[512,512]{1,0:T(8,128)}, f32[512,512]{1,0:T(8,128)}, f32[512,512]{1,0:T(8,128)}) custom-call(bf16[2,512,128]{2,1,0:T(8,128)(2,1)S(1)} %pad_maximum_fusion.3.own, bf16[2,512,128]{2,1,0:T(8,128)(2,1)S(1)} %copy-done.4, f32[512,512]{1,0:T(8,128)S(1)} %copy-done, f32[512,512]{1,0:T(8,128)S(1)} %copy-done.1, f32[512,512]{1,0:T(8,128)S(1)} %copy-done.2), custom_call_target="tpu_custom_call" | custom-call | flops 5242880 | bytes 6815744 | tf_op jit(solution)/shard_map/pallas_call | solution.py:245
  110.6 8.0 %all-to-all-done = bf16[32,4,2,512]{3,2,1,0:T(2,128)(2,1)} async-done(((bf16[32,4,2,512]{3,2,1,0:T(2,128)(2,1)}), bf16[32,4,2,512]{3,2,1,0:T(2,128)(2,1)}, u32[]{:S(2)}, u32[]{:S(2)}) %all-to-all-start) | async-done | bytes 262176 | tf_op jit(solution)/shard_map/all_to_all | solution.py:332
  118.5 1.8 %copy.59 = bf16[128,2,512]{2,1,0:T(2,128)(2,1)} copy(bf16[128,2,512]{2,1,0:T(2,128)(2,1)} %bitcast.45) | data formatting | bytes 524288
  (84 shorter events, 17.2 us)
Async XLA Ops:
  16.3 6.6 %collective-permute-start = (bf16[8192,128]{1,0:T(8,128)(2,1)}, bf16[8192,128]{1,0:T(8,128)(2,1)}, u32[]{:S(2)}, u32[]{:S(2)}) collective-permute-start(bf16[8192,128]{1,0:T(8,128)(2,1)} %get-tuple-element.21), channel_id=1, source_target_pairs={{0,32},{1,33},{2,34},{3,35},{4,36},{5,37},{6,38},{7,39},{8,40},{9,... | collective-permute-start | bytes 6291464 | tf_op jit(solution)/shard_map/ppermute | solution.py:56
  16.4 13.4 %collective-permute-start.4 = (bf16[8192,128]{1,0:T(8,128)(2,1)}, bf16[8192,128]{1,0:T(8,128)(2,1)S(1)}, u32[]{:S(2)}, u32[]{:S(2)}) collective-permute-start(bf16[8192,128]{1,0:T(8,128)(2,1)} %get-tuple-element.27), channel_id=1, source_target_pairs={{0,32},{1,33},{2,34},{3,35},{4,36},{5,37},{6,38},{7,39},{8,40},{9,... | collective-permute-start | bytes 6291464 | tf_op jit(solution)/shard_map/ppermute | solution.py:56
  24.4 17.1 %collective-permute-start.14 = (bf16[2560,128]{1,0:T(8,128)(2,1)S(1)}, bf16[2560,128]{1,0:T(8,128)(2,1)S(1)}, u32[]{:S(2)}, u32[]{:S(2)}) collective-permute-start(bf16[2560,128]{1,0:T(8,128)(2,1)S(1)} %add_convert_fusion.7), channel_id=1, source_target_pairs={{0,1},{1,0},{2,3},{3,2},{4,5},{5,4},{6,7},{7,6},{8,9},{9,8},{10,11... | collective-permute-start | bytes 1966088 | tf_op jit(solution)/shard_map/ppermute | solution.py:56
  28.2 19.1 %collective-permute-start.2 = (bf16[5632,128]{1,0:T(8,128)(2,1)S(1)}, bf16[5632,128]{1,0:T(8,128)(2,1)S(1)}, u32[]{:S(2)}, u32[]{:S(2)}) collective-permute-start(bf16[5632,128]{1,0:T(8,128)(2,1)S(1)} %add_convert_fusion.3), channel_id=1, source_target_pairs={{0,8},{1,9},{2,10},{3,11},{4,12},{5,13},{6,14},{7,15},{8,0},{9,1},... | collective-permute-start | bytes 4325384 | tf_op jit(solution)/shard_map/ppermute | solution.py:56
  29.8 11.7 %collective-permute-start.1 = (bf16[8192,128]{1,0:T(8,128)(2,1)S(1)}, bf16[8192,128]{1,0:T(8,128)(2,1)S(1)}, u32[]{:S(2)}, u32[]{:S(2)}) collective-permute-start(bf16[8192,128]{1,0:T(8,128)(2,1)S(1)} %copy-done.11), channel_id=1, source_target_pairs={{0,32},{1,33},{2,34},{3,35},{4,36},{5,37},{6,38},{7,39},{8,40},{9,... | collective-permute-start | bytes 6291464 | tf_op jit(solution)/shard_map/ppermute | solution.py:56
  29.9 11.6 %copy-start.10 = (bf16[8192,128]{1,0:T(8,128)(2,1)S(1)}, bf16[8192,128]{1,0:T(8,128)(2,1)}, u32[]{:S(2)}) copy-start(bf16[8192,128]{1,0:T(8,128)(2,1)} %get-tuple-element.28) | copy-start | bytes 6291460
  29.9 11.7 %copy-start.7 = (bf16[8192,128]{1,0:T(8,128)(2,1)S(1)}, bf16[8192,128]{1,0:T(8,128)(2,1)}, u32[]{:S(2)}) copy-start(bf16[8192,128]{1,0:T(8,128)(2,1)} %get-tuple-element.19) | copy-start | bytes 6291460
  30.4 20.4 %collective-permute-start.16 = (bf16[2560,128]{1,0:T(8,128)(2,1)S(1)}, bf16[2560,128]{1,0:T(8,128)(2,1)S(1)}, u32[]{:S(2)}, u32[]{:S(2)}) collective-permute-start(bf16[2560,128]{1,0:T(8,128)(2,1)S(1)} %add_convert_fusion.5), channel_id=1, source_target_pairs={{0,3},{1,2},{2,1},{3,0},{4,7},{5,6},{6,5},{7,4},{8,11},{9,10},{10,... | collective-permute-start | bytes 1966088 | tf_op jit(solution)/shard_map/ppermute | solution.py:56
  33.3 20.2 %collective-permute-start.6 = (bf16[5632,128]{1,0:T(8,128)(2,1)S(1)}, bf16[5632,128]{1,0:T(8,128)(2,1)S(1)}, u32[]{:S(2)}, u32[]{:S(2)}) collective-permute-start(bf16[5632,128]{1,0:T(8,128)(2,1)S(1)} %add_convert_fusion.1), channel_id=1, source_target_pairs={{0,24},{1,25},{2,26},{3,27},{4,28},{5,29},{6,30},{7,31},{8,16},{9,... | collective-permute-start | bytes 4325384 | tf_op jit(solution)/shard_map/ppermute | solution.py:56
  41.5 9.3 %collective-permute-start.5 = (bf16[8192,128]{1,0:T(8,128)(2,1)S(1)}, bf16[8192,128]{1,0:T(8,128)(2,1)S(1)}, u32[]{:S(2)}, u32[]{:S(2)}) collective-permute-start(bf16[8192,128]{1,0:T(8,128)(2,1)S(1)} %copy-done.10), channel_id=1, source_target_pairs={{0,32},{1,33},{2,34},{3,35},{4,36},{5,37},{6,38},{7,39},{8,40},{9,... | collective-permute-start | bytes 6291464 | tf_op jit(solution)/shard_map/ppermute | solution.py:56
  41.8 14.0 %collective-permute-start.15 = (bf16[1280,128]{1,0:T(8,128)(2,1)S(1)}, bf16[1280,128]{1,0:T(8,128)(2,1)S(1)}, u32[]{:S(2)}, u32[]{:S(2)}) collective-permute-start(bf16[1280,128]{1,0:T(8,128)(2,1)S(1)} %slice.428), channel_id=1, source_target_pairs={{0,3},{1,2},{2,1},{3,0},{4,7},{5,6},{6,5},{7,4},{8,11},{9,10},{10,... | collective-permute-start | bytes 983048 | tf_op jit(solution)/shard_map/ppermute | solution.py:56
  47.9 17.3 %collective-permute-start.3 = (bf16[2816,128]{1,0:T(8,128)(2,1)S(1)}, bf16[2816,128]{1,0:T(8,128)(2,1)S(1)}, u32[]{:S(2)}, u32[]{:S(2)}) collective-permute-start(bf16[2816,128]{1,0:T(8,128)(2,1)S(1)} %slice.390), channel_id=1, source_target_pairs={{0,24},{1,25},{2,26},{3,27},{4,28},{5,29},{6,30},{7,31},{8,16},{9,... | collective-permute-start | bytes 2162696 | tf_op jit(solution)/shard_map/ppermute | solution.py:56
  51.2 8.6 %collective-permute-start.17 = (bf16[1280,128]{1,0:T(8,128)(2,1)S(1)}, bf16[1280,128]{1,0:T(8,128)(2,1)S(1)}, u32[]{:S(2)}, u32[]{:S(2)}) collective-permute-start(bf16[1280,128]{1,0:T(8,128)(2,1)S(1)} %slice.432), channel_id=1, source_target_pairs={{0,1},{1,0},{2,3},{3,2},{4,5},{5,4},{6,7},{7,6},{8,9},{9,8},{10,11... | collective-permute-start | bytes 983048 | tf_op jit(solution)/shard_map/ppermute | solution.py:56
  54.1 13.3 %collective-permute-start.7 = (bf16[2816,128]{1,0:T(8,128)(2,1)S(1)}, bf16[2816,128]{1,0:T(8,128)(2,1)S(1)}, u32[]{:S(2)}, u32[]{:S(2)}) collective-permute-start(bf16[2816,128]{1,0:T(8,128)(2,1)S(1)} %slice.394), channel_id=1, source_target_pairs={{0,8},{1,9},{2,10},{3,11},{4,12},{5,13},{6,14},{7,15},{8,0},{9,1},... | collective-permute-start | bytes 2162696 | tf_op jit(solution)/shard_map/ppermute | solution.py:56
  59.9 12.6 %collective-permute-start.18 = (bf16[2,4,80,128]{3,2,0,1:T(8,128)(2,1)S(1)}, bf16[2,4,80,128]{3,2,0,1:T(8,128)(2,1)S(1)}, u32[]{:S(2)}, u32[]{:S(2)}) collective-permute-start(bf16[2,4,80,128]{3,2,0,1:T(8,128)(2,1)S(1)} %pad_maximum_fusion.4), channel_id=1, source_target_pairs={{0,8},{1,9},{2,10},{3,11},{4,12},{5,13},{6,14},{7,15},{8,16},{9,17... | collective-permute-start | bytes 491528 | tf_op jit(solution)/shard_map/ppermute | solution.py:56
  61.5 13.3 %collective-permute-start.19 = (bf16[2,4,80,128]{3,2,0,1:T(8,128)(2,1)S(1)}, bf16[2,4,80,128]{3,2,0,1:T(8,128)(2,1)S(1)}, u32[]{:S(2)}, u32[]{:S(2)}) collective-permute-start(bf16[2,4,80,128]{3,2,0,1:T(8,128)(2,1)S(1)} %pad_maximum_fusion.5), channel_id=1, source_target_pairs={{0,24},{1,25},{2,26},{3,27},{4,28},{5,29},{6,30},{7,31},{8,0},{9,1... | collective-permute-start | bytes 491528 | tf_op jit(solution)/shard_map/ppermute | solution.py:56
  63.3 11.5 %collective-permute-start.20 = (bf16[2,4,80,128]{3,2,0,1:T(8,128)(2,1)S(1)}, bf16[2,4,80,128]{3,2,0,1:T(8,128)(2,1)S(1)}, u32[]{:S(2)}, u32[]{:S(2)}) collective-permute-start(bf16[2,4,80,128]{3,2,0,1:T(8,128)(2,1)S(1)} %pad_maximum_fusion.6), channel_id=1, source_target_pairs={{0,16},{1,17},{2,18},{3,19},{4,20},{5,21},{6,22},{7,23},{8,24},{9,... | collective-permute-start | bytes 491528 | tf_op jit(solution)/shard_map/ppermute | solution.py:56
  67.7 11.0 %collective-permute-start.8 = (bf16[2,4,176,128]{3,2,0,1:T(8,128)(2,1)S(1)}, bf16[2,4,176,128]{3,2,0,1:T(8,128)(2,1)S(1)}, u32[]{:S(2)}, u32[]{:S(2)}) collective-permute-start(bf16[2,4,176,128]{3,2,0,1:T(8,128)(2,1)S(1)} %pad_maximum_fusion), channel_id=1, source_target_pairs={{0,64},{1,65},{2,66},{3,67},{4,68},{5,69},{6,70},{7,71},{8,72},{9,... | collective-permute-start | bytes 1081352 | tf_op jit(solution)/shard_map/ppermute | solution.py:56
  71.0 9.2 %collective-permute-start.9 = (bf16[2,4,176,128]{3,2,0,1:T(8,128)(2,1)S(1)}, bf16[2,4,176,128]{3,2,0,1:T(8,128)(2,1)S(1)}, u32[]{:S(2)}, u32[]{:S(2)}) collective-permute-start(bf16[2,4,176,128]{3,2,0,1:T(8,128)(2,1)S(1)} %pad_maximum_fusion.1), channel_id=1, source_target_pairs={{0,68},{1,69},{2,70},{3,71},{4,64},{5,65},{6,66},{7,67},{8,76},{9,... | collective-permute-start | bytes 1081352 | tf_op jit(solution)/shard_map/ppermute | solution.py:56
  72.5 11.1 %collective-permute-start.10 = (bf16[2,4,176,128]{3,2,0,1:T(8,128)(2,1)S(1)}, bf16[2,4,176,128]{3,2,0,1:T(8,128)(2,1)S(1)}, u32[]{:S(2)}, u32[]{:S(2)}) collective-permute-start(bf16[2,4,176,128]{3,2,0,1:T(8,128)(2,1)S(1)} %pad_maximum_fusion.2), channel_id=1, source_target_pairs={{0,4},{1,5},{2,6},{3,7},{4,0},{5,1},{6,2},{7,3},{8,12},{9,13},{10,... | collective-permute-start | bytes 1081352 | tf_op jit(solution)/shard_map/ppermute | solution.py:56
  74.8 23.7 %copy-start = (f32[512,512]{1,0:T(8,128)S(1)}, f32[512,512]{1,0:T(8,128)}, u32[]{:S(2)}) copy-start(f32[512,512]{1,0:T(8,128)} %master.3) | copy-start | bytes 3145732
  74.8 23.7 %copy-start.1 = (f32[512,512]{1,0:T(8,128)S(1)}, f32[512,512]{1,0:T(8,128)}, u32[]{:S(2)}) copy-start(f32[512,512]{1,0:T(8,128)} %moment1.3) | copy-start | bytes 3145732
  74.8 23.7 %copy-start.2 = (f32[512,512]{1,0:T(8,128)S(1)}, f32[512,512]{1,0:T(8,128)}, u32[]{:S(2)}) copy-start(f32[512,512]{1,0:T(8,128)} %moment2.3) | copy-start | bytes 3145732
  74.9 12.2 %collective-permute-start.21 = (bf16[2,80,128]{2,1,0:T(8,128)(2,1)S(1)}, bf16[2,80,128]{2,1,0:T(8,128)(2,1)S(1)}, u32[]{:S(2)}, u32[]{:S(2)}) collective-permute-start(bf16[2,80,128]{2,1,0:T(8,128)(2,1)S(1)} %get-tuple-element.53), channel_id=1, source_target_pairs={{0,64},{1,65},{2,66},{3,67},{4,68},{5,69},{6,70},{7,71},{8,72},{9,... | collective-permute-start | bytes 122888 | tf_op jit(solution)/shard_map/ppermute | solution.py:56
  75.8 12.6 %collective-permute-start.23 = (bf16[2,80,128]{2,1,0:T(8,128)(2,1)S(1)}, bf16[2,80,128]{2,1,0:T(8,128)(2,1)S(1)}, u32[]{:S(2)}, u32[]{:S(2)}) collective-permute-start(bf16[2,80,128]{2,1,0:T(8,128)(2,1)S(1)} %get-tuple-element.54), channel_id=1, source_target_pairs={{0,4},{1,5},{2,6},{3,7},{4,0},{5,1},{6,2},{7,3},{8,12},{9,13},{10,... | collective-permute-start | bytes 122888 | tf_op jit(solution)/shard_map/ppermute | solution.py:56
  78.6 9.7 %collective-permute-start.22 = (bf16[2,80,128]{2,1,0:T(8,128)(2,1)S(1)}, bf16[2,80,128]{2,1,0:T(8,128)(2,1)S(1)}, u32[]{:S(2)}, u32[]{:S(2)}) collective-permute-start(bf16[2,80,128]{2,1,0:T(8,128)(2,1)S(1)} %get-tuple-element.55), channel_id=1, source_target_pairs={{0,68},{1,69},{2,70},{3,71},{4,64},{5,65},{6,66},{7,67},{8,76},{9,... | collective-permute-start | bytes 122888 | tf_op jit(solution)/shard_map/ppermute | solution.py:56
  83.8 5.8 %collective-permute-start.11 = (bf16[2,176,128]{2,1,0:T(8,128)(2,1)S(1)}, bf16[2,176,128]{2,1,0:T(8,128)(2,1)S(1)}, u32[]{:S(2)}, u32[]{:S(2)}) collective-permute-start(bf16[2,176,128]{2,1,0:T(8,128)(2,1)S(1)} %get-tuple-element.42), channel_id=1, source_target_pairs={{0,1},{1,2},{2,3},{3,0},{4,5},{5,6},{6,7},{7,4},{8,9},{9,10},{10,1... | collective-permute-start | bytes 270344 | tf_op jit(solution)/shard_map/ppermute | solution.py:56
  84.6 6.0 %collective-permute-start.13 = (bf16[2,176,128]{2,1,0:T(8,128)(2,1)S(1)}, bf16[2,176,128]{2,1,0:T(8,128)(2,1)S(1)}, u32[]{:S(2)}, u32[]{:S(2)}) collective-permute-start(bf16[2,176,128]{2,1,0:T(8,128)(2,1)S(1)} %get-tuple-element.43), channel_id=1, source_target_pairs={{0,2},{1,3},{2,0},{3,1},{4,6},{5,7},{6,4},{7,5},{8,10},{9,11},{10,... | collective-permute-start | bytes 270344 | tf_op jit(solution)/shard_map/ppermute | solution.py:56
  87.1 4.5 %collective-permute-start.12 = (bf16[2,176,128]{2,1,0:T(8,128)(2,1)S(1)}, bf16[2,176,128]{2,1,0:T(8,128)(2,1)S(1)}, u32[]{:S(2)}, u32[]{:S(2)}) collective-permute-start(bf16[2,176,128]{2,1,0:T(8,128)(2,1)S(1)} %get-tuple-element.44), channel_id=1, source_target_pairs={{0,3},{1,0},{2,1},{3,2},{4,7},{5,4},{6,5},{7,6},{8,11},{9,8},{10,9... | collective-permute-start | bytes 270344 | tf_op jit(solution)/shard_map/ppermute | solution.py:56
  91.8 5.0 %collective-permute-start.24 = (bf16[512,128]{1,0:T(8,128)(2,1)S(1)}, bf16[512,128]{1,0:T(8,128)(2,1)S(1)}, u32[]{:S(2)}, u32[]{:S(2)}) collective-permute-start(bf16[512,128]{1,0:T(8,128)(2,1)S(1)} %get-tuple-element.57), channel_id=1, source_target_pairs={{0,64},{1,65},{2,66},{3,67},{4,68},{5,69},{6,70},{7,71},{8,72},{9,... | collective-permute-start | bytes 393224 | tf_op jit(solution)/shard_map/ppermute | solution.py:56
  96.9 1.6 %collective-permute-start.25 = (bf16[2,512,128]{2,1,0:T(8,128)(2,1)S(1)}, bf16[2,512,128]{2,1,0:T(8,128)(2,1)S(1)}, u32[]{:S(2)}, u32[]{:S(2)}) collective-permute-start(bf16[2,512,128]{2,1,0:T(8,128)(2,1)S(1)} %pad_maximum_fusion.3.own), channel_id=1, source_target_pairs={{0,32},{1,33},{2,34},{3,35},{4,36},{5,37},{6,38},{7,39},{8,40},{9,... | collective-permute-start | bytes 786440 | tf_op jit(solution)/shard_map/ppermute | solution.py:56
  100.6 18.0 %all-to-all-start = ((bf16[32,4,2,512]{3,2,1,0:T(2,128)(2,1)}), bf16[32,4,2,512]{3,2,1,0:T(2,128)(2,1)}, u32[]{:S(2)}, u32[]{:S(2)}) async-start(bf16[32,4,2,512]{3,2,1,0:T(2,128)(2,1)} %bitcast.77), calls=%async_computation | async-start | bytes 524288 | tf_op jit(solution)/shard_map/all_to_all | solution.py:332
  (7 other events, 30.5 us)

commit v3 on v0

v3 whole, which is shorter than its diff:
```python
import functools

import jax
import jax.numpy as jnp
from jax import lax
from jax.experimental import pallas as pl
from jax.experimental.pallas import tpu as pltpu
from jax.sharding import PartitionSpec as P

BLOCK_ROWS = 2
AXES = ("rep", "fsdp")
SIDE = 4

bias_first = 1.0 - 0.9**10
bias_second = 1.0 - 0.95**10

ORDERS = ((0, 1, 2), (1, 2, 0))


def coords(index):
    rep, fsdp = divmod(index, 32)
    y_lo, core = divmod(rep, 2)
    x, rest = divmod(fsdp, 8)
    y_hi, z = divmod(rest, 4)
    return x, y_hi * 2 + y_lo, z, core


def index_of(x, y, z, core):
    return ((y % 2) * 2 + core) * 32 + x * 8 + (y // 2) * 4 + z


def ring_pairs(stage, distance):
    pairs = []
    for device in range(128):
        place = list(coords(device))
        axis = ORDERS[place[3]][stage]
        place[axis] = (place[axis] + distance) % SIDE
        pairs.append((device, index_of(*place)))
    return pairs


def swap_pairs(odd):
    pairs = []
    for device in range(128):
        place = list(coords(device))
        axis = ORDERS[place[3]][0]
        place[axis] = (((place[axis] + odd) ^ 1) - odd) % SIDE
        pairs.append((device, index_of(*place)))
    return pairs


def rep_pairs(bit):
    return [(device, (((device // 32) ^ bit) * 32) + device % 32) for device in range(128)]


def send(value, pairs):
    return lax.ppermute(value, AXES, pairs)


def split_body(groups, cot, tokens, *refs):
    outs, (cot_t, held, kept, in_sem, cot_sem, sem) = refs[:-6], refs[-6:]
    columns = cot.shape[1]
    count = SIDE * SIDE
    rep, fsdp = lax.axis_index("rep"), lax.axis_index("fsdp")
    core, y_lo = lax.rem(rep, 2), rep // 2
    place = (fsdp // 8, lax.rem(fsdp // 4, 2) * 2 + y_lo, lax.rem(fsdp, 4))

    def fetch(at):
        side, half, is_sent = groups[at]
        target = core if side == 0 else 1 - core
        is_first = target == 0
        parity = lax.rem(jnp.where(is_first, place[0], place[1]), 2)
        even, odd = 1 + 2 * parity, 3 - 2 * parity
        distances = (odd if half else even, 2) if is_sent else (0, even if half else odd)
        tile = 0
        for one in distances:
            for two in (half, half + 2):
                for three in range(SIDE):
                    x = lax.rem(place[0] + jnp.where(is_first, one, three), SIDE)
                    y = lax.rem(place[1] + jnp.where(is_first, two, one), SIDE)
                    z = lax.rem(place[2] + jnp.where(is_first, three, two), SIDE)
                    lane = (x * 8 + (y // 2) * 4 + z) * 512 + lax.rem(y, 2) * 256 + target * 128
                    pltpu.make_async_copy(
                        tokens.at[:, pl.ds(pl.multiple_of(lane, 128), 128)],
                        held.at[at, :, pl.ds(tile * 128, 128)],
                        in_sem.at[at],
                    ).start()
                    tile += 1

    cot_copy = pltpu.make_async_copy(cot, cot_t.at[1], cot_sem)
    cot_copy.start()
    fetch(0)
    fetch(1)
    cot_copy.wait()
    cot_t[0] = cot_t[1].T
    copies = []
    done = 0
    for at in range(len(groups)):
        pltpu.make_async_copy(held.at[at], held.at[at], in_sem.at[at]).wait()
        if at + 2 < len(groups):
            fetch(at + 2)
        total = jnp.dot(cot_t[0], held[at], preferred_element_type=jnp.float32)
        parts = 1 if groups[at][2] else 2
        per_part = count // parts
        rows = per_part * columns
        for tile in range(count):
            piece = total[:, tile * 128 : (tile + 1) * 128].astype(jnp.bfloat16)
            part, index = divmod(tile, per_part)
            if groups[at][0] == 0:
                outs[done + part][index * columns : (index + 1) * columns] = piece
            else:
                kept[at, tile * columns : (tile + 1) * columns] = piece
        for part in range(parts):
            if groups[at][0] == 1:
                copy = pltpu.make_async_copy(
                    kept.at[at, pl.ds(part * rows, rows)], outs[done], sem.at[done]
                )
                copy.start()
                copies.append(copy)
            done += 1
    for copy in copies:
        copy.wait()


def split_sums(tokens, cotangent, groups):
    depth = tokens.shape[0]
    columns = cotangent.shape[1]
    rows = SIDE * SIDE * columns
    outs, specs = [], []
    for side, _, is_sent in groups:
        sizes = [rows] if is_sent else [rows // 2] * 2
        for size in sizes:
            place = pltpu.HBM if side else pltpu.VMEM
            outs.append(place((size, 128), jnp.bfloat16))
            specs.append(pl.BlockSpec(memory_space=pl.ANY if side else pltpu.VMEM))
    leaving = max(1, sum(side for side, _, _ in groups))
    return pl.pallas_call(
        functools.partial(split_body, groups),
        out_shape=outs,
        in_specs=[pl.BlockSpec(memory_space=pl.ANY)] * 2,
        out_specs=specs,
        scratch_shapes=[
            pltpu.VMEM((2, columns, depth), jnp.bfloat16),
            pltpu.VMEM((len(groups), depth, SIDE * SIDE * 128), jnp.bfloat16),
            pltpu.VMEM((leaving, rows, 128), jnp.bfloat16),
            pltpu.SemaphoreType.DMA((len(groups),)),
            pltpu.SemaphoreType.DMA,
            pltpu.SemaphoreType.DMA((len(outs),)),
        ],
        compiler_params=pltpu.CompilerParams(vmem_limit_bytes=32 * 1024 * 1024),
        cost_estimate=pl.CostEstimate(
            flops=2 * depth * rows * 128 * len(groups),
            bytes_accessed=512 * rows * len(groups),
            transcendentals=0,
        ),
    )(
        pltpu.with_memory_space_constraint(cotangent, pltpu.HBM),
        pltpu.with_memory_space_constraint(tokens, pltpu.HBM),
    )


def updated(grad, master, moment1, moment2):
    first = 0.9 * moment1 + 0.1 * grad
    second = 0.95 * moment2 + 0.05 * grad * grad
    update = first / bias_first / (jnp.sqrt(second / bias_second) + 1e-08)
    return master - 0.05 * (update + 0.1 * master), first, second


def rep_grad(own, other, at):
    rep = lax.axis_index("rep")
    core, y_lo = lax.rem(rep, 2), rep // 2
    index = y_lo if at // 2 == 0 else 1 - y_lo
    piece = jnp.where(core == at % 2, own[index], other[index])
    return piece.T.astype(jnp.float32)


def weight_body(own, other, master, moment1, moment2, selector, outgoing, weight):
    for at in range(4):
        rows = slice(at * 128, (at + 1) * 128)
        new, _, _ = updated(rep_grad(own, other, at), master[rows], moment1[rows], moment2[rows])
        weight[rows] = new.astype(jnp.bfloat16)
    outgoing[...] = jnp.dot(
        selector[...], weight[...], preferred_element_type=jnp.float32
    ).astype(jnp.bfloat16)


def unpack_body(rows, blocks):
    blocks[...] = rows[...].reshape(blocks.shape)


def unpacked(rows, block_rows):
    vmem = pl.BlockSpec(memory_space=pltpu.VMEM)
    shape = (rows.shape[0] // block_rows, block_rows, rows.shape[1])
    return pl.pallas_call(
        unpack_body,
        out_shape=jax.ShapeDtypeStruct(shape, rows.dtype),
        in_specs=[vmem],
        out_specs=vmem,
    )(rows)


def adam_body(own, other, master, moment1, moment2, *refs):
    outs, kept, sem = refs[:3], refs[3:6], refs[6]
    copies = []
    for at in range(4):
        rows = slice(at * 128, (at + 1) * 128)
        values = updated(rep_grad(own, other, at), master[rows], moment1[rows], moment2[rows])
        for k in range(3):
            kept[k][rows] = values[k]
            copy = pltpu.make_async_copy(
                kept[k].at[pl.ds(at * 128, 128)], outs[k].at[pl.ds(at * 128, 128)], sem.at[k, at]
            )
            copy.start()
            copies.append(copy)
    for copy in copies:
        copy.wait()


def adam(own, other, master, moment1, moment2, selector):
    rows, columns = master.shape
    size = rows * columns
    params = pltpu.CompilerParams(vmem_limit_bytes=12 * 1024 * 1024)
    vmem = pl.BlockSpec(memory_space=pltpu.VMEM)
    outgoing = pl.pallas_call(
        weight_body,
        out_shape=jax.ShapeDtypeStruct((selector.shape[0], columns), jnp.bfloat16),
        in_specs=[vmem] * 6,
        out_specs=vmem,
        scratch_shapes=[pltpu.VMEM((rows, columns), jnp.bfloat16)],
        compiler_params=params,
        cost_estimate=pl.CostEstimate(
            flops=20 * size, bytes_accessed=14 * size, transcendentals=0
        ),
    )(own, other, master, moment1, moment2, selector)
    state = pl.pallas_call(
        adam_body,
        out_shape=[jax.ShapeDtypeStruct((rows, columns), jnp.float32)] * 3,
        in_specs=[vmem] * 5,
        out_specs=[pl.BlockSpec(memory_space=pl.ANY)] * 3,
        scratch_shapes=[pltpu.VMEM((rows, columns), jnp.float32)] * 3
        + [pltpu.SemaphoreType.DMA((3, 4))],
        compiler_params=params,
        cost_estimate=pl.CostEstimate(
            flops=20 * size, bytes_accessed=26 * size, transcendentals=0
        ),
    )(own, other, master, moment1, moment2)
    return outgoing, state


def after(value, *earlier):
    return lax.optimization_barrier((value, *earlier))[0]


def combine_body(plan, *refs):
    outs = refs[len(refs) - len(plan) :]
    for out, segments in zip(outs, plan):
        begin = 0
        for rows, terms in segments:
            chunk = next(size for size in (768, 512, rows) if rows % size == 0)

            def one(step, carry, begin=begin, terms=terms, chunk=chunk, out=out):
                total = 0.0
                for source, start in terms:
                    at = pl.multiple_of(start + step * chunk, 16)
                    total = total + refs[source][pl.ds(at, chunk)].astype(jnp.float32)
                at = pl.multiple_of(begin + step * chunk, 16)
                out[pl.ds(at, chunk)] = total.astype(jnp.bfloat16)
                return carry

            lax.fori_loop(0, rows // chunk, one, 0)
            begin += rows


def combine(inputs, plan, flops=0):
    vmem = pl.BlockSpec(memory_space=pltpu.VMEM)
    sizes = [sum(rows for rows, _ in segments) for segments in plan]
    return pl.pallas_call(
        functools.partial(combine_body, plan),
        out_shape=[pltpu.VMEM((size, 128), jnp.bfloat16) for size in sizes],
        in_specs=[vmem] * len(inputs),
        out_specs=[vmem] * len(plan),
        compiler_params=pltpu.CompilerParams(
            vmem_limit_bytes=256 * (sum(sizes) + sum(value.shape[0] for value in inputs)) + 2**21
        ),
        cost_estimate=pl.CostEstimate(flops=flops, bytes_accessed=0, transcendentals=0),
    )(*inputs)


def total(inputs):
    rows = inputs[0].shape[0]
    return combine(inputs, [[(rows, [(k, 0) for k in range(len(inputs))])]])[0]


def summed(tokens, cotangent, early):
    columns = cotangent.shape[1]
    far = (2, 1, 3)
    other = split_sums(tokens, cotangent, [(1, 0, True), (1, 1, True)])
    own = split_sums(tokens, after(cotangent, *other), [(0, 0, True), (0, 1, True)])
    beside = [send(value, rep_pairs(1)) for value in other]
    last = []
    came = []
    for odd in range(2):
        last = [total([own[odd], after(beside[odd], *last)])]
        came.append(send(last[0], swap_pairs(odd)))

    both = split_sums(
        tokens, after(cotangent, *last), [(side, half, False) for side in (1, 0) for half in range(2)]
    )
    beside = [send(value, rep_pairs(1)) for value in both[:4]]

    rows = 8 * columns
    half_sums = combine(
        [both[5], both[7], *came],
        [[(rows, [(odd, 0), (2 + odd, rows)])] for odd in range(2)],
        flops=10**11,
    )
    sent = combine(
        [*half_sums, beside[1], beside[3]],
        [[(rows, [(odd, 0), (2 + odd, 0)])] for odd in range(2)],
    )
    got = [send(sent[odd], swap_pairs(1 - odd)) for odd in range(2)]
    near = combine(
        [both[4], both[6], after(beside[0], *sent), beside[2], *came],
        [[(rows, [(odd, 0), (2 + odd, 0), (4 + odd, 0)])] for odd in range(2)],
    )

    rows = 4 * columns
    sums = [None] * SIDE
    for odd in range(2):
        sums[odd], sums[odd + 2] = combine(
            [near[odd], after(got[odd], early)], [[(rows, [(0, at), (1, at)])] for at in (0, rows)]
        )
    parts = [sums[0]] + [send(sums[at], ring_pairs(1, at)) for at in far]
    sums = combine(
        parts, [[(columns, [(k, at * columns) for k in range(SIDE)])] for at in range(SIDE)]
    )
    return total([sums[0]] + [send(sums[at], ring_pairs(2, at)) for at in (1, 3, 2)])


def select_body(capacity, fsdp_count, owner, selector):
    blocks = owner.shape[1]
    shape = (blocks, blocks)
    mine = owner[pl.ds(lax.axis_index("fsdp"), 1), :]
    by_lane = jnp.broadcast_to(mine, shape)
    earlier = lax.broadcasted_iota(jnp.int32, shape, 0) < lax.broadcasted_iota(jnp.int32, shape, 1)
    same = jnp.where(by_lane.T == by_lane, 1.0, 0.0)
    rank = jnp.sum(jnp.where(earlier, same, 0.0), axis=0, keepdims=True)
    slot = (mine % fsdp_count * capacity).astype(jnp.float32) + rank
    slot = jnp.where(mine // fsdp_count == lax.axis_index("rep"), slot, -1.0)
    rows = blocks * BLOCK_ROWS
    block = lax.broadcasted_iota(jnp.int32, (blocks, rows), 0)
    row = lax.broadcasted_iota(jnp.int32, (blocks, rows), 1)
    spread = jnp.where(row // BLOCK_ROWS == block, 1.0, 0.0).astype(jnp.bfloat16)
    slot = jnp.dot(
        jnp.broadcast_to(slot, (16, blocks)).astype(jnp.bfloat16),
        spread,
        preferred_element_type=jnp.float32,
    )[:1]
    shape = selector.shape
    slot_row = lax.broadcasted_iota(jnp.int32, shape, 0)
    row = lax.broadcasted_iota(jnp.int32, shape, 1)
    at_slot = (slot_row // BLOCK_ROWS).astype(jnp.float32) == slot
    at_row = slot_row % BLOCK_ROWS == row % BLOCK_ROWS
    selector[...] = jnp.where(jnp.logical_and(at_slot, at_row), 1.0, 0.0).astype(jnp.bfloat16)


def select_blocks(owner, capacity, fsdp_count):
    vmem = pl.BlockSpec(memory_space=pltpu.VMEM)
    shape = (fsdp_count * capacity * BLOCK_ROWS, owner.shape[1] * BLOCK_ROWS)
    return pl.pallas_call(
        functools.partial(select_body, capacity, fsdp_count),
        out_shape=jax.ShapeDtypeStruct(shape, jnp.bfloat16),
        in_specs=[vmem],
        out_specs=vmem,
        compiler_params=pltpu.CompilerParams(vmem_limit_bytes=8 * 1024 * 1024),
        cost_estimate=pl.CostEstimate(flops=0, bytes_accessed=0, transcendentals=0),
    )(owner)


def per_device(tokens, cotangent, master, moment1, moment2, owner):
    fsdp_count = lax.axis_size("fsdp")
    rep_count = lax.axis_size("rep")
    shard_rows = master.shape[0]
    columns = master.shape[1]
    local_blocks = shard_rows // BLOCK_ROWS
    capacity = 2 * local_blocks // (rep_count * fsdp_count)
    owner, cotangent = lax.optimization_barrier(
        (owner.reshape(fsdp_count, local_blocks), cotangent)
    )
    selector = select_blocks(owner, capacity, fsdp_count)
    mine = summed(tokens, cotangent, selector)
    beside = send(mine, rep_pairs(2))
    own = jnp.stack([mine, beside])
    other = send(own, rep_pairs(1))
    outgoing, state = adam(own, other, master, moment1, moment2, selector)
    outgoing = outgoing.reshape(fsdp_count, capacity * BLOCK_ROWS, columns)
    received = lax.all_to_all(outgoing, "fsdp", split_axis=0, concat_axis=0, tiled=True)
    upload = unpacked(received.reshape(fsdp_count * capacity * BLOCK_ROWS, columns), BLOCK_ROWS)
    return (*state, upload)


def solution(mesh):
    placed = (
        P(("rep", "fsdp"), None),
        P(("rep", "fsdp"), None),
        P("fsdp", None),
        P("fsdp", None),
        P("fsdp", None),
        P(),
    )
    return jax.shard_map(
        per_device,
        mesh=mesh,
        in_specs=placed,
        out_specs=(
            P("fsdp", None),
            P("fsdp", None),
            P("fsdp", None),
            P(("rep", "fsdp"), None, None),
        ),
        check_vma=False,
    )
```

time: 324 us -> 117 us (0.36)
  waiting for transfers between devices: 264 us -> 59.7 us
  Pallas kernels: 0 us -> 29.3 us
  starting transfers between devices: 0.08 us -> 24.2 us
  blocking collectives: 20.4 us -> 0 us
  matrix products: 18.6 us -> 0 us
  between operations: 14.1 us -> 0.89 us
  other arithmetic: 4.57 us -> 0.03 us
    reduce_scatter x1 -> x0, waiting for transfers between devices: 227 us -> none  [per_device(): lax.psum_scatter(lax.dot_general(tokens, cotangent, (((0,), (0,)), ((), (...]
    ppermute x0 -> x18, waiting for transfers between devices: none -> 51.8 us  [send(): return lax.ppermute(value, AXES, pairs)]
    psum x1 -> x0, waiting for transfers between devices: 37.2 us -> none  [per_device(): grad = lax.psum(shard_grad, 'rep').astype(jnp.float32)]
    pallas_call x0 -> x16, Pallas kernels: none -> 29.3 us  [the longest x3 20 us: split_sums(): pl.pallas_call(functools.partial(split_body, groups), out_shape=outs, in_...]
    all_to_all x1 -> x0, blocking collectives: 20.4 us -> none  [per_device(): lax.all_to_all(outgoing, 'fsdp', split_axis=0, concat_axis=0, tiled=True)]
    ppermute x0 -> x18, starting transfers between devices: none -> 19 us  [send(): return lax.ppermute(value, AXES, pairs)]
    dot_general x2 -> x0, matrix products: 18.6 us -> none  [the longest x1 18.4 us: per_device(): lax.dot_general(tokens, cotangent, (((0,), (0,)), ((), ())), preferred_el...]
    all_to_all x0 -> x1, waiting for transfers between devices: none -> 7.96 us  [per_device(): lax.all_to_all(outgoing, 'fsdp', split_axis=0, concat_axis=0, tiled=True)]
  transfers between devices with their start and end apart: 2 -> 19, of which waited for: 2 -> 12; matrix products, arithmetic and copies ran while one was open for 0% -> 0% of each run, Pallas kernels for 0% -> 16%
where the time goes in v3:
time: 117 us
  waiting for transfers between devices  59.7 us (51%)
  Pallas kernels  29.3 us (25%)
  starting transfers between devices  24.2 us (21%)
  local copies, waits for them, and re-layouts  2.43 us (2%)
    ppermute x18, waiting for transfers between devices, send(): return lax.ppermute(value, AXES, pairs)  51.8 us
    pallas_call x3, Pallas kernels, split_sums(): pl.pallas_call(functools.partial(split_body, groups), out_shape=outs, in_...  20 us
    ppermute x18, starting transfers between devices, send(): return lax.ppermute(value, AXES, pairs)  19 us
    all_to_all x1, waiting for transfers between devices, per_device(): lax.all_to_all(outgoing, 'fsdp', split_axis=0, concat_axis=0, tiled=True)  7.96 us
    all_to_all x1, starting transfers between devices, per_device(): lax.all_to_all(outgoing, 'fsdp', split_axis=0, concat_axis=0, tiled=True)  5.28 us
    pallas_call x9, Pallas kernels, combine(): pl.pallas_call(functools.partial(combine_body, plan), out_shape=[pltpu.VM...  3.95 us
  transfers between devices with their start and end apart: 19, of which 12 were waited for; matrix products, arithmetic and copies ran while one was open for 0% of the time, Pallas kernels for 16%

profile of v3, /device:TPU:0, one launch (start us, length us, event | category | flops | bytes accessed | tf_op | source)
XLA Modules:
  0.0 116.6 jit_solution(14006666687899827102)
XLA Ops:
  0.6 0.8 reshape.17.owner
  1.4 6.7 %shard_map.93 = (bf16[8192,128]{1,0:T(8,128)(2,1)}, bf16[8192,128]{1,0:T(8,128)(2,1)}) custom-call(bf16[512,512]{1,0:T(8,128)(2,1)} %cot.2, bf16[512,16384]{1,0:T(8,128)(2,1)} %tokens.5), custom_call_target="tpu_custom_call" | custom-call | flops 2147483648 | bytes 8388608 | tf_op jit(solution)/shard_map/pallas_call | solution.py:137
  8.7 5.3 %shard_map.94 = (bf16[8192,128]{1,0:T(8,128)(2,1)S(1)}, bf16[8192,128]{1,0:T(8,128)(2,1)S(1)}) custom-call(bf16[512,512]{1,0:T(8,128)(2,1)} %cot.2, bf16[512,16384]{1,0:T(8,128)(2,1)} %tokens.5), custom_call_target="tpu_custom_call" | custom-call | flops 2147483648 | bytes 8388608 | tf_op jit(solution)/shard_map/pallas_call | solution.py:137
  14.6 1.0 collective-permute-done.refs_1_
  16.1 2.9 %collective-permute-start.4 = (bf16[8192,128]{1,0:T(8,128)(2,1)S(1)}, bf16[8192,128]{1,0:T(8,128)(2,1)S(1)}, u32[]{:S(2)}, u32[]{:S(2)}) collective-permute-start(bf16[8192,128]{1,0:T(8,128)(2,1)S(1)} %shard_map.96), channel_id=1, source_target_pairs={{0,24},{1,25},{2,26},{3,27},{4,28},{5,29},{6,30},{7,31},{8,16},{9,... | collective-permute-start | bytes 6291464 | tf_op jit(solution)/shard_map/ppermute | solution.py:57
  19.3 8.0 %shard_map.97 = (bf16[4096,128]{1,0:T(8,128)(2,1)}, bf16[4096,128]{1,0:T(8,128)(2,1)}, bf16[4096,128]{1,0:T(8,128)(2,1)}, bf16[4096,128]{1,0:T(8,128)(2,1)}, bf1...) custom-call(bf16[512,512]{1,0:T(8,128)(2,1)} %cot.2, ...), custom_call_target="tpu_custom_call" | custom-call | flops 4294967296 | bytes 16777216 | tf_op jit(solution)/shard_map/pallas_call | solution.py:137
  27.9 15.5 %collective-permute-done.4.refs_3_.refs_5_ = bf16[8192,128]{1,0:T(8,128)(2,1)S(1)} collective-permute-done((bf16[8192,128]{1,0:T(8,128)(2,1)S(1)}, bf16[8192,128]{1,0:T(8,128)(2,1)S(1)}, u32[]{:S(2)}, u32[]{:S(2)}) %collective-permute-start.4) | collective-permute-done | bytes 2097184 | tf_op jit(solution)/shard_map/ppermute | solution.py:57
  43.5 1.6 %collective-permute-done.3.refs_2_.refs_4_ = bf16[8192,128]{1,0:T(8,128)(2,1)S(1)} collective-permute-done((bf16[8192,128]{1,0:T(8,128)(2,1)S(1)}, bf16[8192,128]{1,0:T(8,128)(2,1)S(1)}, u32[]{:S(2)}, u32[]{:S(2)}) %collective-permute-start.3) | collective-permute-done | bytes 2097184 | tf_op jit(solution)/shard_map/ppermute | solution.py:57
  45.7 0.6 shard_map.99
  46.5 1.1 collective-permute-start.8
  48.0 0.8 shard_map.100
  48.9 12.3 %collective-permute-done.10.refs_1_ = bf16[4096,128]{1,0:T(8,128)(2,1)S(1)} collective-permute-done((bf16[4096,128]{1,0:T(8,128)(2,1)S(1)}, bf16[4096,128]{1,0:T(8,128)(2,1)S(1)}, u32[]{:S(2)}, u32[]{:S(2)}) %collective-permute-start.10) | collective-permute-done | bytes 1048608 | tf_op jit(solution)/shard_map/ppermute | solution.py:57
  61.4 1.8 %collective-permute-start.11 = (bf16[2048,128]{1,0:T(8,128)(2,1)S(1)}, bf16[2048,128]{1,0:T(8,128)(2,1)S(1)}, u32[]{:S(2)}, u32[]{:S(2)}) collective-permute-start(bf16[2048,128]{1,0:T(8,128)(2,1)S(1)} %get-tuple-element.69), channel_id=1, source_target_pairs={{0,64},{1,65},{2,66},{3,67},{4,68},{5,69},{6,70},{7,71},{8,72},{9,... | collective-permute-start | bytes 1572872 | tf_op jit(solution)/shard_map/ppermute | solution.py:57
  63.2 1.7 %collective-permute-start.12 = (bf16[2048,128]{1,0:T(8,128)(2,1)S(1)}, bf16[2048,128]{1,0:T(8,128)(2,1)S(1)}, u32[]{:S(2)}, u32[]{:S(2)}) collective-permute-start(bf16[2048,128]{1,0:T(8,128)(2,1)S(1)} %get-tuple-element.70), channel_id=1, source_target_pairs={{0,68},{1,69},{2,70},{3,71},{4,64},{5,65},{6,66},{7,67},{8,76},{9,... | collective-permute-start | bytes 1572872 | tf_op jit(solution)/shard_map/ppermute | solution.py:57
  65.2 2.1 %collective-permute-start.9 = (bf16[2048,128]{1,0:T(8,128)(2,1)S(1)}, bf16[2048,128]{1,0:T(8,128)(2,1)S(1)}, u32[]{:S(2)}, u32[]{:S(2)}) collective-permute-start(bf16[2048,128]{1,0:T(8,128)(2,1)S(1)} %get-tuple-element.66), channel_id=1, source_target_pairs={{0,4},{1,5},{2,6},{3,7},{4,0},{5,1},{6,2},{7,3},{8,12},{9,13},{10,... | collective-permute-start | bytes 1572872 | tf_op jit(solution)/shard_map/ppermute | solution.py:57
  67.3 4.8 %collective-permute-done.11.refs_2_ = bf16[2048,128]{1,0:T(8,128)(2,1)S(1)} collective-permute-done((bf16[2048,128]{1,0:T(8,128)(2,1)S(1)}, bf16[2048,128]{1,0:T(8,128)(2,1)S(1)}, u32[]{:S(2)}, u32[]{:S(2)}) %collective-permute-start.11) | collective-permute-done | bytes 524320 | tf_op jit(solution)/shard_map/ppermute | solution.py:57
  72.4 6.5 %collective-permute-done.9.refs_1_ = bf16[2048,128]{1,0:T(8,128)(2,1)S(1)} collective-permute-done((bf16[2048,128]{1,0:T(8,128)(2,1)S(1)}, bf16[2048,128]{1,0:T(8,128)(2,1)S(1)}, u32[]{:S(2)}, u32[]{:S(2)}) %collective-permute-start.9) | collective-permute-done | bytes 524320 | tf_op jit(solution)/shard_map/ppermute | solution.py:57
  79.2 2.0 %collective-permute-start.13 = (bf16[512,128]{1,0:T(8,128)(2,1)S(1)}, bf16[512,128]{1,0:T(8,128)(2,1)S(1)}, u32[]{:S(2)}, u32[]{:S(2)}) collective-permute-start(bf16[512,128]{1,0:T(8,128)(2,1)S(1)} %get-tuple-element.72), channel_id=1, source_target_pairs={{0,1},{1,2},{2,3},{3,0},{4,5},{5,6},{6,7},{7,4},{8,9},{9,10},{10,1... | collective-permute-start | bytes 393224 | tf_op jit(solution)/shard_map/ppermute | solution.py:57
  81.2 2.2 %collective-permute-start.14 = (bf16[512,128]{1,0:T(8,128)(2,1)S(1)}, bf16[512,128]{1,0:T(8,128)(2,1)S(1)}, u32[]{:S(2)}, u32[]{:S(2)}) collective-permute-start(bf16[512,128]{1,0:T(8,128)(2,1)S(1)} %get-tuple-element.73), channel_id=1, source_target_pairs={{0,3},{1,0},{2,1},{3,2},{4,7},{5,4},{6,5},{7,6},{8,11},{9,8},{10,9... | collective-permute-start | bytes 393224 | tf_op jit(solution)/shard_map/ppermute | solution.py:57
  83.4 1.8 %collective-permute-start.15 = (bf16[512,128]{1,0:T(8,128)(2,1)S(1)}, bf16[512,128]{1,0:T(8,128)(2,1)S(1)}, u32[]{:S(2)}, u32[]{:S(2)}) collective-permute-start(bf16[512,128]{1,0:T(8,128)(2,1)S(1)} %get-tuple-element.74), channel_id=1, source_target_pairs={{0,2},{1,3},{2,0},{3,1},{4,6},{5,7},{6,4},{7,5},{8,10},{9,11},{10,... | collective-permute-start | bytes 393224 | tf_op jit(solution)/shard_map/ppermute | solution.py:57
  85.1 1.1 collective-permute-done.13.refs_1_
  86.2 3.6 %collective-permute-done.15.refs_3_ = bf16[512,128]{1,0:T(8,128)(2,1)S(1)} collective-permute-done((bf16[512,128]{1,0:T(8,128)(2,1)S(1)}, bf16[512,128]{1,0:T(8,128)(2,1)S(1)}, u32[]{:S(2)}, u32[]{:S(2)}) %collective-permute-start.15) | collective-permute-done | bytes 131104 | tf_op jit(solution)/shard_map/ppermute | solution.py:57
  89.9 1.5 %collective-permute-start.16 = (bf16[512,128]{1,0:T(8,128)(2,1)S(1)}, bf16[512,128]{1,0:T(8,128)(2,1)S(1)}, u32[]{:S(2)}, u32[]{:S(2)}) collective-permute-start(bf16[512,128]{1,0:T(8,128)(2,1)S(1)} %shard_map.105), channel_id=1, source_target_pairs={{0,64},{1,65},{2,66},{3,67},{4,68},{5,69},{6,70},{7,71},{8,72},{9,... | collective-permute-start | bytes 393224 | tf_op jit(solution)/shard_map/ppermute | solution.py:57
  91.4 3.5 %collective-permute-done.16 = bf16[512,128]{1,0:T(8,128)(2,1)S(1)} collective-permute-done((bf16[512,128]{1,0:T(8,128)(2,1)S(1)}, bf16[512,128]{1,0:T(8,128)(2,1)S(1)}, u32[]{:S(2)}, u32[]{:S(2)}) %collective-permute-start.16) | collective-permute-done | bytes 131104 | tf_op jit(solution)/shard_map/ppermute | solution.py:57
  95.1 1.5 %collective-permute-done.17.other = bf16[2,512,128]{2,1,0:T(8,128)(2,1)S(1)} collective-permute-done((bf16[2,512,128]{2,1,0:T(8,128)(2,1)S(1)}, bf16[2,512,128]{2,1,0:T(8,128)(2,1)S(1)}, u32[]{:S(2)}, u32[]{:S(2)}) %collective-permute-start.17) | collective-permute-done | bytes 262176 | tf_op jit(solution)/shard_map/ppermute | solution.py:57
  96.6 1.3 %shard_map.107 = bf16[256,512]{1,0:T(8,128)(2,1)S(1)} custom-call(bf16[2,512,128]{2,1,0:T(8,128)(2,1)S(1)} %pad_maximum_fusion.own, bf16[2,512,128]{2,1,0:T(8,128)(2,1)S(1)} %collective-permute-done.17.other, f32[512,512]{1,0:T(8,128)S(1)} %copy-done, f32[512,512]{1,0:T(8,128)S(1)} %copy-done.1, f32[512,512]{1,0:T(8,128)S(1)} %copy-done.2, ...), custom_call_target="tpu_custom_call" | custom-call | flops 5242880 | bytes 3670016 | tf_op jit(solution)/shard_map/pallas_call | solution.py:224
  98.0 0.7 copy-done.5
  98.6 5.3 %all-to-all-start = ((bf16[32,8,512]{2,1,0:T(8,128)(2,1)}), bf16[32,8,512]{2,1,0:T(8,128)(2,1)}, u32[]{:S(2)}, u32[]{:S(2)}) async-start(bf16[32,8,512]{2,1,0:T(8,128)(2,1)} %bitcast.4), calls=%async_computation | async-start | bytes 524288 | tf_op jit(solution)/shard_map/all_to_all | solution.py:397
  103.9 0.9 copy-done.4
  104.9 2.1 %shard_map.106 = (f32[512,512]{1,0:T(8,128)}, f32[512,512]{1,0:T(8,128)}, f32[512,512]{1,0:T(8,128)}) custom-call(bf16[2,512,128]{2,1,0:T(8,128)(2,1)S(1)} %pad_maximum_fusion.own, bf16[2,512,128]{2,1,0:T(8,128)(2,1)S(1)} %copy-done.4, f32[512,512]{1,0:T(8,128)S(1)} %copy-done, f32[512,512]{1,0:T(8,128)S(1)} %copy-done.1, f32[512,512]{1,0:T(8,128)S(1)} %copy-done.2), custom_call_target="tpu_custom_call" | custom-call | flops 5242880 | bytes 6815744 | tf_op jit(solution)/shard_map/pallas_call | solution.py:235
  107.0 8.0 %all-to-all-done = bf16[32,8,512]{2,1,0:T(8,128)(2,1)} async-done(((bf16[32,8,512]{2,1,0:T(8,128)(2,1)}), bf16[32,8,512]{2,1,0:T(8,128)(2,1)}, u32[]{:S(2)}, u32[]{:S(2)}) %all-to-all-start) | async-done | bytes 262176 | tf_op jit(solution)/shard_map/all_to_all | solution.py:397
  114.9 1.7 %shard_map.108 = bf16[128,2,512]{2,1,0:T(2,128)(2,1)} custom-call(bf16[256,512]{1,0:T(8,128)(2,1)} %bitcast.3.rows), custom_call_target="tpu_custom_call" | custom-call | tf_op jit(solution)/shard_map/pallas_call | solution.py:194
  (36 shorter events, 5.2 us)
Async XLA Ops:
  8.1 5.9 %collective-permute-start.1 = (bf16[8192,128]{1,0:T(8,128)(2,1)}, bf16[8192,128]{1,0:T(8,128)(2,1)S(1)}, u32[]{:S(2)}, u32[]{:S(2)}) collective-permute-start(bf16[8192,128]{1,0:T(8,128)(2,1)} %get-tuple-element.42), channel_id=1, source_target_pairs={{0,32},{1,33},{2,34},{3,35},{4,36},{5,37},{6,38},{7,39},{8,40},{9,... | collective-permute-start | bytes 6291464 | tf_op jit(solution)/shard_map/ppermute | solution.py:57
  8.2 7.4 %collective-permute-start = (bf16[8192,128]{1,0:T(8,128)(2,1)}, bf16[8192,128]{1,0:T(8,128)(2,1)S(1)}, u32[]{:S(2)}, u32[]{:S(2)}) collective-permute-start(bf16[8192,128]{1,0:T(8,128)(2,1)} %get-tuple-element.43), channel_id=1, source_target_pairs={{0,32},{1,33},{2,34},{3,35},{4,36},{5,37},{6,38},{7,39},{8,40},{9,... | collective-permute-start | bytes 6291464 | tf_op jit(solution)/shard_map/ppermute | solution.py:57
  16.1 27.3 %collective-permute-start.4 = (bf16[8192,128]{1,0:T(8,128)(2,1)S(1)}, bf16[8192,128]{1,0:T(8,128)(2,1)S(1)}, u32[]{:S(2)}, u32[]{:S(2)}) collective-permute-start(bf16[8192,128]{1,0:T(8,128)(2,1)S(1)} %shard_map.96), channel_id=1, source_target_pairs={{0,24},{1,25},{2,26},{3,27},{4,28},{5,29},{6,30},{7,31},{8,16},{9,... | collective-permute-start | bytes 6291464 | tf_op jit(solution)/shard_map/ppermute | solution.py:57
  19.1 26.0 %collective-permute-start.3 = (bf16[8192,128]{1,0:T(8,128)(2,1)S(1)}, bf16[8192,128]{1,0:T(8,128)(2,1)S(1)}, u32[]{:S(2)}, u32[]{:S(2)}) collective-permute-start(bf16[8192,128]{1,0:T(8,128)(2,1)S(1)} %shard_map.95), channel_id=1, source_target_pairs={{0,8},{1,9},{2,10},{3,11},{4,12},{5,13},{6,14},{7,15},{8,0},{9,1},... | collective-permute-start | bytes 6291464 | tf_op jit(solution)/shard_map/ppermute | solution.py:57
  27.2 18.4 %collective-permute-start.5 = (bf16[4096,128]{1,0:T(8,128)(2,1)}, bf16[4096,128]{1,0:T(8,128)(2,1)S(1)}, u32[]{:S(2)}, u32[]{:S(2)}) collective-permute-start(bf16[4096,128]{1,0:T(8,128)(2,1)} %get-tuple-element.56), channel_id=1, source_target_pairs={{0,32},{1,33},{2,34},{3,35},{4,36},{5,37},{6,38},{7,39},{8,40},{9,... | collective-permute-start | bytes 3145736 | tf_op jit(solution)/shard_map/ppermute | solution.py:57
  27.3 18.3 %collective-permute-start.6 = (bf16[4096,128]{1,0:T(8,128)(2,1)}, bf16[4096,128]{1,0:T(8,128)(2,1)S(1)}, u32[]{:S(2)}, u32[]{:S(2)}) collective-permute-start(bf16[4096,128]{1,0:T(8,128)(2,1)} %get-tuple-element.57), channel_id=1, source_target_pairs={{0,32},{1,33},{2,34},{3,35},{4,36},{5,37},{6,38},{7,39},{8,40},{9,... | collective-permute-start | bytes 3145736 | tf_op jit(solution)/shard_map/ppermute | solution.py:57
  27.8 20.2 %collective-permute-start.2 = (bf16[4096,128]{1,0:T(8,128)(2,1)}, bf16[4096,128]{1,0:T(8,128)(2,1)S(1)}, u32[]{:S(2)}, u32[]{:S(2)}) collective-permute-start(bf16[4096,128]{1,0:T(8,128)(2,1)} %get-tuple-element.51), channel_id=1, source_target_pairs={{0,32},{1,33},{2,34},{3,35},{4,36},{5,37},{6,38},{7,39},{8,40},{9,... | collective-permute-start | bytes 3145736 | tf_op jit(solution)/shard_map/ppermute | solution.py:57
  43.5 4.6 %collective-permute-start.7 = (bf16[4096,128]{1,0:T(8,128)(2,1)}, bf16[4096,128]{1,0:T(8,128)(2,1)S(1)}, u32[]{:S(2)}, u32[]{:S(2)}) collective-permute-start(bf16[4096,128]{1,0:T(8,128)(2,1)} %get-tuple-element.61), channel_id=1, source_target_pairs={{0,32},{1,33},{2,34},{3,35},{4,36},{5,37},{6,38},{7,39},{8,40},{9,... | collective-permute-start | bytes 3145736 | tf_op jit(solution)/shard_map/ppermute | solution.py:57
  46.2 14.9 %collective-permute-start.10 = (bf16[4096,128]{1,0:T(8,128)(2,1)S(1)}, bf16[4096,128]{1,0:T(8,128)(2,1)S(1)}, u32[]{:S(2)}, u32[]{:S(2)}) collective-permute-start(bf16[4096,128]{1,0:T(8,128)(2,1)S(1)} %get-tuple-element.59), channel_id=1, source_target_pairs={{0,8},{1,9},{2,10},{3,11},{4,12},{5,13},{6,14},{7,15},{8,0},{9,1},... | collective-permute-start | bytes 3145736 | tf_op jit(solution)/shard_map/ppermute | solution.py:57
  46.5 18.3 %collective-permute-start.8 = (bf16[4096,128]{1,0:T(8,128)(2,1)S(1)}, bf16[4096,128]{1,0:T(8,128)(2,1)S(1)}, u32[]{:S(2)}, u32[]{:S(2)}) collective-permute-start(bf16[4096,128]{1,0:T(8,128)(2,1)S(1)} %get-tuple-element.58), channel_id=1, source_target_pairs={{0,24},{1,25},{2,26},{3,27},{4,28},{5,29},{6,30},{7,31},{8,16},{9,... | collective-permute-start | bytes 3145736 | tf_op jit(solution)/shard_map/ppermute | solution.py:57
  61.4 10.6 %collective-permute-start.11 = (bf16[2048,128]{1,0:T(8,128)(2,1)S(1)}, bf16[2048,128]{1,0:T(8,128)(2,1)S(1)}, u32[]{:S(2)}, u32[]{:S(2)}) collective-permute-start(bf16[2048,128]{1,0:T(8,128)(2,1)S(1)} %get-tuple-element.69), channel_id=1, source_target_pairs={{0,64},{1,65},{2,66},{3,67},{4,68},{5,69},{6,70},{7,71},{8,72},{9,... | collective-permute-start | bytes 1572872 | tf_op jit(solution)/shard_map/ppermute | solution.py:57
  63.2 9.2 %collective-permute-start.12 = (bf16[2048,128]{1,0:T(8,128)(2,1)S(1)}, bf16[2048,128]{1,0:T(8,128)(2,1)S(1)}, u32[]{:S(2)}, u32[]{:S(2)}) collective-permute-start(bf16[2048,128]{1,0:T(8,128)(2,1)S(1)} %get-tuple-element.70), channel_id=1, source_target_pairs={{0,68},{1,69},{2,70},{3,71},{4,64},{5,65},{6,66},{7,67},{8,76},{9,... | collective-permute-start | bytes 1572872 | tf_op jit(solution)/shard_map/ppermute | solution.py:57
  65.2 31.4 %copy-start = (f32[512,512]{1,0:T(8,128)S(1)}, f32[512,512]{1,0:T(8,128)}, u32[]{:S(2)}) copy-start(f32[512,512]{1,0:T(8,128)} %master.3) | copy-start | bytes 3145732
  65.2 31.4 %copy-start.1 = (f32[512,512]{1,0:T(8,128)S(1)}, f32[512,512]{1,0:T(8,128)}, u32[]{:S(2)}) copy-start(f32[512,512]{1,0:T(8,128)} %moment1.3) | copy-start | bytes 3145732
  65.2 31.4 %copy-start.2 = (f32[512,512]{1,0:T(8,128)S(1)}, f32[512,512]{1,0:T(8,128)}, u32[]{:S(2)}) copy-start(f32[512,512]{1,0:T(8,128)} %moment2.3) | copy-start | bytes 3145732
  65.2 13.7 %collective-permute-start.9 = (bf16[2048,128]{1,0:T(8,128)(2,1)S(1)}, bf16[2048,128]{1,0:T(8,128)(2,1)S(1)}, u32[]{:S(2)}, u32[]{:S(2)}) collective-permute-start(bf16[2048,128]{1,0:T(8,128)(2,1)S(1)} %get-tuple-element.66), channel_id=1, source_target_pairs={{0,4},{1,5},{2,6},{3,7},{4,0},{5,1},{6,2},{7,3},{8,12},{9,13},{10,... | collective-permute-start | bytes 1572872 | tf_op jit(solution)/shard_map/ppermute | solution.py:57
  79.2 7.1 %collective-permute-start.13 = (bf16[512,128]{1,0:T(8,128)(2,1)S(1)}, bf16[512,128]{1,0:T(8,128)(2,1)S(1)}, u32[]{:S(2)}, u32[]{:S(2)}) collective-permute-start(bf16[512,128]{1,0:T(8,128)(2,1)S(1)} %get-tuple-element.72), channel_id=1, source_target_pairs={{0,1},{1,2},{2,3},{3,0},{4,5},{5,6},{6,7},{7,4},{8,9},{9,10},{10,1... | collective-permute-start | bytes 393224 | tf_op jit(solution)/shard_map/ppermute | solution.py:57
  81.2 5.1 %collective-permute-start.14 = (bf16[512,128]{1,0:T(8,128)(2,1)S(1)}, bf16[512,128]{1,0:T(8,128)(2,1)S(1)}, u32[]{:S(2)}, u32[]{:S(2)}) collective-permute-start(bf16[512,128]{1,0:T(8,128)(2,1)S(1)} %get-tuple-element.73), channel_id=1, source_target_pairs={{0,3},{1,0},{2,1},{3,2},{4,7},{5,4},{6,5},{7,6},{8,11},{9,8},{10,9... | collective-permute-start | bytes 393224 | tf_op jit(solution)/shard_map/ppermute | solution.py:57
  83.4 6.5 %collective-permute-start.15 = (bf16[512,128]{1,0:T(8,128)(2,1)S(1)}, bf16[512,128]{1,0:T(8,128)(2,1)S(1)}, u32[]{:S(2)}, u32[]{:S(2)}) collective-permute-start(bf16[512,128]{1,0:T(8,128)(2,1)S(1)} %get-tuple-element.74), channel_id=1, source_target_pairs={{0,2},{1,3},{2,0},{3,1},{4,6},{5,7},{6,4},{7,5},{8,10},{9,11},{10,... | collective-permute-start | bytes 393224 | tf_op jit(solution)/shard_map/ppermute | solution.py:57
  89.9 5.0 %collective-permute-start.16 = (bf16[512,128]{1,0:T(8,128)(2,1)S(1)}, bf16[512,128]{1,0:T(8,128)(2,1)S(1)}, u32[]{:S(2)}, u32[]{:S(2)}) collective-permute-start(bf16[512,128]{1,0:T(8,128)(2,1)S(1)} %shard_map.105), channel_id=1, source_target_pairs={{0,64},{1,65},{2,66},{3,67},{4,68},{5,69},{6,70},{7,71},{8,72},{9,... | collective-permute-start | bytes 393224 | tf_op jit(solution)/shard_map/ppermute | solution.py:57
  95.0 1.6 %collective-permute-start.17 = (bf16[2,512,128]{2,1,0:T(8,128)(2,1)S(1)}, bf16[2,512,128]{2,1,0:T(8,128)(2,1)S(1)}, u32[]{:S(2)}, u32[]{:S(2)}) collective-permute-start(bf16[2,512,128]{2,1,0:T(8,128)(2,1)S(1)} %pad_maximum_fusion.own), channel_id=1, source_target_pairs={{0,32},{1,33},{2,34},{3,35},{4,36},{5,37},{6,38},{7,39},{8,40},{9,... | collective-permute-start | bytes 786440 | tf_op jit(solution)/shard_map/ppermute | solution.py:57
  96.6 1.3 %copy-start.3 = (bf16[2,512,128]{2,1,0:T(8,128)(2,1)}, bf16[2,512,128]{2,1,0:T(8,128)(2,1)S(1)}, u32[]{:S(2)}) copy-start(bf16[2,512,128]{2,1,0:T(8,128)(2,1)S(1)} %collective-permute-done.17.other) | copy-start | bytes 786436
  97.9 0.7 copy-start.5
  98.6 16.3 %all-to-all-start = ((bf16[32,8,512]{2,1,0:T(8,128)(2,1)}), bf16[32,8,512]{2,1,0:T(8,128)(2,1)}, u32[]{:S(2)}, u32[]{:S(2)}) async-start(bf16[32,8,512]{2,1,0:T(8,128)(2,1)} %bitcast.4), calls=%async_computation | async-start | bytes 524288 | tf_op jit(solution)/shard_map/all_to_all | solution.py:397
  103.9 1.0 copy-start.4

commit v4 on v3

--- a/solution.py
+++ b/solution.py
@@ -74,7 +74,7 @@
         distances = (odd if half else even, 2) if is_sent else (0, even if half else odd)
         tile = 0
         for one in distances:
-            for two in (half, half + 2):
+            for two in (1 - half, 3 - half):
                 for three in range(SIDE):
                     x = lax.rem(place[0] + jnp.where(is_first, one, three), SIDE)
                     y = lax.rem(place[1] + jnp.where(is_first, two, one), SIDE)
@@ -174,37 +174,13 @@
     return piece.T.astype(jnp.float32)
 
 
-def weight_body(own, other, master, moment1, moment2, selector, outgoing, weight):
-    for at in range(4):
-        rows = slice(at * 128, (at + 1) * 128)
-        new, _, _ = updated(rep_grad(own, other, at), master[rows], moment1[rows], moment2[rows])
-        weight[rows] = new.astype(jnp.bfloat16)
-    outgoing[...] = jnp.dot(
-        selector[...], weight[...], preferred_element_type=jnp.float32
-    ).astype(jnp.bfloat16)
-
-
-def unpack_body(rows, blocks):
-    blocks[...] = rows[...].reshape(blocks.shape)
-
-
-def unpacked(rows, block_rows):
-    vmem = pl.BlockSpec(memory_space=pltpu.VMEM)
-    shape = (rows.shape[0] // block_rows, block_rows, rows.shape[1])
-    return pl.pallas_call(
-        unpack_body,
-        out_shape=jax.ShapeDtypeStruct(shape, rows.dtype),
-        in_specs=[vmem],
-        out_specs=vmem,
-    )(rows)
-
-
-def adam_body(own, other, master, moment1, moment2, *refs):
-    outs, kept, sem = refs[:3], refs[3:6], refs[6]
+def adam_body(own, other, master, moment1, moment2, selector, *refs):
+    outgoing, outs, weight, kept, sem = refs[0], refs[1:4], refs[4], refs[5:8], refs[8]
     copies = []
     for at in range(4):
         rows = slice(at * 128, (at + 1) * 128)
         values = updated(rep_grad(own, other, at), master[rows], moment1[rows], moment2[rows])
+        weight[rows] = values[0].astype(jnp.bfloat16)
         for k in range(3):
             kept[k][rows] = values[k]
             copy = pltpu.make_async_copy(
@@ -212,6 +188,8 @@
             )
             copy.start()
             copies.append(copy)
+    chosen = jnp.dot(selector[...], weight[...], preferred_element_type=jnp.float32)
+    outgoing[...] = chosen.astype(jnp.bfloat16).reshape(outgoing.shape)
     for copy in copies:
         copy.wait()
 
@@ -219,31 +197,22 @@
 def adam(own, other, master, moment1, moment2, selector):
     rows, columns = master.shape
     size = rows * columns
-    params = pltpu.CompilerParams(vmem_limit_bytes=12 * 1024 * 1024)
     vmem = pl.BlockSpec(memory_space=pltpu.VMEM)
-    outgoing = pl.pallas_call(
-        weight_body,
-        out_shape=jax.ShapeDtypeStruct((selector.shape[0], columns), jnp.bfloat16),
+    slots = (selector.shape[0] // BLOCK_ROWS, BLOCK_ROWS, columns)
+    outgoing, *state = pl.pallas_call(
+        adam_body,
+        out_shape=[jax.ShapeDtypeStruct(slots, jnp.bfloat16)]
+        + [jax.ShapeDtypeStruct((rows, columns), jnp.float32)] * 3,
         in_specs=[vmem] * 6,
-        out_specs=vmem,
-        scratch_shapes=[pltpu.VMEM((rows, columns), jnp.bfloat16)],
-        compiler_params=params,
-        cost_estimate=pl.CostEstimate(
-            flops=20 * size, bytes_accessed=14 * size, transcendentals=0
-        ),
-    )(own, other, master, moment1, moment2, selector)
-    state = pl.pallas_call(
-        adam_body,
-        out_shape=[jax.ShapeDtypeStruct((rows, columns), jnp.float32)] * 3,
-        in_specs=[vmem] * 5,
-        out_specs=[pl.BlockSpec(memory_space=pl.ANY)] * 3,
-        scratch_shapes=[pltpu.VMEM((rows, columns), jnp.float32)] * 3
+        out_specs=[vmem] + [pl.BlockSpec(memory_space=pl.ANY)] * 3,
+        scratch_shapes=[pltpu.VMEM((rows, columns), jnp.bfloat16)]
+        + [pltpu.VMEM((rows, columns), jnp.float32)] * 3
         + [pltpu.SemaphoreType.DMA((3, 4))],
-        compiler_params=params,
+        compiler_params=pltpu.CompilerParams(vmem_limit_bytes=16 * 1024 * 1024),
         cost_estimate=pl.CostEstimate(
             flops=20 * size, bytes_accessed=26 * size, transcendentals=0
         ),
-    )(own, other, master, moment1, moment2)
+    )(own, other, master, moment1, moment2, selector)
     return outgoing, state
 
 
@@ -327,7 +296,7 @@
     rows = 4 * columns
     sums = [None] * SIDE
     for odd in range(2):
-        sums[odd], sums[odd + 2] = combine(
+        sums[1 - odd], sums[3 - odd] = combine(
             [near[odd], after(got[odd], early)], [[(rows, [(0, at), (1, at)])] for at in (0, rows)]
         )
     parts = [sums[0]] + [send(sums[at], ring_pairs(1, at)) for at in far]
@@ -338,9 +307,10 @@
 
 
 def select_body(capacity, fsdp_count, owner, selector):
-    blocks = owner.shape[1]
+    blocks = owner.shape[0] // fsdp_count
     shape = (blocks, blocks)
-    mine = owner[pl.ds(lax.axis_index("fsdp"), 1), :]
+    first = pl.multiple_of(lax.axis_index("fsdp") * blocks, blocks)
+    mine = owner[pl.ds(first, blocks)].reshape(1, blocks)
     by_lane = jnp.broadcast_to(mine, shape)
     earlier = lax.broadcasted_iota(jnp.int32, shape, 0) < lax.broadcasted_iota(jnp.int32, shape, 1)
     same = jnp.where(by_lane.T == by_lane, 1.0, 0.0)
@@ -366,7 +336,7 @@
 
 def select_blocks(owner, capacity, fsdp_count):
     vmem = pl.BlockSpec(memory_space=pltpu.VMEM)
-    shape = (fsdp_count * capacity * BLOCK_ROWS, owner.shape[1] * BLOCK_ROWS)
+    shape = (fsdp_count * capacity * BLOCK_ROWS, owner.shape[0] // fsdp_count * BLOCK_ROWS)
     return pl.pallas_call(
         functools.partial(select_body, capacity, fsdp_count),
         out_shape=jax.ShapeDtypeStruct(shape, jnp.bfloat16),
@@ -384,18 +354,15 @@
     columns = master.shape[1]
     local_blocks = shard_rows // BLOCK_ROWS
     capacity = 2 * local_blocks // (rep_count * fsdp_count)
-    owner, cotangent = lax.optimization_barrier(
-        (owner.reshape(fsdp_count, local_blocks), cotangent)
-    )
     selector = select_blocks(owner, capacity, fsdp_count)
     mine = summed(tokens, cotangent, selector)
     beside = send(mine, rep_pairs(2))
     own = jnp.stack([mine, beside])
     other = send(own, rep_pairs(1))
     outgoing, state = adam(own, other, master, moment1, moment2, selector)
-    outgoing = outgoing.reshape(fsdp_count, capacity * BLOCK_ROWS, columns)
+    outgoing = outgoing.reshape(fsdp_count, capacity, BLOCK_ROWS, columns)
     received = lax.all_to_all(outgoing, "fsdp", split_axis=0, concat_axis=0, tiled=True)
-    upload = unpacked(received.reshape(fsdp_count * capacity * BLOCK_ROWS, columns), BLOCK_ROWS)
+    upload = received.reshape(fsdp_count * capacity, BLOCK_ROWS, columns)
     return (*state, upload)
 
 

time: 117 us -> 116 us (level)
  blocking collectives: 0 us -> 16 us
  waiting for transfers between devices: 59.7 us -> 53.2 us
  starting transfers between devices: 24.2 us -> 18.8 us
  Pallas kernels: 29.3 us -> 26.4 us
  local copies, waits for them, and re-layouts: 2.43 us -> 0.73 us
    all_to_all x0 -> x1, blocking collectives: none -> 16 us  [per_device(): lax.all_to_all(outgoing, 'fsdp', split_axis=0, concat_axis=0, tiled=True)]
    all_to_all x1 -> x0, waiting for transfers between devices: 7.96 us -> none  [per_device(): lax.all_to_all(outgoing, 'fsdp', split_axis=0, concat_axis=0, tiled=True)]
    all_to_all x1 -> x0, starting transfers between devices: 5.28 us -> none  [per_device(): lax.all_to_all(outgoing, 'fsdp', split_axis=0, concat_axis=0, tiled=True)]
    pallas_call x3 -> x1, Pallas kernels: 5.09 us -> 2.28 us  [adam(): pl.pallas_call(adam_body, out_shape=[jax.ShapeDtypeStruct(slots, jnp.bflo...]
    ppermute x18, waiting for transfers between devices: 51.8 us -> 53.2 us  [send(): return lax.ppermute(value, AXES, pairs)]
  transfers between devices with their start and end apart: 19 -> 18, of which waited for: 12 -> 11; matrix products, arithmetic and copies ran while one was open for 0% -> 0% of each run, Pallas kernels for 16% -> 14%
where the time goes in v4:
time: 116 us
  waiting for transfers between devices  53.2 us (46%)
  Pallas kernels  26.4 us (23%)
  starting transfers between devices  18.8 us (16%)
  blocking collectives  16 us (14%)
    ppermute x18, waiting for transfers between devices, send(): return lax.ppermute(value, AXES, pairs)  53.2 us
    pallas_call x3, Pallas kernels, split_sums(): pl.pallas_call(functools.partial(split_body, groups), out_shape=outs, in_...  19.9 us
    ppermute x18, starting transfers between devices, send(): return lax.ppermute(value, AXES, pairs)  18.8 us
    all_to_all x1, blocking collectives, per_device(): lax.all_to_all(outgoing, 'fsdp', split_axis=0, concat_axis=0, tiled=True)  16 us
    pallas_call x9, Pallas kernels, combine(): pl.pallas_call(functools.partial(combine_body, plan), out_shape=[pltpu.VM...  3.95 us
  transfers between devices with their start and end apart: 18, of which 11 were waited for; matrix products, arithmetic and copies ran while one was open for 0% of the time, Pallas kernels for 14%

profile of v4, /device:TPU:0, one launch (start us, length us, event | category | flops | bytes accessed | tf_op | source)
XLA Modules:
  0.0 115.9 jit_solution(6147386677632160051)
XLA Ops:
  0.6 6.7 %shard_map.93 = (bf16[8192,128]{1,0:T(8,128)(2,1)}, bf16[8192,128]{1,0:T(8,128)(2,1)}) custom-call(bf16[512,512]{1,0:T(8,128)(2,1)} %cot.3, bf16[512,16384]{1,0:T(8,128)(2,1)} %tokens.5), custom_call_target="tpu_custom_call" | custom-call | flops 2147483648 | bytes 8388608 | tf_op jit(solution)/shard_map/pallas_call | solution.py:137
  7.4 0.5 collective-permute-start
  7.9 5.3 %shard_map.94 = (bf16[8192,128]{1,0:T(8,128)(2,1)S(1)}, bf16[8192,128]{1,0:T(8,128)(2,1)S(1)}) custom-call(bf16[512,512]{1,0:T(8,128)(2,1)} %cot.3, bf16[512,16384]{1,0:T(8,128)(2,1)} %tokens.5), custom_call_target="tpu_custom_call" | custom-call | flops 2147483648 | bytes 8388608 | tf_op jit(solution)/shard_map/pallas_call | solution.py:137
  13.2 0.6 shard_map.95
  13.7 1.0 collective-permute-done.refs_1_
  14.7 0.6 shard_map.96
  15.3 2.9 %collective-permute-start.4 = (bf16[8192,128]{1,0:T(8,128)(2,1)S(1)}, bf16[8192,128]{1,0:T(8,128)(2,1)S(1)}, u32[]{:S(2)}, u32[]{:S(2)}) collective-permute-start(bf16[8192,128]{1,0:T(8,128)(2,1)S(1)} %shard_map.96), channel_id=1, source_target_pairs={{0,24},{1,25},{2,26},{3,27},{4,28},{5,29},{6,30},{7,31},{8,16},{9,... | collective-permute-start | bytes 6291464 | tf_op jit(solution)/shard_map/ppermute | solution.py:57
  18.4 8.0 %shard_map.97 = (bf16[4096,128]{1,0:T(8,128)(2,1)}, bf16[4096,128]{1,0:T(8,128)(2,1)}, bf16[4096,128]{1,0:T(8,128)(2,1)}, bf16[4096,128]{1,0:T(8,128)(2,1)}, bf1...) custom-call(bf16[512,512]{1,0:T(8,128)(2,1)} %cot.3, ...), custom_call_target="tpu_custom_call" | custom-call | flops 4294967296 | bytes 16777216 | tf_op jit(solution)/shard_map/pallas_call | solution.py:137
  26.5 0.5 collective-permute-start.6
  27.1 15.5 %collective-permute-done.4.refs_3_.refs_5_ = bf16[8192,128]{1,0:T(8,128)(2,1)S(1)} collective-permute-done((bf16[8192,128]{1,0:T(8,128)(2,1)S(1)}, bf16[8192,128]{1,0:T(8,128)(2,1)S(1)}, u32[]{:S(2)}, u32[]{:S(2)}) %collective-permute-start.4) | collective-permute-done | bytes 2097184 | tf_op jit(solution)/shard_map/ppermute | solution.py:57
  42.6 1.6 %collective-permute-done.3.refs_2_.refs_4_ = bf16[8192,128]{1,0:T(8,128)(2,1)S(1)} collective-permute-done((bf16[8192,128]{1,0:T(8,128)(2,1)S(1)}, bf16[8192,128]{1,0:T(8,128)(2,1)S(1)}, u32[]{:S(2)}, u32[]{:S(2)}) %collective-permute-start.3) | collective-permute-done | bytes 2097184 | tf_op jit(solution)/shard_map/ppermute | solution.py:57
  44.3 0.6 shard_map.98
  44.8 0.6 shard_map.99
  45.4 1.3 %collective-permute-start.10 = (bf16[4096,128]{1,0:T(8,128)(2,1)S(1)}, bf16[4096,128]{1,0:T(8,128)(2,1)S(1)}, u32[]{:S(2)}, u32[]{:S(2)}) collective-permute-start(bf16[4096,128]{1,0:T(8,128)(2,1)S(1)} %get-tuple-element.56), channel_id=1, source_target_pairs={{0,24},{1,25},{2,26},{3,27},{4,28},{5,29},{6,30},{7,31},{8,16},{9,... | collective-permute-start | bytes 3145736 | tf_op jit(solution)/shard_map/ppermute | solution.py:57
  47.1 0.8 shard_map.100
  47.9 13.6 %collective-permute-done.10.refs_1_ = bf16[4096,128]{1,0:T(8,128)(2,1)S(1)} collective-permute-done((bf16[4096,128]{1,0:T(8,128)(2,1)S(1)}, bf16[4096,128]{1,0:T(8,128)(2,1)S(1)}, u32[]{:S(2)}, u32[]{:S(2)}) %collective-permute-start.10) | collective-permute-done | bytes 1048608 | tf_op jit(solution)/shard_map/ppermute | solution.py:57
  61.8 1.8 %collective-permute-start.11 = (bf16[2048,128]{1,0:T(8,128)(2,1)S(1)}, bf16[2048,128]{1,0:T(8,128)(2,1)S(1)}, u32[]{:S(2)}, u32[]{:S(2)}) collective-permute-start(bf16[2048,128]{1,0:T(8,128)(2,1)S(1)} %get-tuple-element.66), channel_id=1, source_target_pairs={{0,64},{1,65},{2,66},{3,67},{4,68},{5,69},{6,70},{7,71},{8,72},{9,... | collective-permute-start | bytes 1572872 | tf_op jit(solution)/shard_map/ppermute | solution.py:57
  63.6 1.7 %collective-permute-start.12 = (bf16[2048,128]{1,0:T(8,128)(2,1)S(1)}, bf16[2048,128]{1,0:T(8,128)(2,1)S(1)}, u32[]{:S(2)}, u32[]{:S(2)}) collective-permute-start(bf16[2048,128]{1,0:T(8,128)(2,1)S(1)} %get-tuple-element.67), channel_id=1, source_target_pairs={{0,68},{1,69},{2,70},{3,71},{4,64},{5,65},{6,66},{7,67},{8,76},{9,... | collective-permute-start | bytes 1572872 | tf_op jit(solution)/shard_map/ppermute | solution.py:57
  65.6 2.1 %collective-permute-start.9 = (bf16[2048,128]{1,0:T(8,128)(2,1)S(1)}, bf16[2048,128]{1,0:T(8,128)(2,1)S(1)}, u32[]{:S(2)}, u32[]{:S(2)}) collective-permute-start(bf16[2048,128]{1,0:T(8,128)(2,1)S(1)} %get-tuple-element.63), channel_id=1, source_target_pairs={{0,4},{1,5},{2,6},{3,7},{4,0},{5,1},{6,2},{7,3},{8,12},{9,13},{10,... | collective-permute-start | bytes 1572872 | tf_op jit(solution)/shard_map/ppermute | solution.py:57
  67.7 4.8 %collective-permute-done.11.refs_2_ = bf16[2048,128]{1,0:T(8,128)(2,1)S(1)} collective-permute-done((bf16[2048,128]{1,0:T(8,128)(2,1)S(1)}, bf16[2048,128]{1,0:T(8,128)(2,1)S(1)}, u32[]{:S(2)}, u32[]{:S(2)}) %collective-permute-start.11) | collective-permute-done | bytes 524320 | tf_op jit(solution)/shard_map/ppermute | solution.py:57
  72.8 6.5 %collective-permute-done.9.refs_1_ = bf16[2048,128]{1,0:T(8,128)(2,1)S(1)} collective-permute-done((bf16[2048,128]{1,0:T(8,128)(2,1)S(1)}, bf16[2048,128]{1,0:T(8,128)(2,1)S(1)}, u32[]{:S(2)}, u32[]{:S(2)}) %collective-permute-start.9) | collective-permute-done | bytes 524320 | tf_op jit(solution)/shard_map/ppermute | solution.py:57
  79.6 2.0 %collective-permute-start.13 = (bf16[512,128]{1,0:T(8,128)(2,1)S(1)}, bf16[512,128]{1,0:T(8,128)(2,1)S(1)}, u32[]{:S(2)}, u32[]{:S(2)}) collective-permute-start(bf16[512,128]{1,0:T(8,128)(2,1)S(1)} %get-tuple-element.69), channel_id=1, source_target_pairs={{0,1},{1,2},{2,3},{3,0},{4,5},{5,6},{6,7},{7,4},{8,9},{9,10},{10,1... | collective-permute-start | bytes 393224 | tf_op jit(solution)/shard_map/ppermute | solution.py:57
  81.5 2.2 %collective-permute-start.14 = (bf16[512,128]{1,0:T(8,128)(2,1)S(1)}, bf16[512,128]{1,0:T(8,128)(2,1)S(1)}, u32[]{:S(2)}, u32[]{:S(2)}) collective-permute-start(bf16[512,128]{1,0:T(8,128)(2,1)S(1)} %get-tuple-element.70), channel_id=1, source_target_pairs={{0,3},{1,0},{2,1},{3,2},{4,7},{5,4},{6,5},{7,6},{8,11},{9,8},{10,9... | collective-permute-start | bytes 393224 | tf_op jit(solution)/shard_map/ppermute | solution.py:57
  83.7 1.8 %collective-permute-start.15 = (bf16[512,128]{1,0:T(8,128)(2,1)S(1)}, bf16[512,128]{1,0:T(8,128)(2,1)S(1)}, u32[]{:S(2)}, u32[]{:S(2)}) collective-permute-start(bf16[512,128]{1,0:T(8,128)(2,1)S(1)} %get-tuple-element.71), channel_id=1, source_target_pairs={{0,2},{1,3},{2,0},{3,1},{4,6},{5,7},{6,4},{7,5},{8,10},{9,11},{10,... | collective-permute-start | bytes 393224 | tf_op jit(solution)/shard_map/ppermute | solution.py:57
  85.5 1.1 collective-permute-done.13.refs_1_
  86.6 3.6 %collective-permute-done.15.refs_3_ = bf16[512,128]{1,0:T(8,128)(2,1)S(1)} collective-permute-done((bf16[512,128]{1,0:T(8,128)(2,1)S(1)}, bf16[512,128]{1,0:T(8,128)(2,1)S(1)}, u32[]{:S(2)}, u32[]{:S(2)}) %collective-permute-start.15) | collective-permute-done | bytes 131104 | tf_op jit(solution)/shard_map/ppermute | solution.py:57
  90.3 1.5 %collective-permute-start.16 = (bf16[512,128]{1,0:T(8,128)(2,1)S(1)}, bf16[512,128]{1,0:T(8,128)(2,1)S(1)}, u32[]{:S(2)}, u32[]{:S(2)}) collective-permute-start(bf16[512,128]{1,0:T(8,128)(2,1)S(1)} %shard_map.105), channel_id=1, source_target_pairs={{0,64},{1,65},{2,66},{3,67},{4,68},{5,69},{6,70},{7,71},{8,72},{9,... | collective-permute-start | bytes 393224 | tf_op jit(solution)/shard_map/ppermute | solution.py:57
  91.8 3.5 %collective-permute-done.16 = bf16[512,128]{1,0:T(8,128)(2,1)S(1)} collective-permute-done((bf16[512,128]{1,0:T(8,128)(2,1)S(1)}, bf16[512,128]{1,0:T(8,128)(2,1)S(1)}, u32[]{:S(2)}, u32[]{:S(2)}) %collective-permute-start.16) | collective-permute-done | bytes 131104 | tf_op jit(solution)/shard_map/ppermute | solution.py:57
  95.5 1.5 %collective-permute-done.17.other = bf16[2,512,128]{2,1,0:T(8,128)(2,1)S(1)} collective-permute-done((bf16[2,512,128]{2,1,0:T(8,128)(2,1)S(1)}, bf16[2,512,128]{2,1,0:T(8,128)(2,1)S(1)}, u32[]{:S(2)}, u32[]{:S(2)}) %collective-permute-start.17) | collective-permute-done | bytes 262176 | tf_op jit(solution)/shard_map/ppermute | solution.py:57
  97.0 2.3 %shard_map.106 = (bf16[128,2,512]{2,1,0:T(2,128)(2,1)S(1)}, f32[512,512]{1,0:T(8,128)}, f32[512,512]{1,0:T(8,128)}, f32[512,512]{1,0:T(8,128)}) custom-call(bf16[2,512,128]{2,1,0:T(8,128)(2,1)S(1)} %pad_maximum_fusion.own, bf16[2,512,128]{2,1,0:T(8,128)(2,1)S(1)} %collective-permute-done.17.other, f32[512,512]{1,0:T(8,128)S(1)} %copy-done, ...), custom_call_target="tpu_custom_call" | custom-call | flops 5242880 | bytes 6815744 | tf_op jit(solution)/shard_map/pallas_call | solution.py:202
  99.3 16.0 %all_to_all.5 = bf16[32,4,2,512]{3,2,1,0:T(2,128)(2,1)S(1)} all-to-all(bf16[32,4,2,512]{3,2,1,0:T(2,128)(2,1)S(1)} %bitcast.5), channel_id=1, replica_groups=mesh['rep'=4,'fsdp'=32] {'fsdp'}, dimensions={0} | all-to-all | bytes 524288 | tf_op jit(solution)/shard_map/all_to_all | solution.py:364
  115.2 0.7 copy.11
  (29 shorter events, 2.2 us)
Async XLA Ops:
  7.3 5.9 %collective-permute-start.1 = (bf16[8192,128]{1,0:T(8,128)(2,1)}, bf16[8192,128]{1,0:T(8,128)(2,1)S(1)}, u32[]{:S(2)}, u32[]{:S(2)}) collective-permute-start(bf16[8192,128]{1,0:T(8,128)(2,1)} %get-tuple-element.40), channel_id=1, source_target_pairs={{0,32},{1,33},{2,34},{3,35},{4,36},{5,37},{6,38},{7,39},{8,40},{9,... | collective-permute-start | bytes 6291464 | tf_op jit(solution)/shard_map/ppermute | solution.py:57
  7.4 7.4 %collective-permute-start = (bf16[8192,128]{1,0:T(8,128)(2,1)}, bf16[8192,128]{1,0:T(8,128)(2,1)S(1)}, u32[]{:S(2)}, u32[]{:S(2)}) collective-permute-start(bf16[8192,128]{1,0:T(8,128)(2,1)} %get-tuple-element.41), channel_id=1, source_target_pairs={{0,32},{1,33},{2,34},{3,35},{4,36},{5,37},{6,38},{7,39},{8,40},{9,... | collective-permute-start | bytes 6291464 | tf_op jit(solution)/shard_map/ppermute | solution.py:57
  15.3 27.3 %collective-permute-start.4 = (bf16[8192,128]{1,0:T(8,128)(2,1)S(1)}, bf16[8192,128]{1,0:T(8,128)(2,1)S(1)}, u32[]{:S(2)}, u32[]{:S(2)}) collective-permute-start(bf16[8192,128]{1,0:T(8,128)(2,1)S(1)} %shard_map.96), channel_id=1, source_target_pairs={{0,24},{1,25},{2,26},{3,27},{4,28},{5,29},{6,30},{7,31},{8,16},{9,... | collective-permute-start | bytes 6291464 | tf_op jit(solution)/shard_map/ppermute | solution.py:57
  18.2 26.0 %collective-permute-start.3 = (bf16[8192,128]{1,0:T(8,128)(2,1)S(1)}, bf16[8192,128]{1,0:T(8,128)(2,1)S(1)}, u32[]{:S(2)}, u32[]{:S(2)}) collective-permute-start(bf16[8192,128]{1,0:T(8,128)(2,1)S(1)} %shard_map.95), channel_id=1, source_target_pairs={{0,8},{1,9},{2,10},{3,11},{4,12},{5,13},{6,14},{7,15},{8,0},{9,1},... | collective-permute-start | bytes 6291464 | tf_op jit(solution)/shard_map/ppermute | solution.py:57
  26.4 18.4 %collective-permute-start.5 = (bf16[4096,128]{1,0:T(8,128)(2,1)}, bf16[4096,128]{1,0:T(8,128)(2,1)S(1)}, u32[]{:S(2)}, u32[]{:S(2)}) collective-permute-start(bf16[4096,128]{1,0:T(8,128)(2,1)} %get-tuple-element.54), channel_id=1, source_target_pairs={{0,32},{1,33},{2,34},{3,35},{4,36},{5,37},{6,38},{7,39},{8,40},{9,... | collective-permute-start | bytes 3145736 | tf_op jit(solution)/shard_map/ppermute | solution.py:57
  26.5 18.3 %collective-permute-start.6 = (bf16[4096,128]{1,0:T(8,128)(2,1)}, bf16[4096,128]{1,0:T(8,128)(2,1)S(1)}, u32[]{:S(2)}, u32[]{:S(2)}) collective-permute-start(bf16[4096,128]{1,0:T(8,128)(2,1)} %get-tuple-element.55), channel_id=1, source_target_pairs={{0,32},{1,33},{2,34},{3,35},{4,36},{5,37},{6,38},{7,39},{8,40},{9,... | collective-permute-start | bytes 3145736 | tf_op jit(solution)/shard_map/ppermute | solution.py:57
  27.0 20.0 %collective-permute-start.2 = (bf16[4096,128]{1,0:T(8,128)(2,1)}, bf16[4096,128]{1,0:T(8,128)(2,1)S(1)}, u32[]{:S(2)}, u32[]{:S(2)}) collective-permute-start(bf16[4096,128]{1,0:T(8,128)(2,1)} %get-tuple-element.49), channel_id=1, source_target_pairs={{0,32},{1,33},{2,34},{3,35},{4,36},{5,37},{6,38},{7,39},{8,40},{9,... | collective-permute-start | bytes 3145736 | tf_op jit(solution)/shard_map/ppermute | solution.py:57
  42.6 4.4 %collective-permute-start.7 = (bf16[4096,128]{1,0:T(8,128)(2,1)}, bf16[4096,128]{1,0:T(8,128)(2,1)S(1)}, u32[]{:S(2)}, u32[]{:S(2)}) collective-permute-start(bf16[4096,128]{1,0:T(8,128)(2,1)} %get-tuple-element.59), channel_id=1, source_target_pairs={{0,32},{1,33},{2,34},{3,35},{4,36},{5,37},{6,38},{7,39},{8,40},{9,... | collective-permute-start | bytes 3145736 | tf_op jit(solution)/shard_map/ppermute | solution.py:57
  44.8 1.9 %copy-start.3 = (s32[8192]{0:T(1024)S(1)}, s32[8192]{0:T(1024)}, u32[]{:S(2)}) copy-start(s32[8192]{0:T(1024)} %owner.1) | copy-start | bytes 98308
  45.4 16.1 %collective-permute-start.10 = (bf16[4096,128]{1,0:T(8,128)(2,1)S(1)}, bf16[4096,128]{1,0:T(8,128)(2,1)S(1)}, u32[]{:S(2)}, u32[]{:S(2)}) collective-permute-start(bf16[4096,128]{1,0:T(8,128)(2,1)S(1)} %get-tuple-element.56), channel_id=1, source_target_pairs={{0,24},{1,25},{2,26},{3,27},{4,28},{5,29},{6,30},{7,31},{8,16},{9,... | collective-permute-start | bytes 3145736 | tf_op jit(solution)/shard_map/ppermute | solution.py:57
  46.7 18.6 %collective-permute-start.8 = (bf16[4096,128]{1,0:T(8,128)(2,1)S(1)}, bf16[4096,128]{1,0:T(8,128)(2,1)S(1)}, u32[]{:S(2)}, u32[]{:S(2)}) collective-permute-start(bf16[4096,128]{1,0:T(8,128)(2,1)S(1)} %get-tuple-element.57), channel_id=1, source_target_pairs={{0,8},{1,9},{2,10},{3,11},{4,12},{5,13},{6,14},{7,15},{8,0},{9,1},... | collective-permute-start | bytes 3145736 | tf_op jit(solution)/shard_map/ppermute | solution.py:57
  61.8 10.6 %collective-permute-start.11 = (bf16[2048,128]{1,0:T(8,128)(2,1)S(1)}, bf16[2048,128]{1,0:T(8,128)(2,1)S(1)}, u32[]{:S(2)}, u32[]{:S(2)}) collective-permute-start(bf16[2048,128]{1,0:T(8,128)(2,1)S(1)} %get-tuple-element.66), channel_id=1, source_target_pairs={{0,64},{1,65},{2,66},{3,67},{4,68},{5,69},{6,70},{7,71},{8,72},{9,... | collective-permute-start | bytes 1572872 | tf_op jit(solution)/shard_map/ppermute | solution.py:57
  63.6 9.2 %collective-permute-start.12 = (bf16[2048,128]{1,0:T(8,128)(2,1)S(1)}, bf16[2048,128]{1,0:T(8,128)(2,1)S(1)}, u32[]{:S(2)}, u32[]{:S(2)}) collective-permute-start(bf16[2048,128]{1,0:T(8,128)(2,1)S(1)} %get-tuple-element.67), channel_id=1, source_target_pairs={{0,68},{1,69},{2,70},{3,71},{4,64},{5,65},{6,66},{7,67},{8,76},{9,... | collective-permute-start | bytes 1572872 | tf_op jit(solution)/shard_map/ppermute | solution.py:57
  65.6 31.4 %copy-start = (f32[512,512]{1,0:T(8,128)S(1)}, f32[512,512]{1,0:T(8,128)}, u32[]{:S(2)}) copy-start(f32[512,512]{1,0:T(8,128)} %master.1) | copy-start | bytes 3145732
  65.6 31.4 %copy-start.1 = (f32[512,512]{1,0:T(8,128)S(1)}, f32[512,512]{1,0:T(8,128)}, u32[]{:S(2)}) copy-start(f32[512,512]{1,0:T(8,128)} %moment1.1) | copy-start | bytes 3145732
  65.6 31.4 %copy-start.2 = (f32[512,512]{1,0:T(8,128)S(1)}, f32[512,512]{1,0:T(8,128)}, u32[]{:S(2)}) copy-start(f32[512,512]{1,0:T(8,128)} %moment2.1) | copy-start | bytes 3145732
  65.6 13.7 %collective-permute-start.9 = (bf16[2048,128]{1,0:T(8,128)(2,1)S(1)}, bf16[2048,128]{1,0:T(8,128)(2,1)S(1)}, u32[]{:S(2)}, u32[]{:S(2)}) collective-permute-start(bf16[2048,128]{1,0:T(8,128)(2,1)S(1)} %get-tuple-element.63), channel_id=1, source_target_pairs={{0,4},{1,5},{2,6},{3,7},{4,0},{5,1},{6,2},{7,3},{8,12},{9,13},{10,... | collective-permute-start | bytes 1572872 | tf_op jit(solution)/shard_map/ppermute | solution.py:57
  79.6 7.1 %collective-permute-start.13 = (bf16[512,128]{1,0:T(8,128)(2,1)S(1)}, bf16[512,128]{1,0:T(8,128)(2,1)S(1)}, u32[]{:S(2)}, u32[]{:S(2)}) collective-permute-start(bf16[512,128]{1,0:T(8,128)(2,1)S(1)} %get-tuple-element.69), channel_id=1, source_target_pairs={{0,1},{1,2},{2,3},{3,0},{4,5},{5,6},{6,7},{7,4},{8,9},{9,10},{10,1... | collective-permute-start | bytes 393224 | tf_op jit(solution)/shard_map/ppermute | solution.py:57
  81.5 5.1 %collective-permute-start.14 = (bf16[512,128]{1,0:T(8,128)(2,1)S(1)}, bf16[512,128]{1,0:T(8,128)(2,1)S(1)}, u32[]{:S(2)}, u32[]{:S(2)}) collective-permute-start(bf16[512,128]{1,0:T(8,128)(2,1)S(1)} %get-tuple-element.70), channel_id=1, source_target_pairs={{0,3},{1,0},{2,1},{3,2},{4,7},{5,4},{6,5},{7,6},{8,11},{9,8},{10,9... | collective-permute-start | bytes 393224 | tf_op jit(solution)/shard_map/ppermute | solution.py:57
  83.7 6.5 %collective-permute-start.15 = (bf16[512,128]{1,0:T(8,128)(2,1)S(1)}, bf16[512,128]{1,0:T(8,128)(2,1)S(1)}, u32[]{:S(2)}, u32[]{:S(2)}) collective-permute-start(bf16[512,128]{1,0:T(8,128)(2,1)S(1)} %get-tuple-element.71), channel_id=1, source_target_pairs={{0,2},{1,3},{2,0},{3,1},{4,6},{5,7},{6,4},{7,5},{8,10},{9,11},{10,... | collective-permute-start | bytes 393224 | tf_op jit(solution)/shard_map/ppermute | solution.py:57
  90.3 5.0 %collective-permute-start.16 = (bf16[512,128]{1,0:T(8,128)(2,1)S(1)}, bf16[512,128]{1,0:T(8,128)(2,1)S(1)}, u32[]{:S(2)}, u32[]{:S(2)}) collective-permute-start(bf16[512,128]{1,0:T(8,128)(2,1)S(1)} %shard_map.105), channel_id=1, source_target_pairs={{0,64},{1,65},{2,66},{3,67},{4,68},{5,69},{6,70},{7,71},{8,72},{9,... | collective-permute-start | bytes 393224 | tf_op jit(solution)/shard_map/ppermute | solution.py:57
  95.4 1.6 %collective-permute-start.17 = (bf16[2,512,128]{2,1,0:T(8,128)(2,1)S(1)}, bf16[2,512,128]{2,1,0:T(8,128)(2,1)S(1)}, u32[]{:S(2)}, u32[]{:S(2)}) collective-permute-start(bf16[2,512,128]{2,1,0:T(8,128)(2,1)S(1)} %pad_maximum_fusion.own), channel_id=1, source_target_pairs={{0,32},{1,33},{2,34},{3,35},{4,36},{5,37},{6,38},{7,39},{8,40},{9,... | collective-permute-start | bytes 786440 | tf_op jit(solution)/shard_map/ppermute | solution.py:57

commit v5 on v4

--- a/solution.py
+++ b/solution.py
@@ -29,21 +29,21 @@
     return ((y % 2) * 2 + core) * 32 + x * 8 + (y // 2) * 4 + z
 
 
-def ring_pairs(stage, distance):
+def far_pairs(stage):
     pairs = []
     for device in range(128):
         place = list(coords(device))
         axis = ORDERS[place[3]][stage]
-        place[axis] = (place[axis] + distance) % SIDE
+        place[axis] = (place[axis] + 2) % SIDE
         pairs.append((device, index_of(*place)))
     return pairs
 
 
-def swap_pairs(odd):
+def swap_pairs(odd, stage=0):
     pairs = []
     for device in range(128):
         place = list(coords(device))
-        axis = ORDERS[place[3]][0]
+        axis = ORDERS[place[3]][stage]
         place[axis] = (((place[axis] + odd) ^ 1) - odd) % SIDE
         pairs.append((device, index_of(*place)))
     return pairs
@@ -69,13 +69,19 @@
         side, half, is_sent = groups[at]
         target = core if side == 0 else 1 - core
         is_first = target == 0
-        parity = lax.rem(jnp.where(is_first, place[0], place[1]), 2)
-        even, odd = 1 + 2 * parity, 3 - 2 * parity
-        distances = (odd if half else even, 2) if is_sent else (0, even if half else odd)
+        near = []
+        for axis in range(3):
+            along = jnp.where(is_first, place[ORDERS[0][axis]], place[ORDERS[1][axis]])
+            parity = lax.rem(along, 2)
+            near.append((1 + 2 * parity, 3 - 2 * parity))
+        if is_sent:
+            distances = (near[0][half], 2)
+        else:
+            distances = (0, near[0][1 - half])
         tile = 0
         for one in distances:
-            for two in (1 - half, 3 - half):
-                for three in range(SIDE):
+            for two in near[1] if half else (0, 2):
+                for three in (0, 2, *near[2]):
                     x = lax.rem(place[0] + jnp.where(is_first, one, three), SIDE)
                     y = lax.rem(place[1] + jnp.where(is_first, two, one), SIDE)
                     z = lax.rem(place[2] + jnp.where(is_first, three, two), SIDE)
@@ -260,9 +266,18 @@
     return combine(inputs, [[(rows, [(k, 0) for k in range(len(inputs))])]])[0]
 
 
+def exchanged(sums, stage):
+    stay, far, even, odd = sums
+    return [
+        stay,
+        send(even, swap_pairs(0, stage)),
+        send(odd, swap_pairs(1, stage)),
+        send(far, far_pairs(stage)),
+    ]
+
+
 def summed(tokens, cotangent, early):
     columns = cotangent.shape[1]
-    far = (2, 1, 3)
     other = split_sums(tokens, cotangent, [(1, 0, True), (1, 1, True)])
     own = split_sums(tokens, after(cotangent, *other), [(0, 0, True), (0, 1, True)])
     beside = [send(value, rep_pairs(1)) for value in other]
@@ -294,16 +309,16 @@
     )
 
     rows = 4 * columns
-    sums = [None] * SIDE
+    sums = []
     for odd in range(2):
-        sums[1 - odd], sums[3 - odd] = combine(
+        sums += combine(
             [near[odd], after(got[odd], early)], [[(rows, [(0, at), (1, at)])] for at in (0, rows)]
         )
-    parts = [sums[0]] + [send(sums[at], ring_pairs(1, at)) for at in far]
     sums = combine(
-        parts, [[(columns, [(k, at * columns) for k in range(SIDE)])] for at in range(SIDE)]
-    )
-    return total([sums[0]] + [send(sums[at], ring_pairs(2, at)) for at in (1, 3, 2)])
+        exchanged(sums, 1),
+        [[(columns, [(k, at * columns) for k in range(SIDE)])] for at in range(SIDE)],
+    )
+    return total(exchanged(sums, 2))
 
 
 def select_body(capacity, fsdp_count, owner, selector):

time: 116 us -> 115 us (level)
  starting transfers between devices: 18.8 us -> 16.4 us
  waiting for transfers between devices: 53.2 us -> 55 us
    ppermute x18, starting transfers between devices: 18.8 us -> 16.4 us  [send(): return lax.ppermute(value, AXES, pairs)]
    ppermute x18, waiting for transfers between devices: 53.2 us -> 55 us  [send(): return lax.ppermute(value, AXES, pairs)]
  transfers between devices with their start and end apart: 18 -> 18, of which waited for: 11 -> 10; matrix products, arithmetic and copies ran while one was open for 0% -> 0% of each run, Pallas kernels for 14% -> 14%
where the time goes in v5:
time: 115 us
  waiting for transfers between devices  55 us (48%)
  Pallas kernels  26.4 us (23%)
  starting transfers between devices  16.4 us (14%)
  blocking collectives  15.4 us (13%)
    ppermute x18, waiting for transfers between devices, send(): return lax.ppermute(value, AXES, pairs)  55 us
    pallas_call x3, Pallas kernels, split_sums(): pl.pallas_call(functools.partial(split_body, groups), out_shape=outs, in_...  19.9 us
    ppermute x18, starting transfers between devices, send(): return lax.ppermute(value, AXES, pairs)  16.4 us
    all_to_all x1, blocking collectives, per_device(): lax.all_to_all(outgoing, 'fsdp', split_axis=0, concat_axis=0, tiled=True)  15.4 us
    pallas_call x9, Pallas kernels, combine(): pl.pallas_call(functools.partial(combine_body, plan), out_shape=[pltpu.VM...  3.95 us
  transfers between devices with their start and end apart: 18, of which 10 were waited for; matrix products, arithmetic and copies ran while one was open for 0% of the time, Pallas kernels for 14%

profile of v5, /device:TPU:0, one launch (start us, length us, event | category | flops | bytes accessed | tf_op | source)
XLA Modules:
  0.0 114.8 jit_solution(14682836547550607666)
XLA Ops:
  0.6 6.7 %shard_map.93 = (bf16[8192,128]{1,0:T(8,128)(2,1)}, bf16[8192,128]{1,0:T(8,128)(2,1)}) custom-call(bf16[512,512]{1,0:T(8,128)(2,1)} %cot.3, bf16[512,16384]{1,0:T(8,128)(2,1)} %tokens.5), custom_call_target="tpu_custom_call" | custom-call | flops 2147483648 | bytes 8388608 | tf_op jit(solution)/shard_map/pallas_call | solution.py:143
  7.4 0.5 collective-permute-start
  7.9 5.3 %shard_map.94 = (bf16[8192,128]{1,0:T(8,128)(2,1)S(1)}, bf16[8192,128]{1,0:T(8,128)(2,1)S(1)}) custom-call(bf16[512,512]{1,0:T(8,128)(2,1)} %cot.3, bf16[512,16384]{1,0:T(8,128)(2,1)} %tokens.5), custom_call_target="tpu_custom_call" | custom-call | flops 2147483648 | bytes 8388608 | tf_op jit(solution)/shard_map/pallas_call | solution.py:143
  13.2 0.6 shard_map.95
  13.7 1.0 collective-permute-done.refs_1_
  14.7 0.6 shard_map.96
  15.3 2.9 %collective-permute-start.4 = (bf16[8192,128]{1,0:T(8,128)(2,1)S(1)}, bf16[8192,128]{1,0:T(8,128)(2,1)S(1)}, u32[]{:S(2)}, u32[]{:S(2)}) collective-permute-start(bf16[8192,128]{1,0:T(8,128)(2,1)S(1)} %shard_map.96), channel_id=1, source_target_pairs={{0,24},{1,25},{2,26},{3,27},{4,28},{5,29},{6,30},{7,31},{8,16},{9,... | collective-permute-start | bytes 6291464 | tf_op jit(solution)/shard_map/ppermute | solution.py:57
  18.4 8.0 %shard_map.97 = (bf16[4096,128]{1,0:T(8,128)(2,1)}, bf16[4096,128]{1,0:T(8,128)(2,1)}, bf16[4096,128]{1,0:T(8,128)(2,1)}, bf16[4096,128]{1,0:T(8,128)(2,1)}, bf1...) custom-call(bf16[512,512]{1,0:T(8,128)(2,1)} %cot.3, ...), custom_call_target="tpu_custom_call" | custom-call | flops 4294967296 | bytes 16777216 | tf_op jit(solution)/shard_map/pallas_call | solution.py:143
  26.5 0.5 collective-permute-start.6
  27.1 15.5 %collective-permute-done.4.refs_3_.refs_5_ = bf16[8192,128]{1,0:T(8,128)(2,1)S(1)} collective-permute-done((bf16[8192,128]{1,0:T(8,128)(2,1)S(1)}, bf16[8192,128]{1,0:T(8,128)(2,1)S(1)}, u32[]{:S(2)}, u32[]{:S(2)}) %collective-permute-start.4) | collective-permute-done | bytes 2097184 | tf_op jit(solution)/shard_map/ppermute | solution.py:57
  42.6 1.6 %collective-permute-done.3.refs_2_.refs_4_ = bf16[8192,128]{1,0:T(8,128)(2,1)S(1)} collective-permute-done((bf16[8192,128]{1,0:T(8,128)(2,1)S(1)}, bf16[8192,128]{1,0:T(8,128)(2,1)S(1)}, u32[]{:S(2)}, u32[]{:S(2)}) %collective-permute-start.3) | collective-permute-done | bytes 2097184 | tf_op jit(solution)/shard_map/ppermute | solution.py:57
  44.3 0.6 shard_map.98
  44.9 0.6 shard_map.99
  45.7 1.1 collective-permute-start.8
  46.9 0.3 shard_map.101.selector
  47.2 0.8 shard_map.100
  48.1 12.2 %collective-permute-done.9.refs_1_ = bf16[4096,128]{1,0:T(8,128)(2,1)S(1)} collective-permute-done((bf16[4096,128]{1,0:T(8,128)(2,1)S(1)}, bf16[4096,128]{1,0:T(8,128)(2,1)S(1)}, u32[]{:S(2)}, u32[]{:S(2)}) %collective-permute-start.9) | collective-permute-done | bytes 1048608 | tf_op jit(solution)/shard_map/ppermute | solution.py:57
  60.6 1.8 %collective-permute-start.10 = (bf16[2048,128]{1,0:T(8,128)(2,1)S(1)}, bf16[2048,128]{1,0:T(8,128)(2,1)S(1)}, u32[]{:S(2)}, u32[]{:S(2)}) collective-permute-start(bf16[2048,128]{1,0:T(8,128)(2,1)S(1)} %get-tuple-element.65), channel_id=1, source_target_pairs={{0,64},{1,65},{2,66},{3,67},{4,68},{5,69},{6,70},{7,71},{8,72},{9,... | collective-permute-start | bytes 1572872 | tf_op jit(solution)/shard_map/ppermute | solution.py:57
  62.4 2.2 %collective-permute-start.11 = (bf16[2048,128]{1,0:T(8,128)(2,1)S(1)}, bf16[2048,128]{1,0:T(8,128)(2,1)S(1)}, u32[]{:S(2)}, u32[]{:S(2)}) collective-permute-start(bf16[2048,128]{1,0:T(8,128)(2,1)S(1)} %get-tuple-element.66), channel_id=1, source_target_pairs={{0,68},{1,69},{2,70},{3,71},{4,64},{5,65},{6,66},{7,67},{8,76},{9,... | collective-permute-start | bytes 1572872 | tf_op jit(solution)/shard_map/ppermute | solution.py:57
  64.9 0.8 collective-permute-start.12
  65.7 4.3 %collective-permute-done.10.refs_1_ = bf16[2048,128]{1,0:T(8,128)(2,1)S(1)} collective-permute-done((bf16[2048,128]{1,0:T(8,128)(2,1)S(1)}, bf16[2048,128]{1,0:T(8,128)(2,1)S(1)}, u32[]{:S(2)}, u32[]{:S(2)}) %collective-permute-start.10) | collective-permute-done | bytes 524320 | tf_op jit(solution)/shard_map/ppermute | solution.py:57
  70.0 8.4 %collective-permute-done.11.refs_2_ = bf16[2048,128]{1,0:T(8,128)(2,1)S(1)} collective-permute-done((bf16[2048,128]{1,0:T(8,128)(2,1)S(1)}, bf16[2048,128]{1,0:T(8,128)(2,1)S(1)}, u32[]{:S(2)}, u32[]{:S(2)}) %collective-permute-start.11) | collective-permute-done | bytes 524320 | tf_op jit(solution)/shard_map/ppermute | solution.py:57
  78.7 2.0 %collective-permute-start.13 = (bf16[512,128]{1,0:T(8,128)(2,1)S(1)}, bf16[512,128]{1,0:T(8,128)(2,1)S(1)}, u32[]{:S(2)}, u32[]{:S(2)}) collective-permute-start(bf16[512,128]{1,0:T(8,128)(2,1)S(1)} %get-tuple-element.69), channel_id=1, source_target_pairs={{0,1},{1,0},{2,3},{3,2},{4,5},{5,4},{6,7},{7,6},{8,9},{9,8},{10,11... | collective-permute-start | bytes 393224 | tf_op jit(solution)/shard_map/ppermute | solution.py:57
  80.7 2.5 %collective-permute-start.14 = (bf16[512,128]{1,0:T(8,128)(2,1)S(1)}, bf16[512,128]{1,0:T(8,128)(2,1)S(1)}, u32[]{:S(2)}, u32[]{:S(2)}) collective-permute-start(bf16[512,128]{1,0:T(8,128)(2,1)S(1)} %get-tuple-element.70), channel_id=1, source_target_pairs={{0,3},{1,2},{2,1},{3,0},{4,7},{5,6},{6,5},{7,4},{8,11},{9,10},{10,... | collective-permute-start | bytes 393224 | tf_op jit(solution)/shard_map/ppermute | solution.py:57
  83.2 1.1 collective-permute-start.15
  84.3 2.9 %collective-permute-done.14.refs_2_ = bf16[512,128]{1,0:T(8,128)(2,1)S(1)} collective-permute-done((bf16[512,128]{1,0:T(8,128)(2,1)S(1)}, bf16[512,128]{1,0:T(8,128)(2,1)S(1)}, u32[]{:S(2)}, u32[]{:S(2)}) %collective-permute-start.14) | collective-permute-done | bytes 131104 | tf_op jit(solution)/shard_map/ppermute | solution.py:57
  87.1 2.5 %collective-permute-done.15.refs_3_ = bf16[512,128]{1,0:T(8,128)(2,1)S(1)} collective-permute-done((bf16[512,128]{1,0:T(8,128)(2,1)S(1)}, bf16[512,128]{1,0:T(8,128)(2,1)S(1)}, u32[]{:S(2)}, u32[]{:S(2)}) %collective-permute-start.15) | collective-permute-done | bytes 131104 | tf_op jit(solution)/shard_map/ppermute | solution.py:57
  89.9 5.0 %collective-permute-done.16 = bf16[512,128]{1,0:T(8,128)(2,1)S(1)} collective-permute-done((bf16[512,128]{1,0:T(8,128)(2,1)S(1)}, bf16[512,128]{1,0:T(8,128)(2,1)S(1)}, u32[]{:S(2)}, u32[]{:S(2)}) %collective-permute-start.16) | collective-permute-done | bytes 131104 | tf_op jit(solution)/shard_map/ppermute | solution.py:57
  94.9 1.5 %collective-permute-done.17.other = bf16[2,512,128]{2,1,0:T(8,128)(2,1)S(1)} collective-permute-done((bf16[2,512,128]{2,1,0:T(8,128)(2,1)S(1)}, bf16[2,512,128]{2,1,0:T(8,128)(2,1)S(1)}, u32[]{:S(2)}, u32[]{:S(2)}) %collective-permute-start.17) | collective-permute-done | bytes 262176 | tf_op jit(solution)/shard_map/ppermute | solution.py:57
  96.5 2.3 %shard_map.106 = (bf16[128,2,512]{2,1,0:T(2,128)(2,1)S(1)}, f32[512,512]{1,0:T(8,128)}, f32[512,512]{1,0:T(8,128)}, f32[512,512]{1,0:T(8,128)}) custom-call(bf16[2,512,128]{2,1,0:T(8,128)(2,1)S(1)} %pad_maximum_fusion.own, bf16[2,512,128]{2,1,0:T(8,128)(2,1)S(1)} %collective-permute-done.17.other, f32[512,512]{1,0:T(8,128)S(1)} %copy-done, ...), custom_call_target="tpu_custom_call" | custom-call | flops 5242880 | bytes 6815744 | tf_op jit(solution)/shard_map/pallas_call | solution.py:208
  98.8 15.4 %all_to_all.5 = bf16[32,4,2,512]{3,2,1,0:T(2,128)(2,1)S(1)} all-to-all(bf16[32,4,2,512]{3,2,1,0:T(2,128)(2,1)S(1)} %bitcast.5), channel_id=1, replica_groups=mesh['rep'=4,'fsdp'=32] {'fsdp'}, dimensions={0} | all-to-all | bytes 524288 | tf_op jit(solution)/shard_map/all_to_all | solution.py:379
  114.1 0.7 copy.11
  (29 shorter events, 1.9 us)
Async XLA Ops:
  7.3 5.9 %collective-permute-start.1 = (bf16[8192,128]{1,0:T(8,128)(2,1)}, bf16[8192,128]{1,0:T(8,128)(2,1)S(1)}, u32[]{:S(2)}, u32[]{:S(2)}) collective-permute-start(bf16[8192,128]{1,0:T(8,128)(2,1)} %get-tuple-element.40), channel_id=1, source_target_pairs={{0,32},{1,33},{2,34},{3,35},{4,36},{5,37},{6,38},{7,39},{8,40},{9,... | collective-permute-start | bytes 6291464 | tf_op jit(solution)/shard_map/ppermute | solution.py:57
  7.4 7.4 %collective-permute-start = (bf16[8192,128]{1,0:T(8,128)(2,1)}, bf16[8192,128]{1,0:T(8,128)(2,1)S(1)}, u32[]{:S(2)}, u32[]{:S(2)}) collective-permute-start(bf16[8192,128]{1,0:T(8,128)(2,1)} %get-tuple-element.41), channel_id=1, source_target_pairs={{0,32},{1,33},{2,34},{3,35},{4,36},{5,37},{6,38},{7,39},{8,40},{9,... | collective-permute-start | bytes 6291464 | tf_op jit(solution)/shard_map/ppermute | solution.py:57
  15.3 27.3 %collective-permute-start.4 = (bf16[8192,128]{1,0:T(8,128)(2,1)S(1)}, bf16[8192,128]{1,0:T(8,128)(2,1)S(1)}, u32[]{:S(2)}, u32[]{:S(2)}) collective-permute-start(bf16[8192,128]{1,0:T(8,128)(2,1)S(1)} %shard_map.96), channel_id=1, source_target_pairs={{0,24},{1,25},{2,26},{3,27},{4,28},{5,29},{6,30},{7,31},{8,16},{9,... | collective-permute-start | bytes 6291464 | tf_op jit(solution)/shard_map/ppermute | solution.py:57
  18.2 26.0 %collective-permute-start.3 = (bf16[8192,128]{1,0:T(8,128)(2,1)S(1)}, bf16[8192,128]{1,0:T(8,128)(2,1)S(1)}, u32[]{:S(2)}, u32[]{:S(2)}) collective-permute-start(bf16[8192,128]{1,0:T(8,128)(2,1)S(1)} %shard_map.95), channel_id=1, source_target_pairs={{0,8},{1,9},{2,10},{3,11},{4,12},{5,13},{6,14},{7,15},{8,0},{9,1},... | collective-permute-start | bytes 6291464 | tf_op jit(solution)/shard_map/ppermute | solution.py:57
  26.4 18.4 %collective-permute-start.5 = (bf16[4096,128]{1,0:T(8,128)(2,1)}, bf16[4096,128]{1,0:T(8,128)(2,1)S(1)}, u32[]{:S(2)}, u32[]{:S(2)}) collective-permute-start(bf16[4096,128]{1,0:T(8,128)(2,1)} %get-tuple-element.54), channel_id=1, source_target_pairs={{0,32},{1,33},{2,34},{3,35},{4,36},{5,37},{6,38},{7,39},{8,40},{9,... | collective-permute-start | bytes 3145736 | tf_op jit(solution)/shard_map/ppermute | solution.py:57
  26.5 18.3 %collective-permute-start.6 = (bf16[4096,128]{1,0:T(8,128)(2,1)}, bf16[4096,128]{1,0:T(8,128)(2,1)S(1)}, u32[]{:S(2)}, u32[]{:S(2)}) collective-permute-start(bf16[4096,128]{1,0:T(8,128)(2,1)} %get-tuple-element.55), channel_id=1, source_target_pairs={{0,32},{1,33},{2,34},{3,35},{4,36},{5,37},{6,38},{7,39},{8,40},{9,... | collective-permute-start | bytes 3145736 | tf_op jit(solution)/shard_map/ppermute | solution.py:57
  27.0 20.2 %collective-permute-start.2 = (bf16[4096,128]{1,0:T(8,128)(2,1)}, bf16[4096,128]{1,0:T(8,128)(2,1)S(1)}, u32[]{:S(2)}, u32[]{:S(2)}) collective-permute-start(bf16[4096,128]{1,0:T(8,128)(2,1)} %get-tuple-element.49), channel_id=1, source_target_pairs={{0,32},{1,33},{2,34},{3,35},{4,36},{5,37},{6,38},{7,39},{8,40},{9,... | collective-permute-start | bytes 3145736 | tf_op jit(solution)/shard_map/ppermute | solution.py:57
  42.6 4.6 %collective-permute-start.7 = (bf16[4096,128]{1,0:T(8,128)(2,1)}, bf16[4096,128]{1,0:T(8,128)(2,1)S(1)}, u32[]{:S(2)}, u32[]{:S(2)}) collective-permute-start(bf16[4096,128]{1,0:T(8,128)(2,1)} %get-tuple-element.59), channel_id=1, source_target_pairs={{0,32},{1,33},{2,34},{3,35},{4,36},{5,37},{6,38},{7,39},{8,40},{9,... | collective-permute-start | bytes 3145736 | tf_op jit(solution)/shard_map/ppermute | solution.py:57
  44.8 2.0 %copy-start.3 = (s32[8192]{0:T(1024)S(1)}, s32[8192]{0:T(1024)}, u32[]{:S(2)}) copy-start(s32[8192]{0:T(1024)} %owner.1) | copy-start | bytes 98308
  45.4 14.9 %collective-permute-start.9 = (bf16[4096,128]{1,0:T(8,128)(2,1)S(1)}, bf16[4096,128]{1,0:T(8,128)(2,1)S(1)}, u32[]{:S(2)}, u32[]{:S(2)}) collective-permute-start(bf16[4096,128]{1,0:T(8,128)(2,1)S(1)} %get-tuple-element.57), channel_id=1, source_target_pairs={{0,8},{1,9},{2,10},{3,11},{4,12},{5,13},{6,14},{7,15},{8,0},{9,1},... | collective-permute-start | bytes 3145736 | tf_op jit(solution)/shard_map/ppermute | solution.py:57
  45.7 18.9 %collective-permute-start.8 = (bf16[4096,128]{1,0:T(8,128)(2,1)S(1)}, bf16[4096,128]{1,0:T(8,128)(2,1)S(1)}, u32[]{:S(2)}, u32[]{:S(2)}) collective-permute-start(bf16[4096,128]{1,0:T(8,128)(2,1)S(1)} %get-tuple-element.56), channel_id=1, source_target_pairs={{0,24},{1,25},{2,26},{3,27},{4,28},{5,29},{6,30},{7,31},{8,16},{9,... | collective-permute-start | bytes 3145736 | tf_op jit(solution)/shard_map/ppermute | solution.py:57
  60.6 9.4 %collective-permute-start.10 = (bf16[2048,128]{1,0:T(8,128)(2,1)S(1)}, bf16[2048,128]{1,0:T(8,128)(2,1)S(1)}, u32[]{:S(2)}, u32[]{:S(2)}) collective-permute-start(bf16[2048,128]{1,0:T(8,128)(2,1)S(1)} %get-tuple-element.65), channel_id=1, source_target_pairs={{0,64},{1,65},{2,66},{3,67},{4,68},{5,69},{6,70},{7,71},{8,72},{9,... | collective-permute-start | bytes 1572872 | tf_op jit(solution)/shard_map/ppermute | solution.py:57
  62.4 16.0 %collective-permute-start.11 = (bf16[2048,128]{1,0:T(8,128)(2,1)S(1)}, bf16[2048,128]{1,0:T(8,128)(2,1)S(1)}, u32[]{:S(2)}, u32[]{:S(2)}) collective-permute-start(bf16[2048,128]{1,0:T(8,128)(2,1)S(1)} %get-tuple-element.66), channel_id=1, source_target_pairs={{0,68},{1,69},{2,70},{3,71},{4,64},{5,65},{6,66},{7,67},{8,76},{9,... | collective-permute-start | bytes 1572872 | tf_op jit(solution)/shard_map/ppermute | solution.py:57
  64.9 31.6 %copy-start = (f32[512,512]{1,0:T(8,128)S(1)}, f32[512,512]{1,0:T(8,128)}, u32[]{:S(2)}) copy-start(f32[512,512]{1,0:T(8,128)} %master.1) | copy-start | bytes 3145732
  64.9 31.6 %copy-start.1 = (f32[512,512]{1,0:T(8,128)S(1)}, f32[512,512]{1,0:T(8,128)}, u32[]{:S(2)}) copy-start(f32[512,512]{1,0:T(8,128)} %moment1.1) | copy-start | bytes 3145732
  64.9 31.5 %copy-start.2 = (f32[512,512]{1,0:T(8,128)S(1)}, f32[512,512]{1,0:T(8,128)}, u32[]{:S(2)}) copy-start(f32[512,512]{1,0:T(8,128)} %moment2.1) | copy-start | bytes 3145732
  64.9 13.5 %collective-permute-start.12 = (bf16[2048,128]{1,0:T(8,128)(2,1)S(1)}, bf16[2048,128]{1,0:T(8,128)(2,1)S(1)}, u32[]{:S(2)}, u32[]{:S(2)}) collective-permute-start(bf16[2048,128]{1,0:T(8,128)(2,1)S(1)} %get-tuple-element.67), channel_id=1, source_target_pairs={{0,4},{1,5},{2,6},{3,7},{4,0},{5,1},{6,2},{7,3},{8,12},{9,13},{10,... | collective-permute-start | bytes 1572872 | tf_op jit(solution)/shard_map/ppermute | solution.py:57
  78.7 5.6 %collective-permute-start.13 = (bf16[512,128]{1,0:T(8,128)(2,1)S(1)}, bf16[512,128]{1,0:T(8,128)(2,1)S(1)}, u32[]{:S(2)}, u32[]{:S(2)}) collective-permute-start(bf16[512,128]{1,0:T(8,128)(2,1)S(1)} %get-tuple-element.69), channel_id=1, source_target_pairs={{0,1},{1,0},{2,3},{3,2},{4,5},{5,4},{6,7},{7,6},{8,9},{9,8},{10,11... | collective-permute-start | bytes 393224 | tf_op jit(solution)/shard_map/ppermute | solution.py:57
  80.7 6.4 %collective-permute-start.14 = (bf16[512,128]{1,0:T(8,128)(2,1)S(1)}, bf16[512,128]{1,0:T(8,128)(2,1)S(1)}, u32[]{:S(2)}, u32[]{:S(2)}) collective-permute-start(bf16[512,128]{1,0:T(8,128)(2,1)S(1)} %get-tuple-element.70), channel_id=1, source_target_pairs={{0,3},{1,2},{2,1},{3,0},{4,7},{5,6},{6,5},{7,4},{8,11},{9,10},{10,... | collective-permute-start | bytes 393224 | tf_op jit(solution)/shard_map/ppermute | solution.py:57
  83.2 6.5 %collective-permute-start.15 = (bf16[512,128]{1,0:T(8,128)(2,1)S(1)}, bf16[512,128]{1,0:T(8,128)(2,1)S(1)}, u32[]{:S(2)}, u32[]{:S(2)}) collective-permute-start(bf16[512,128]{1,0:T(8,128)(2,1)S(1)} %get-tuple-element.71), channel_id=1, source_target_pairs={{0,2},{1,3},{2,0},{3,1},{4,6},{5,7},{6,4},{7,5},{8,10},{9,11},{10,... | collective-permute-start | bytes 393224 | tf_op jit(solution)/shard_map/ppermute | solution.py:57
  89.8 5.0 %collective-permute-start.16 = (bf16[512,128]{1,0:T(8,128)(2,1)S(1)}, bf16[512,128]{1,0:T(8,128)(2,1)S(1)}, u32[]{:S(2)}, u32[]{:S(2)}) collective-permute-start(bf16[512,128]{1,0:T(8,128)(2,1)S(1)} %shard_map.105), channel_id=1, source_target_pairs={{0,64},{1,65},{2,66},{3,67},{4,68},{5,69},{6,70},{7,71},{8,72},{9,... | collective-permute-start | bytes 393224 | tf_op jit(solution)/shard_map/ppermute | solution.py:57
  94.8 1.6 %collective-permute-start.17 = (bf16[2,512,128]{2,1,0:T(8,128)(2,1)S(1)}, bf16[2,512,128]{2,1,0:T(8,128)(2,1)S(1)}, u32[]{:S(2)}, u32[]{:S(2)}) collective-permute-start(bf16[2,512,128]{2,1,0:T(8,128)(2,1)S(1)} %pad_maximum_fusion.own), channel_id=1, source_target_pairs={{0,32},{1,33},{2,34},{3,35},{4,36},{5,37},{6,38},{7,39},{8,40},{9,... | collective-permute-start | bytes 786440 | tf_op jit(solution)/shard_map/ppermute | solution.py:57

commit v6 on v5

--- a/solution.py
+++ b/solution.py
@@ -293,11 +293,13 @@
     beside = [send(value, rep_pairs(1)) for value in both[:4]]
 
     rows = 8 * columns
-    half_sums = combine(
-        [both[5], both[7], *came],
-        [[(rows, [(odd, 0), (2 + odd, rows)])] for odd in range(2)],
-        flops=10**11,
-    )
+    half_sums = []
+    for odd, flops in ((0, 2 * 10**10), (1, 10**11)):
+        half_sums += combine(
+            [after(both[5 + 2 * odd], *half_sums), came[odd]],
+            [[(rows, [(0, 0), (1, rows)])]],
+            flops=flops,
+        )
     sent = combine(
         [*half_sums, beside[1], beside[3]],
         [[(rows, [(odd, 0), (2 + odd, 0)])] for odd in range(2)],

time: 115 us -> 115 us (level)
  waiting for transfers between devices: 55 us -> 52 us
  starting transfers between devices: 16.4 us -> 18.1 us
    ppermute x18, waiting for transfers between devices: 55 us -> 52 us  [send(): return lax.ppermute(value, AXES, pairs)]
    ppermute x18, starting transfers between devices: 16.4 us -> 18.1 us  [send(): return lax.ppermute(value, AXES, pairs)]
    pallas_call x9 -> x10, Pallas kernels: 3.95 us -> 3.94 us  [combine(): pl.pallas_call(functools.partial(combine_body, plan), out_shape=[pltpu.VM...]
  transfers between devices with their start and end apart: 18 -> 18, of which waited for: 10 -> 9; matrix products, arithmetic and copies ran while one was open for 0% -> 0% of each run, Pallas kernels for 14% -> 15%
where the time goes in v6:
time: 115 us
  waiting for transfers between devices  52 us (45%)
  Pallas kernels  26.4 us (23%)
  starting transfers between devices  18.1 us (16%)
  blocking collectives  16.3 us (14%)
    ppermute x18, waiting for transfers between devices, send(): return lax.ppermute(value, AXES, pairs)  52 us
    pallas_call x3, Pallas kernels, split_sums(): pl.pallas_call(functools.partial(split_body, groups), out_shape=outs, in_...  19.9 us
    ppermute x18, starting transfers between devices, send(): return lax.ppermute(value, AXES, pairs)  18.1 us
    all_to_all x1, blocking collectives, per_device(): lax.all_to_all(outgoing, 'fsdp', split_axis=0, concat_axis=0, tiled=True)  16.3 us
    pallas_call x10, Pallas kernels, combine(): pl.pallas_call(functools.partial(combine_body, plan), out_shape=[pltpu.VM...  3.94 us
  transfers between devices with their start and end apart: 18, of which 9 were waited for; matrix products, arithmetic and copies ran while one was open for 0% of the time, Pallas kernels for 15%

profile of v6, /device:TPU:0, one launch (start us, length us, event | category | flops | bytes accessed | tf_op | source)
XLA Modules:
  0.0 114.5 jit_solution(7162288069976723442)
XLA Ops:
  0.6 6.6 %shard_map.93 = (bf16[8192,128]{1,0:T(8,128)(2,1)}, bf16[8192,128]{1,0:T(8,128)(2,1)}) custom-call(bf16[512,512]{1,0:T(8,128)(2,1)} %cot.3, bf16[512,16384]{1,0:T(8,128)(2,1)} %tokens.5), custom_call_target="tpu_custom_call" | custom-call | flops 2147483648 | bytes 8388608 | tf_op jit(solution)/shard_map/pallas_call | solution.py:143
  7.4 0.5 collective-permute-start
  7.9 5.3 %shard_map.94 = (bf16[8192,128]{1,0:T(8,128)(2,1)S(1)}, bf16[8192,128]{1,0:T(8,128)(2,1)S(1)}) custom-call(bf16[512,512]{1,0:T(8,128)(2,1)} %cot.3, bf16[512,16384]{1,0:T(8,128)(2,1)} %tokens.5), custom_call_target="tpu_custom_call" | custom-call | flops 2147483648 | bytes 8388608 | tf_op jit(solution)/shard_map/pallas_call | solution.py:143
  13.2 0.6 shard_map.95
  13.7 1.7 %collective-permute-start.3 = (bf16[8192,128]{1,0:T(8,128)(2,1)S(1)}, bf16[8192,128]{1,0:T(8,128)(2,1)S(1)}, u32[]{:S(2)}, u32[]{:S(2)}) collective-permute-start(bf16[8192,128]{1,0:T(8,128)(2,1)S(1)} %shard_map.95), channel_id=1, source_target_pairs={{0,8},{1,9},{2,10},{3,11},{4,12},{5,13},{6,14},{7,15},{8,0},{9,1},... | collective-permute-start | bytes 6291464 | tf_op jit(solution)/shard_map/ppermute | solution.py:57
  15.4 0.6 shard_map.96
  15.9 2.3 %collective-permute-start.4 = (bf16[8192,128]{1,0:T(8,128)(2,1)S(1)}, bf16[8192,128]{1,0:T(8,128)(2,1)S(1)}, u32[]{:S(2)}, u32[]{:S(2)}) collective-permute-start(bf16[8192,128]{1,0:T(8,128)(2,1)S(1)} %shard_map.96), channel_id=1, source_target_pairs={{0,24},{1,25},{2,26},{3,27},{4,28},{5,29},{6,30},{7,31},{8,16},{9,... | collective-permute-start | bytes 6291464 | tf_op jit(solution)/shard_map/ppermute | solution.py:57
  18.2 8.0 %shard_map.97 = (bf16[4096,128]{1,0:T(8,128)(2,1)}, bf16[4096,128]{1,0:T(8,128)(2,1)}, bf16[4096,128]{1,0:T(8,128)(2,1)}, bf16[4096,128]{1,0:T(8,128)(2,1)}, bf1...) custom-call(bf16[512,512]{1,0:T(8,128)(2,1)} %cot.3, ...), custom_call_target="tpu_custom_call" | custom-call | flops 4294967296 | bytes 16777216 | tf_op jit(solution)/shard_map/pallas_call | solution.py:143
  26.4 0.4 collective-permute-start.6
  26.9 12.9 %collective-permute-done.3.refs_1_.refs_4_ = bf16[8192,128]{1,0:T(8,128)(2,1)S(1)} collective-permute-done((bf16[8192,128]{1,0:T(8,128)(2,1)S(1)}, bf16[8192,128]{1,0:T(8,128)(2,1)S(1)}, u32[]{:S(2)}, u32[]{:S(2)}) %collective-permute-start.3) | collective-permute-done | bytes 2097184 | tf_op jit(solution)/shard_map/ppermute | solution.py:57
  40.1 3.1 %collective-permute-done.4.refs_1_.refs_5_ = bf16[8192,128]{1,0:T(8,128)(2,1)S(1)} collective-permute-done((bf16[8192,128]{1,0:T(8,128)(2,1)S(1)}, bf16[8192,128]{1,0:T(8,128)(2,1)S(1)}, u32[]{:S(2)}, u32[]{:S(2)}) %collective-permute-start.4) | collective-permute-done | bytes 2097184 | tf_op jit(solution)/shard_map/ppermute | solution.py:57
  43.6 0.6 shard_map.100
  44.2 2.3 %collective-permute-start.8 = (bf16[4096,128]{1,0:T(8,128)(2,1)S(1)}, bf16[4096,128]{1,0:T(8,128)(2,1)S(1)}, u32[]{:S(2)}, u32[]{:S(2)}) collective-permute-start(bf16[4096,128]{1,0:T(8,128)(2,1)S(1)} %get-tuple-element.54), channel_id=1, source_target_pairs={{0,24},{1,25},{2,26},{3,27},{4,28},{5,29},{6,30},{7,31},{8,16},{9,... | collective-permute-start | bytes 3145736 | tf_op jit(solution)/shard_map/ppermute | solution.py:57
  46.5 0.3 shard_map.102.selector
  46.8 0.8 shard_map.101
  47.7 11.3 %collective-permute-done.9.refs_1_ = bf16[4096,128]{1,0:T(8,128)(2,1)S(1)} collective-permute-done((bf16[4096,128]{1,0:T(8,128)(2,1)S(1)}, bf16[4096,128]{1,0:T(8,128)(2,1)S(1)}, u32[]{:S(2)}, u32[]{:S(2)}) %collective-permute-start.9) | collective-permute-done | bytes 1048608 | tf_op jit(solution)/shard_map/ppermute | solution.py:57
  59.3 1.8 %collective-permute-start.10 = (bf16[2048,128]{1,0:T(8,128)(2,1)S(1)}, bf16[2048,128]{1,0:T(8,128)(2,1)S(1)}, u32[]{:S(2)}, u32[]{:S(2)}) collective-permute-start(bf16[2048,128]{1,0:T(8,128)(2,1)S(1)} %get-tuple-element.63), channel_id=1, source_target_pairs={{0,64},{1,65},{2,66},{3,67},{4,68},{5,69},{6,70},{7,71},{8,72},{9,... | collective-permute-start | bytes 1572872 | tf_op jit(solution)/shard_map/ppermute | solution.py:57
  61.1 2.2 %collective-permute-start.11 = (bf16[2048,128]{1,0:T(8,128)(2,1)S(1)}, bf16[2048,128]{1,0:T(8,128)(2,1)S(1)}, u32[]{:S(2)}, u32[]{:S(2)}) collective-permute-start(bf16[2048,128]{1,0:T(8,128)(2,1)S(1)} %get-tuple-element.64), channel_id=1, source_target_pairs={{0,68},{1,69},{2,70},{3,71},{4,64},{5,65},{6,66},{7,67},{8,76},{9,... | collective-permute-start | bytes 1572872 | tf_op jit(solution)/shard_map/ppermute | solution.py:57
  63.3 0.3 shard_map.103
  63.7 0.8 collective-permute-start.12
  64.5 4.3 %collective-permute-done.10.refs_1_ = bf16[2048,128]{1,0:T(8,128)(2,1)S(1)} collective-permute-done((bf16[2048,128]{1,0:T(8,128)(2,1)S(1)}, bf16[2048,128]{1,0:T(8,128)(2,1)S(1)}, u32[]{:S(2)}, u32[]{:S(2)}) %collective-permute-start.10) | collective-permute-done | bytes 524320 | tf_op jit(solution)/shard_map/ppermute | solution.py:57
  68.8 8.4 %collective-permute-done.11.refs_2_ = bf16[2048,128]{1,0:T(8,128)(2,1)S(1)} collective-permute-done((bf16[2048,128]{1,0:T(8,128)(2,1)S(1)}, bf16[2048,128]{1,0:T(8,128)(2,1)S(1)}, u32[]{:S(2)}, u32[]{:S(2)}) %collective-permute-start.11) | collective-permute-done | bytes 524320 | tf_op jit(solution)/shard_map/ppermute | solution.py:57
  77.4 2.0 %collective-permute-start.13 = (bf16[512,128]{1,0:T(8,128)(2,1)S(1)}, bf16[512,128]{1,0:T(8,128)(2,1)S(1)}, u32[]{:S(2)}, u32[]{:S(2)}) collective-permute-start(bf16[512,128]{1,0:T(8,128)(2,1)S(1)} %get-tuple-element.67), channel_id=1, source_target_pairs={{0,1},{1,0},{2,3},{3,2},{4,5},{5,4},{6,7},{7,6},{8,9},{9,8},{10,11... | collective-permute-start | bytes 393224 | tf_op jit(solution)/shard_map/ppermute | solution.py:57
  79.4 2.5 %collective-permute-start.14 = (bf16[512,128]{1,0:T(8,128)(2,1)S(1)}, bf16[512,128]{1,0:T(8,128)(2,1)S(1)}, u32[]{:S(2)}, u32[]{:S(2)}) collective-permute-start(bf16[512,128]{1,0:T(8,128)(2,1)S(1)} %get-tuple-element.68), channel_id=1, source_target_pairs={{0,3},{1,2},{2,1},{3,0},{4,7},{5,6},{6,5},{7,4},{8,11},{9,10},{10,... | collective-permute-start | bytes 393224 | tf_op jit(solution)/shard_map/ppermute | solution.py:57
  81.9 1.1 collective-permute-start.15
  83.0 2.9 %collective-permute-done.14.refs_2_ = bf16[512,128]{1,0:T(8,128)(2,1)S(1)} collective-permute-done((bf16[512,128]{1,0:T(8,128)(2,1)S(1)}, bf16[512,128]{1,0:T(8,128)(2,1)S(1)}, u32[]{:S(2)}, u32[]{:S(2)}) %collective-permute-start.14) | collective-permute-done | bytes 131104 | tf_op jit(solution)/shard_map/ppermute | solution.py:57
  85.9 2.5 %collective-permute-done.15.refs_3_ = bf16[512,128]{1,0:T(8,128)(2,1)S(1)} collective-permute-done((bf16[512,128]{1,0:T(8,128)(2,1)S(1)}, bf16[512,128]{1,0:T(8,128)(2,1)S(1)}, u32[]{:S(2)}, u32[]{:S(2)}) %collective-permute-start.15) | collective-permute-done | bytes 131104 | tf_op jit(solution)/shard_map/ppermute | solution.py:57
  88.6 5.0 %collective-permute-done.16 = bf16[512,128]{1,0:T(8,128)(2,1)S(1)} collective-permute-done((bf16[512,128]{1,0:T(8,128)(2,1)S(1)}, bf16[512,128]{1,0:T(8,128)(2,1)S(1)}, u32[]{:S(2)}, u32[]{:S(2)}) %collective-permute-start.16) | collective-permute-done | bytes 131104 | tf_op jit(solution)/shard_map/ppermute | solution.py:57
  93.7 1.5 %collective-permute-done.17.other = bf16[2,512,128]{2,1,0:T(8,128)(2,1)S(1)} collective-permute-done((bf16[2,512,128]{2,1,0:T(8,128)(2,1)S(1)}, bf16[2,512,128]{2,1,0:T(8,128)(2,1)S(1)}, u32[]{:S(2)}, u32[]{:S(2)}) %collective-permute-start.17) | collective-permute-done | bytes 262176 | tf_op jit(solution)/shard_map/ppermute | solution.py:57
  95.2 2.3 %shard_map.107 = (bf16[128,2,512]{2,1,0:T(2,128)(2,1)S(1)}, f32[512,512]{1,0:T(8,128)}, f32[512,512]{1,0:T(8,128)}, f32[512,512]{1,0:T(8,128)}) custom-call(bf16[2,512,128]{2,1,0:T(8,128)(2,1)S(1)} %pad_maximum_fusion.own, bf16[2,512,128]{2,1,0:T(8,128)(2,1)S(1)} %collective-permute-done.17.other, f32[512,512]{1,0:T(8,128)S(1)} %copy-done, ...), custom_call_target="tpu_custom_call" | custom-call | flops 5242880 | bytes 6815744 | tf_op jit(solution)/shard_map/pallas_call | solution.py:208
  97.5 16.3 %all_to_all.5 = bf16[32,4,2,512]{3,2,1,0:T(2,128)(2,1)S(1)} all-to-all(bf16[32,4,2,512]{3,2,1,0:T(2,128)(2,1)S(1)} %bitcast.5), channel_id=1, replica_groups=mesh['rep'=4,'fsdp'=32] {'fsdp'}, dimensions={0} | all-to-all | bytes 524288 | tf_op jit(solution)/shard_map/all_to_all | solution.py:381
  113.8 0.7 copy.11
  (30 shorter events, 1.9 us)
Async XLA Ops:
  7.3 5.9 %collective-permute-start.1 = (bf16[8192,128]{1,0:T(8,128)(2,1)}, bf16[8192,128]{1,0:T(8,128)(2,1)S(1)}, u32[]{:S(2)}, u32[]{:S(2)}) collective-permute-start(bf16[8192,128]{1,0:T(8,128)(2,1)} %get-tuple-element.39), channel_id=1, source_target_pairs={{0,32},{1,33},{2,34},{3,35},{4,36},{5,37},{6,38},{7,39},{8,40},{9,... | collective-permute-start | bytes 6291464 | tf_op jit(solution)/shard_map/ppermute | solution.py:57
  7.4 8.0 %collective-permute-start = (bf16[8192,128]{1,0:T(8,128)(2,1)}, bf16[8192,128]{1,0:T(8,128)(2,1)S(1)}, u32[]{:S(2)}, u32[]{:S(2)}) collective-permute-start(bf16[8192,128]{1,0:T(8,128)(2,1)} %get-tuple-element.40), channel_id=1, source_target_pairs={{0,32},{1,33},{2,34},{3,35},{4,36},{5,37},{6,38},{7,39},{8,40},{9,... | collective-permute-start | bytes 6291464 | tf_op jit(solution)/shard_map/ppermute | solution.py:57
  13.7 26.1 %collective-permute-start.3 = (bf16[8192,128]{1,0:T(8,128)(2,1)S(1)}, bf16[8192,128]{1,0:T(8,128)(2,1)S(1)}, u32[]{:S(2)}, u32[]{:S(2)}) collective-permute-start(bf16[8192,128]{1,0:T(8,128)(2,1)S(1)} %shard_map.95), channel_id=1, source_target_pairs={{0,8},{1,9},{2,10},{3,11},{4,12},{5,13},{6,14},{7,15},{8,0},{9,1},... | collective-permute-start | bytes 6291464 | tf_op jit(solution)/shard_map/ppermute | solution.py:57
  15.9 27.3 %collective-permute-start.4 = (bf16[8192,128]{1,0:T(8,128)(2,1)S(1)}, bf16[8192,128]{1,0:T(8,128)(2,1)S(1)}, u32[]{:S(2)}, u32[]{:S(2)}) collective-permute-start(bf16[8192,128]{1,0:T(8,128)(2,1)S(1)} %shard_map.96), channel_id=1, source_target_pairs={{0,24},{1,25},{2,26},{3,27},{4,28},{5,29},{6,30},{7,31},{8,16},{9,... | collective-permute-start | bytes 6291464 | tf_op jit(solution)/shard_map/ppermute | solution.py:57
  26.2 17.4 %collective-permute-start.5 = (bf16[4096,128]{1,0:T(8,128)(2,1)}, bf16[4096,128]{1,0:T(8,128)(2,1)S(1)}, u32[]{:S(2)}, u32[]{:S(2)}) collective-permute-start(bf16[4096,128]{1,0:T(8,128)(2,1)} %get-tuple-element.52), channel_id=1, source_target_pairs={{0,32},{1,33},{2,34},{3,35},{4,36},{5,37},{6,38},{7,39},{8,40},{9,... | collective-permute-start | bytes 3145736 | tf_op jit(solution)/shard_map/ppermute | solution.py:57
  26.4 17.2 %collective-permute-start.6 = (bf16[4096,128]{1,0:T(8,128)(2,1)}, bf16[4096,128]{1,0:T(8,128)(2,1)S(1)}, u32[]{:S(2)}, u32[]{:S(2)}) collective-permute-start(bf16[4096,128]{1,0:T(8,128)(2,1)} %get-tuple-element.53), channel_id=1, source_target_pairs={{0,32},{1,33},{2,34},{3,35},{4,36},{5,37},{6,38},{7,39},{8,40},{9,... | collective-permute-start | bytes 3145736 | tf_op jit(solution)/shard_map/ppermute | solution.py:57
  26.8 20.0 %collective-permute-start.2 = (bf16[4096,128]{1,0:T(8,128)(2,1)}, bf16[4096,128]{1,0:T(8,128)(2,1)S(1)}, u32[]{:S(2)}, u32[]{:S(2)}) collective-permute-start(bf16[4096,128]{1,0:T(8,128)(2,1)} %get-tuple-element.48), channel_id=1, source_target_pairs={{0,32},{1,33},{2,34},{3,35},{4,36},{5,37},{6,38},{7,39},{8,40},{9,... | collective-permute-start | bytes 3145736 | tf_op jit(solution)/shard_map/ppermute | solution.py:57
  39.8 7.0 %collective-permute-start.7 = (bf16[4096,128]{1,0:T(8,128)(2,1)}, bf16[4096,128]{1,0:T(8,128)(2,1)S(1)}, u32[]{:S(2)}, u32[]{:S(2)}) collective-permute-start(bf16[4096,128]{1,0:T(8,128)(2,1)} %get-tuple-element.57), channel_id=1, source_target_pairs={{0,32},{1,33},{2,34},{3,35},{4,36},{5,37},{6,38},{7,39},{8,40},{9,... | collective-permute-start | bytes 3145736 | tf_op jit(solution)/shard_map/ppermute | solution.py:57
  43.5 3.0 %copy-start.3 = (s32[8192]{0:T(1024)S(1)}, s32[8192]{0:T(1024)}, u32[]{:S(2)}) copy-start(s32[8192]{0:T(1024)} %owner.1) | copy-start | bytes 98308
  44.1 14.9 %collective-permute-start.9 = (bf16[4096,128]{1,0:T(8,128)(2,1)S(1)}, bf16[4096,128]{1,0:T(8,128)(2,1)S(1)}, u32[]{:S(2)}, u32[]{:S(2)}) collective-permute-start(bf16[4096,128]{1,0:T(8,128)(2,1)S(1)} %get-tuple-element.55), channel_id=1, source_target_pairs={{0,8},{1,9},{2,10},{3,11},{4,12},{5,13},{6,14},{7,15},{8,0},{9,1},... | collective-permute-start | bytes 3145736 | tf_op jit(solution)/shard_map/ppermute | solution.py:57
  44.2 19.1 %collective-permute-start.8 = (bf16[4096,128]{1,0:T(8,128)(2,1)S(1)}, bf16[4096,128]{1,0:T(8,128)(2,1)S(1)}, u32[]{:S(2)}, u32[]{:S(2)}) collective-permute-start(bf16[4096,128]{1,0:T(8,128)(2,1)S(1)} %get-tuple-element.54), channel_id=1, source_target_pairs={{0,24},{1,25},{2,26},{3,27},{4,28},{5,29},{6,30},{7,31},{8,16},{9,... | collective-permute-start | bytes 3145736 | tf_op jit(solution)/shard_map/ppermute | solution.py:57
  59.3 9.4 %collective-permute-start.10 = (bf16[2048,128]{1,0:T(8,128)(2,1)S(1)}, bf16[2048,128]{1,0:T(8,128)(2,1)S(1)}, u32[]{:S(2)}, u32[]{:S(2)}) collective-permute-start(bf16[2048,128]{1,0:T(8,128)(2,1)S(1)} %get-tuple-element.63), channel_id=1, source_target_pairs={{0,64},{1,65},{2,66},{3,67},{4,68},{5,69},{6,70},{7,71},{8,72},{9,... | collective-permute-start | bytes 1572872 | tf_op jit(solution)/shard_map/ppermute | solution.py:57
  61.1 16.0 %collective-permute-start.11 = (bf16[2048,128]{1,0:T(8,128)(2,1)S(1)}, bf16[2048,128]{1,0:T(8,128)(2,1)S(1)}, u32[]{:S(2)}, u32[]{:S(2)}) collective-permute-start(bf16[2048,128]{1,0:T(8,128)(2,1)S(1)} %get-tuple-element.64), channel_id=1, source_target_pairs={{0,68},{1,69},{2,70},{3,71},{4,64},{5,65},{6,66},{7,67},{8,76},{9,... | collective-permute-start | bytes 1572872 | tf_op jit(solution)/shard_map/ppermute | solution.py:57
  63.6 31.6 %copy-start = (f32[512,512]{1,0:T(8,128)S(1)}, f32[512,512]{1,0:T(8,128)}, u32[]{:S(2)}) copy-start(f32[512,512]{1,0:T(8,128)} %master.1) | copy-start | bytes 3145732
  63.6 31.6 %copy-start.1 = (f32[512,512]{1,0:T(8,128)S(1)}, f32[512,512]{1,0:T(8,128)}, u32[]{:S(2)}) copy-start(f32[512,512]{1,0:T(8,128)} %moment1.1) | copy-start | bytes 3145732
  63.6 31.5 %copy-start.2 = (f32[512,512]{1,0:T(8,128)S(1)}, f32[512,512]{1,0:T(8,128)}, u32[]{:S(2)}) copy-start(f32[512,512]{1,0:T(8,128)} %moment2.1) | copy-start | bytes 3145732
  63.7 13.5 %collective-permute-start.12 = (bf16[2048,128]{1,0:T(8,128)(2,1)S(1)}, bf16[2048,128]{1,0:T(8,128)(2,1)S(1)}, u32[]{:S(2)}, u32[]{:S(2)}) collective-permute-start(bf16[2048,128]{1,0:T(8,128)(2,1)S(1)} %get-tuple-element.65), channel_id=1, source_target_pairs={{0,4},{1,5},{2,6},{3,7},{4,0},{5,1},{6,2},{7,3},{8,12},{9,13},{10,... | collective-permute-start | bytes 1572872 | tf_op jit(solution)/shard_map/ppermute | solution.py:57
  77.4 5.6 %collective-permute-start.13 = (bf16[512,128]{1,0:T(8,128)(2,1)S(1)}, bf16[512,128]{1,0:T(8,128)(2,1)S(1)}, u32[]{:S(2)}, u32[]{:S(2)}) collective-permute-start(bf16[512,128]{1,0:T(8,128)(2,1)S(1)} %get-tuple-element.67), channel_id=1, source_target_pairs={{0,1},{1,0},{2,3},{3,2},{4,5},{5,4},{6,7},{7,6},{8,9},{9,8},{10,11... | collective-permute-start | bytes 393224 | tf_op jit(solution)/shard_map/ppermute | solution.py:57
  79.4 6.4 %collective-permute-start.14 = (bf16[512,128]{1,0:T(8,128)(2,1)S(1)}, bf16[512,128]{1,0:T(8,128)(2,1)S(1)}, u32[]{:S(2)}, u32[]{:S(2)}) collective-permute-start(bf16[512,128]{1,0:T(8,128)(2,1)S(1)} %get-tuple-element.68), channel_id=1, source_target_pairs={{0,3},{1,2},{2,1},{3,0},{4,7},{5,6},{6,5},{7,4},{8,11},{9,10},{10,... | collective-permute-start | bytes 393224 | tf_op jit(solution)/shard_map/ppermute | solution.py:57
  81.9 6.5 %collective-permute-start.15 = (bf16[512,128]{1,0:T(8,128)(2,1)S(1)}, bf16[512,128]{1,0:T(8,128)(2,1)S(1)}, u32[]{:S(2)}, u32[]{:S(2)}) collective-permute-start(bf16[512,128]{1,0:T(8,128)(2,1)S(1)} %get-tuple-element.69), channel_id=1, source_target_pairs={{0,2},{1,3},{2,0},{3,1},{4,6},{5,7},{6,4},{7,5},{8,10},{9,11},{10,... | collective-permute-start | bytes 393224 | tf_op jit(solution)/shard_map/ppermute | solution.py:57
  88.5 5.0 %collective-permute-start.16 = (bf16[512,128]{1,0:T(8,128)(2,1)S(1)}, bf16[512,128]{1,0:T(8,128)(2,1)S(1)}, u32[]{:S(2)}, u32[]{:S(2)}) collective-permute-start(bf16[512,128]{1,0:T(8,128)(2,1)S(1)} %shard_map.106), channel_id=1, source_target_pairs={{0,64},{1,65},{2,66},{3,67},{4,68},{5,69},{6,70},{7,71},{8,72},{9,... | collective-permute-start | bytes 393224 | tf_op jit(solution)/shard_map/ppermute | solution.py:57
  93.6 1.6 %collective-permute-start.17 = (bf16[2,512,128]{2,1,0:T(8,128)(2,1)S(1)}, bf16[2,512,128]{2,1,0:T(8,128)(2,1)S(1)}, u32[]{:S(2)}, u32[]{:S(2)}) collective-permute-start(bf16[2,512,128]{2,1,0:T(8,128)(2,1)S(1)} %pad_maximum_fusion.own), channel_id=1, source_target_pairs={{0,32},{1,33},{2,34},{3,35},{4,36},{5,37},{6,38},{7,39},{8,40},{9,... | collective-permute-start | bytes 786440 | tf_op jit(solution)/shard_map/ppermute | solution.py:57
